TPU v7x, 512 devices: a whole 4x4x16 slice. The times are simulated.
512 devices in a mesh: depth: 4 (over y_lo, core), rows: 8 (over y_hi, x), cols: 16 (over z).
Axes of the slice: x: 4, y: 4 (y_hi: 2, y_lo: 2; y = y_hi * 2 + y_lo), z: 16, core: 2. Of those that a mesh axis runs over, the one named last changes fastest.
Arguments:
- voltage: float32 [16, 128, 2048], P('depth', 'rows', 'cols'), may hold values from -6 to 6
- states: float32 [16, 128, 41, 2048], P('depth', 'rows', None, 'cols'), may hold values from 0 to 1
- cell_tags: int32 [16, 128, 2048], P('depth', 'rows', 'cols'), may hold values from 0 to 2, as said below
- fibre_ids: int32 [16, 128, 2048], P('depth', 'rows', 'cols'), may hold values from 0 to 7
- loan_states: float32 [512, 16, 4, 41, 128], P(('depth', 'rows', 'cols')), may hold values from 0 to 1
- loan_tags: int32 [512, 16, 4, 128], P(('depth', 'rows', 'cols')), may hold values from 0 to 2, as said below
- lend_block: int32 [512, 16, 4], P(('depth', 'rows', 'cols')), may hold values from 0 to 63, as said below
- lend_count: int32 [512, 16], P(('depth', 'rows', 'cols')), may hold values from 0 to 4, as said below
- diffuse_main: float32 [3, 8], replicated, may hold values from 0.02 to 0.08
- diffuse_cross: float32 [3, 8], replicated, may hold values from -0.02 to 0.02
- gate_half: float32 [3, 41], replicated, may hold values from -1 to 1
- gate_slope: float32 [3, 41], replicated, may hold values from 0.2 to 1
- gate_rate: float32 [3, 41], replicated, may hold values from 0.05 to 3
- conductance: float32 [3, 41], replicated, may hold values from -1 to 1
- reversal: float32 [3, 41], replicated, may hold values from -1 to 1
Outputs:
- voltage_out: float32 [16, 128, 2048], P('depth', 'rows', 'cols')
- states_out: float32 [16, 128, 41, 2048], P('depth', 'rows', None, 'cols')
Inputs may be any that keep to these rules, and one draw needn't show every extreme that they name: `cell_tags`: column c of a voxel's device decides its mix: columns below 8 are mostly ventricle, the others mostly atrium and scar. `loan_tags`: mostly ventricle. `lend_block`: for each device, its 64 block ids are all different. `lend_count`: nonzero only where the device's column c is below 8 and the lender column is not; for such a device column c + 8 gets exactly 4.
All inputs are finite; a program needn't handle non-finite values.
Results may differ from a plain program's by a relative error of at most 0.0003.
Values sent between devices are 32-bit elements; how exact they have to be, the bound alone decides.
No kernel may reach another device: no remote copies, remote signals or barrier semaphores. Data moves between devices by JAX's collectives and lax.ppermute only.
A program may use at most 64 MiB of HBM per device.

v0:
```python
import jax
import jax.numpy as jnp
from jax import lax
from jax.sharding import PartitionSpec as P

STATES = 41
ATRIAL = 21
SCAR = 5
REGIONS = 8
STEPS = 2


def with_halo(value, sides, width):
    for axis, dim in sides:
        peers, length = (lax.axis_size(axis), value.shape[dim])
        up = [(i, (i + 1) % peers) for i in range(peers - 1)]
        down = [(j, i) for i, j in up]
        last = lax.slice_in_dim(value, length - width, length, axis=dim)
        leading = lax.slice_in_dim(value, 0, width, axis=dim)
        before = lax.ppermute(last, axis, up)
        after = lax.ppermute(leading, axis, down)
        value = jnp.concatenate([before, value, after], axis=dim)
    return value


def select_rows(table, kinds):
    marks = kinds[..., None, :]
    return jnp.where(
        marks == 0, table[0][:, None], jnp.where(marks == 1, table[1][:, None], table[2][:, None])
    )


def react(gates, potential, kinds, gate_half, gate_slope, gate_rate, conductance, reversal):
    level = potential[..., None, :]
    scaled = (level - select_rows(gate_half, kinds)) / select_rows(gate_slope, kinds)
    steady = jax.nn.sigmoid(scaled)
    decay = jnp.exp(-select_rows(gate_rate, kinds) * (1.0 + 0.5 * jnp.tanh(scaled)))
    count = jnp.where(kinds == 0, STATES, jnp.where(kinds == 1, ATRIAL, SCAR))[..., None, :]
    number = lax.broadcasted_iota(jnp.int32, gates.shape, gates.ndim - 2)
    fresh = jnp.where(number < count, steady + (gates - steady) * decay, jnp.float32(0.0))
    current = jnp.sum(
        select_rows(conductance, kinds) * fresh * (level - select_rows(reversal, kinds)), axis=-2
    )
    return (fresh, current)


def stencil(padded, main_coef, cross_coef):

    def offset(shift_x, shift_y, shift_z):
        return padded[
            1 + shift_x : padded.shape[0] - 1 + shift_x,
            1 + shift_y : padded.shape[1] - 1 + shift_y,
            1 + shift_z : padded.shape[2] - 1 + shift_z,
        ]

    centre = offset(0, 0, 0)
    total = main_coef[0] * (offset(1, 0, 0) + offset(-1, 0, 0) - 2.0 * centre)
    total = total + main_coef[1] * (offset(0, 1, 0) + offset(0, -1, 0) - 2.0 * centre)
    total = total + main_coef[2] * (offset(0, 0, 1) + offset(0, 0, -1) - 2.0 * centre)
    total = total + 0.5 * cross_coef[0] * (
        offset(1, 1, 0) - offset(1, -1, 0) - offset(-1, 1, 0) + offset(-1, -1, 0)
    )
    total = total + 0.5 * cross_coef[1] * (
        offset(1, 0, 1) - offset(1, 0, -1) - offset(-1, 0, 1) + offset(-1, 0, -1)
    )
    total = total + 0.5 * cross_coef[2] * (
        offset(0, 1, 1) - offset(0, 1, -1) - offset(0, -1, 1) + offset(0, -1, -1)
    )
    return centre + total


def region_coef(table, fibre_ids):
    onehot = (fibre_ids[None] == jnp.arange(REGIONS, dtype=jnp.int32)[:, None, None, None]).astype(
        jnp.float32
    )
    return jnp.einsum("cr,rxyz->cxyz", table, onehot, precision=lax.Precision.HIGHEST)


def brick_faces(field):
    return with_halo(field, (("depth", 0), ("rows", 1), ("cols", 2)), 1)


def local(
    voltage,
    states,
    cell_tags,
    fibre_ids,
    loan_states,
    loan_tags,
    lend_block,
    lend_count,
    diffuse_main,
    diffuse_cross,
    gate_half,
    gate_slope,
    gate_rate,
    conductance,
    reversal,
):
    tables = (gate_half, gate_slope, gate_rate, conductance, reversal)
    depth_x, depth_y, line = voltage.shape
    nblock = depth_x * depth_y
    nstate = states.shape[2]
    ncols = lend_block.shape[1]
    cap_slots = lend_block.shape[2]
    main_coef = region_coef(diffuse_main, fibre_ids)
    cross_coef = region_coef(diffuse_cross, fibre_ids)
    blocks = lend_block[0]
    alive = jnp.arange(cap_slots, dtype=jnp.int32)[None, :] < lend_count[0][:, None]
    target = jnp.where(alive, blocks, nblock).reshape(-1)
    sources = blocks.reshape(-1)
    on_loan = loan_states[0]
    loan_kinds = loan_tags[0]
    for step in range(STEPS):
        diffused = stencil(brick_faces(voltage), main_coef, cross_coef)
        lines = diffused.reshape(nblock, line)[sources].reshape(ncols, cap_slots, line)
        received = lax.all_to_all(lines, "cols", split_axis=0, concat_axis=0, tiled=True)
        states, current = react(states, diffused, cell_tags, *tables)
        on_loan, loan_current = react(on_loan, received, loan_kinds, *tables)
        back_current = lax.all_to_all(loan_current, "cols", split_axis=0, concat_axis=0, tiled=True)
        current = (
            current.reshape(nblock, line)
            .at[target]
            .set(back_current.reshape(-1, line), mode="drop")
            .reshape(depth_x, depth_y, line)
        )
        voltage = diffused - 0.25 * current
    back_states = lax.all_to_all(on_loan, "cols", split_axis=0, concat_axis=0, tiled=True)
    grouped = states.reshape(nblock, nstate, line)
    grouped = grouped.at[target].set(back_states.reshape(-1, nstate, line), mode="drop")
    return (voltage, grouped.reshape(depth_x, depth_y, nstate, line))


def solution(mesh):
    in_specs = (
        P("depth", "rows", "cols"),
        P("depth", "rows", None, "cols"),
        P("depth", "rows", "cols"),
        P("depth", "rows", "cols"),
        P(("depth", "rows", "cols"), None, None, None, None),
        P(("depth", "rows", "cols"), None, None, None),
        P(("depth", "rows", "cols"), None, None),
        P(("depth", "rows", "cols"), None),
        P(),
        P(),
        P(),
        P(),
        P(),
        P(),
        P(),
    )
    out_specs = (P("depth", "rows", "cols"), P("depth", "rows", None, "cols"))
    return jax.shard_map(local, mesh=mesh, in_specs=in_specs, out_specs=out_specs, check_vma=False)
```

profile of v0, /device:TPU:38, one launch (start us, length us, event | category | flops | bytes accessed | tf_op | source)
XLA Modules:
  0.0 228.8 jit_solution(812378173916621340)
XLA Ops:
  0.6 0.0 copy-start
  0.6 0.0 copy-start.2
  0.7 0.8 fusion.61
  1.4 1.3 collective-permute-start
  2.7 3.0 %collective-permute-start.1 = (f32[1,16,128]{2,1,0:T(8,128)S(1)}, f32[1,16,128]{2,1,0:T(8,128)S(1)}, u32[]{:S(2)}, u32[]{:S(2)}) collective-permute-start(f32[1,16,128]{2,1,0:T(8,128)S(1)} %get-tuple-element.40), channel_id=1, source_target_pairs={{0,128},{128,256},{256,384},{1,129},{129,257},{257,385},{2,130},{1... | collective-permute-start | bytes 24584 | tf_op jit(solution)/shard_map/ppermute | solution.py:20
  5.7 0.8 select_select_fusion.9
  6.5 0.8 select_select_fusion.8
  7.3 1.0 convolution_bitcast_fusion
  8.3 0.0 copy-start.3
  8.4 0.0 copy-start.1
  8.4 0.1 fusion.56
  8.4 1.1 fusion.6
  9.6 0.8 slice_bitcast_fusion.8
  10.4 0.8 slice_bitcast_fusion.2
  11.2 0.7 iota_compare_fusion.5
  11.9 0.1 lt.79
  12.0 0.8 copy.32
  12.8 0.1 squeeze.13
  12.9 0.8 constant_dynamic-update-slice_fusion.1
  13.6 2.7 %collective-permute-start.2 = (f32[6,1,128]{2,1,0:T(1,128)S(1)}, f32[6,1,128]{2,1,0:T(1,128)S(1)}, u32[]{:S(2)}, u32[]{:S(2)}) collective-permute-start(f32[6,1,128]{2,1,0:T(1,128)S(1)} %get-tuple-element.35), channel_id=1, source_target_pairs={{16,0},{32,16},{48,32},{64,48},{80,64},{96,80},{112,96},{17,1},{33... | collective-permute-start | bytes 9224 | tf_op jit(solution)/shard_map/ppermute | solution.py:21
  16.4 6.7 %collective-permute-start.3 = (f32[6,1,128]{2,1,0:T(1,128)S(1)}, f32[6,1,128]{2,1,0:T(1,128)S(1)}, u32[]{:S(2)}, u32[]{:S(2)}) collective-permute-start(f32[6,1,128]{2,1,0:T(1,128)S(1)} %get-tuple-element.36), channel_id=1, source_target_pairs={{0,16},{16,32},{32,48},{48,64},{64,80},{80,96},{96,112},{1,17},{17... | collective-permute-start | bytes 9224 | tf_op jit(solution)/shard_map/ppermute | solution.py:20
  23.1 1.3 collective-permute-done.3
  24.4 0.1 fusion.58
  24.5 2.0 collective-permute-start.4
  26.5 3.8 %collective-permute-start.5 = (f32[6,18,1]{2,1,0:T(8,128)S(1)}, f32[6,18,1]{2,1,0:T(8,128)S(1)}, u32[]{:S(2)}, u32[]{:S(2)}) collective-permute-start(f32[6,18,1]{2,1,0:T(8,128)S(1)} %get-tuple-element.26), channel_id=1, source_target_pairs={{0,1},{1,2},{2,3},{3,4},{4,5},{5,6},{6,7},{7,8},{8,9},{9,10},{10,1... | collective-permute-start | bytes 1304 | tf_op jit(solution)/shard_map/ppermute | solution.py:20
  30.4 0.4 collective-permute-done.4
  30.8 2.0 collective-permute-done.5
  32.8 0.1 pad_maximum_fusion
  32.9 0.1 fusion.17
  33.1 1.2 gather_fusion
  34.2 16.4 %all-to-all-start = ((f32[16,4,128]{2,1,0:T(4,128)}), f32[16,4,128]{2,1,0:T(4,128)S(1)}, u32[]{:S(2)}, u32[]{:S(2)}) async-start(f32[16,4,128]{2,1,0:T(4,128)} %bitcast.34), calls=%async_computation | async-start | bytes 65536 | tf_op jit(solution)/shard_map/all_to_all | solution.py:117
  50.7 11.4 %all-to-all-done = f32[16,4,128]{2,1,0:T(4,128)S(1)} async-done(((f32[16,4,128]{2,1,0:T(4,128)}), f32[16,4,128]{2,1,0:T(4,128)S(1)}, u32[]{:S(2)}, u32[]{:S(2)}) %all-to-all-start) | async-done | bytes 32800 | tf_op jit(solution)/shard_map/all_to_all | solution.py:117
  62.1 5.9 %multiply_reduce_fusion.2 = (f32[16,4,128]{2,1,0:T(4,128)}, f32[16,4,41,128]{3,1,2,0:T(4,128)S(1)}) fusion(f32[41]{0:T(128)S(1)} %get-tuple-element.54, f32[41]{0:T(128)S(1)} %get-tuple-element.55, f32[41]{0:T(128)S(1)} %get-tuple-element.53, f32[16,4,128]{2,1,0:T(4,128)S(1)} %all-to-all-done, f32[41]{0:T(128)S(1)} %get-tuple-element.51, ...), kind=kLoop, calls=%fused_computation.16 | loop fusion | flops 9396224 | bytes 2804124 | tf_op jit(solution)/shard_map/reduce_sum | solution.py:41
  68.0 4.5 %all-to-all-start.1 = ((f32[16,4,128]{2,1,0:T(4,128)}), f32[16,4,128]{2,1,0:T(4,128)S(1)}, u32[]{:S(2)}, u32[]{:S(2)}) async-start(f32[16,4,128]{2,1,0:T(4,128)} %get-tuple-element.10), calls=%async_computation.1 | async-start | bytes 65536 | tf_op jit(solution)/shard_map/all_to_all | solution.py:120
  72.6 3.4 %multiply_reduce_fusion.3 = (f32[4,16,128]{2,1,0:T(8,128)S(1)}, f32[4,16,41,128]{3,1,0,2:T(8,128)S(1)}) fusion(f32[41]{0:T(128)S(1)} %get-tuple-element.54, f32[41]{0:T(128)S(1)} %get-tuple-element.55, f32[41]{0:T(128)S(1)} %get-tuple-element.53, f32[4,16,128]{2,1,0:T(8,128)S(1)} %fusion.17, f32[41]{0:T(128)S(1)} %get-tuple-element.51, ...), kind=kLoop, calls=%fused_computation.24 | loop fusion | flops 9396224 | bytes 2804124 | tf_op jit(solution)/shard_map/reduce_sum | solution.py:41
  76.0 7.8 %all-to-all-done.1 = f32[16,4,128]{2,1,0:T(4,128)S(1)} async-done(((f32[16,4,128]{2,1,0:T(4,128)}), f32[16,4,128]{2,1,0:T(4,128)S(1)}, u32[]{:S(2)}, u32[]{:S(2)}) %all-to-all-start.1) | async-done | bytes 32800 | tf_op jit(solution)/shard_map/all_to_all | solution.py:120
  83.8 0.8 scatter_fusion
  84.6 1.3 collective-permute-start.7
  85.9 1.3 collective-permute-start.6
  87.2 3.6 %collective-permute-done.6 = f32[1,16,128]{2,1,0:T(8,128)S(1)} collective-permute-done((f32[1,16,128]{2,1,0:T(8,128)S(1)}, f32[1,16,128]{2,1,0:T(8,128)S(1)}, u32[]{:S(2)}, u32[]{:S(2)}) %collective-permute-start.6) | collective-permute-done | bytes 8224 | tf_op jit(solution)/shard_map/ppermute | solution.py:21
  90.8 8.4 %collective-permute-start.9 = (f32[6,1,128]{2,1,0:T(1,128)S(1)}, f32[6,1,128]{2,1,0:T(1,128)S(1)}, u32[]{:S(2)}, u32[]{:S(2)}) collective-permute-start(f32[6,1,128]{2,1,0:T(1,128)S(1)} %get-tuple-element.33), channel_id=1, source_target_pairs={{0,16},{16,32},{32,48},{48,64},{64,80},{80,96},{96,112},{1,17},{17... | collective-permute-start | bytes 9224 | tf_op jit(solution)/shard_map/ppermute | solution.py:20
  99.2 1.9 collective-permute-start.8
  101.1 7.2 %collective-permute-done.8 = f32[6,1,128]{2,1,0:T(1,128)S(1)} collective-permute-done((f32[6,1,128]{2,1,0:T(1,128)S(1)}, f32[6,1,128]{2,1,0:T(1,128)S(1)}, u32[]{:S(2)}, u32[]{:S(2)}) %collective-permute-start.8) | collective-permute-done | bytes 3104 | tf_op jit(solution)/shard_map/ppermute | solution.py:21
  108.3 0.1 fusion.57
  108.4 3.5 %collective-permute-start.10 = (f32[6,18,1]{2,1,0:T(8,128)S(1)}, f32[6,18,1]{2,1,0:T(8,128)S(1)}, u32[]{:S(2)}, u32[]{:S(2)}) collective-permute-start(f32[6,18,1]{2,1,0:T(8,128)S(1)} %get-tuple-element.23), channel_id=1, source_target_pairs={{1,0},{2,1},{3,2},{4,3},{5,4},{6,5},{7,6},{8,7},{9,8},{10,9},{11,1... | collective-permute-start | bytes 1304 | tf_op jit(solution)/shard_map/ppermute | solution.py:21
  111.9 2.4 %collective-permute-start.11 = (f32[6,18,1]{2,1,0:T(8,128)S(1)}, f32[6,18,1]{2,1,0:T(8,128)S(1)}, u32[]{:S(2)}, u32[]{:S(2)}) collective-permute-start(f32[6,18,1]{2,1,0:T(8,128)S(1)} %get-tuple-element.24), channel_id=1, source_target_pairs={{0,1},{1,2},{2,3},{3,4},{4,5},{5,6},{6,7},{7,8},{8,9},{9,10},{10,1... | collective-permute-start | bytes 1304 | tf_op jit(solution)/shard_map/ppermute | solution.py:20
  114.3 1.1 collective-permute-done.10
  115.4 3.2 %collective-permute-done.11 = f32[6,18,1]{2,1,0:T(8,128)S(1)} collective-permute-done((f32[6,18,1]{2,1,0:T(8,128)S(1)}, f32[6,18,1]{2,1,0:T(8,128)S(1)}, u32[]{:S(2)}, u32[]{:S(2)}) %collective-permute-start.11) | collective-permute-done | bytes 464 | tf_op jit(solution)/shard_map/ppermute | solution.py:20
  118.6 0.1 pad_maximum_fusion.1
  118.8 0.1 fusion.28
  118.9 0.6 gather_fusion.1
  119.5 17.4 %all_to_all.25 = f32[16,4,128]{2,1,0:T(4,128)S(1)} all-to-all(f32[16,4,128]{2,1,0:T(4,128)S(1)} %bitcast.125), channel_id=1, replica_groups=mesh['depth'=4,'rows'=8,'cols'=16] {'cols'}, dimensions={0} | all-to-all | bytes 65536 | tf_op jit(solution)/shard_map/all_to_all | solution.py:117
  136.9 6.0 %multiply_reduce_fusion = (f32[16,4,128]{2,1,0:T(4,128)S(1)}, f32[16,4,41,128]{3,1,2,0:T(4,128)}) fusion(f32[16,4,128]{2,1,0:T(4,128)S(1)} %all_to_all.25, f32[41]{0:T(128)S(1)} %get-tuple-element.54, f32[41]{0:T(128)S(1)} %get-tuple-element.55, f32[41]{0:T(128)S(1)} %get-tuple-element.53, f32[41]{0:T(128)S(1)} %get-tuple-element.51, ...), kind=kLoop, calls=%fused_computation.12 | loop fusion | flops 9396224 | bytes 2804124 | tf_op jit(solution)/shard_map/reduce_sum | solution.py:41
  142.9 14.8 %all_to_all.26 = f32[16,4,128]{2,1,0:T(4,128)S(1)} all-to-all(f32[16,4,128]{2,1,0:T(4,128)S(1)} %get-tuple-element.6), channel_id=1, replica_groups=mesh['depth'=4,'rows'=8,'cols'=16] {'cols'}, dimensions={0} | all-to-all | bytes 65536 | tf_op jit(solution)/shard_map/all_to_all | solution.py:120
  157.7 5.1 %all-to-all-start.4 = ((f32[16,4,41,128]{3,1,2,0:T(4,128)}), f32[16,4,41,128]{3,1,2,0:T(4,128)S(1)}, u32[]{:S(2)}, u32[]{:S(2)}) async-start(f32[16,4,41,128]{3,1,2,0:T(4,128)} %get-tuple-element.7), calls=%async_computation.4 | async-start | bytes 2686976 | tf_op jit(solution)/shard_map/all_to_all | solution.py:128
  162.8 1.7 multiply_reduce_fusion.1
  164.5 0.8 copy.34
  165.3 0.8 scatter_fusion.1
  166.2 0.6 sub.163
  166.8 56.0 %all-to-all-done.4 = f32[16,4,41,128]{3,1,2,0:T(4,128)S(1)} async-done(((f32[16,4,41,128]{3,1,2,0:T(4,128)}), f32[16,4,41,128]{3,1,2,0:T(4,128)S(1)}, u32[]{:S(2)}, u32[]{:S(2)}) %all-to-all-start.4) | async-done | bytes 1343520 | tf_op jit(solution)/shard_map/all_to_all | solution.py:128
  222.7 0.4 copy.33
  223.1 0.8 copy.35
  223.9 3.3 %scatter_fusion.2 = f32[64,41,128]{2,1,0:T(8,128)S(1)} fusion(f32[64,41,128]{2,1,0:T(8,128)S(1)} %copy.34, s32[64]{0:T(128)S(1)} %get-tuple-element.57, f32[64,41,128]{2,1,0:T(8,128)S(1)} %copy.35), kind=kCustom, calls=%fused_computation.4 | custom fusion | bytes 4030720 | tf_op jit(solution)/shard_map/scatter | solution.py:130
  227.3 1.5 copy.37
  (24 shorter events, 0.1 us)
Async XLA Ops:
  0.6 6.7 %copy-start = (f32[3,8]{1,0:T(4,128)S(1)}, f32[3,8]{1,0:T(4,128)}, u32[]{:S(2)}) copy-start(f32[3,8]{1,0:T(4,128)} %param.23) | copy-start | bytes 292
  0.6 32.3 %copy-start.2 = (f32[4,16,128]{2,1,0:T(8,128)S(1)}, f32[4,16,128]{2,1,0:T(8,128)}, u32[]{:S(2)}) copy-start(f32[4,16,128]{2,1,0:T(8,128)} %param.15) | copy-start | bytes 98308
  1.4 12.2 %collective-permute-start = (f32[1,16,128]{2,1,0:T(8,128)S(1)}, f32[1,16,128]{2,1,0:T(8,128)S(1)}, u32[]{:S(2)}, u32[]{:S(2)}) collective-permute-start(f32[1,16,128]{2,1,0:T(8,128)S(1)} %get-tuple-element.39), channel_id=1, source_target_pairs={{128,0},{256,128},{384,256},{129,1},{257,129},{385,257},{130,2},{2... | collective-permute-start | bytes 24584 | tf_op jit(solution)/shard_map/ppermute | solution.py:21
  2.7 10.1 %collective-permute-start.1 = (f32[1,16,128]{2,1,0:T(8,128)S(1)}, f32[1,16,128]{2,1,0:T(8,128)S(1)}, u32[]{:S(2)}, u32[]{:S(2)}) collective-permute-start(f32[1,16,128]{2,1,0:T(8,128)S(1)} %get-tuple-element.40), channel_id=1, source_target_pairs={{0,128},{128,256},{256,384},{1,129},{129,257},{257,385},{2,130},{1... | collective-permute-start | bytes 24584 | tf_op jit(solution)/shard_map/ppermute | solution.py:20
  8.3 42.3 %copy-start.3 = (f32[3,41]{1,0:T(4,128)S(1)}, f32[3,41]{1,0:T(4,128)}, u32[]{:S(2)}) copy-start(f32[3,41]{1,0:T(4,128)} %param.28) | copy-start | bytes 1480
  8.4 53.8 %copy-start.1 = (f32[1,16,4,41,128]{4,2,3,1,0:T(4,128)S(1)}, f32[1,16,4,41,128]{4,2,3,1,0:T(4,128)}, u32[]{:S(2)}) copy-start(f32[1,16,4,41,128]{4,2,3,1,0:T(4,128)} %param.19) | copy-start | bytes 4030468
  13.6 9.5 %collective-permute-start.2 = (f32[6,1,128]{2,1,0:T(1,128)S(1)}, f32[6,1,128]{2,1,0:T(1,128)S(1)}, u32[]{:S(2)}, u32[]{:S(2)}) collective-permute-start(f32[6,1,128]{2,1,0:T(1,128)S(1)} %get-tuple-element.35), channel_id=1, source_target_pairs={{16,0},{32,16},{48,32},{64,48},{80,64},{96,80},{112,96},{17,1},{33... | collective-permute-start | bytes 9224 | tf_op jit(solution)/shard_map/ppermute | solution.py:21
  16.4 8.0 %collective-permute-start.3 = (f32[6,1,128]{2,1,0:T(1,128)S(1)}, f32[6,1,128]{2,1,0:T(1,128)S(1)}, u32[]{:S(2)}, u32[]{:S(2)}) collective-permute-start(f32[6,1,128]{2,1,0:T(1,128)S(1)} %get-tuple-element.36), channel_id=1, source_target_pairs={{0,16},{16,32},{32,48},{48,64},{64,80},{80,96},{96,112},{1,17},{17... | collective-permute-start | bytes 9224 | tf_op jit(solution)/shard_map/ppermute | solution.py:20
  24.5 6.3 %collective-permute-start.4 = (f32[6,18,1]{2,1,0:T(8,128)S(1)}, f32[6,18,1]{2,1,0:T(8,128)S(1)}, u32[]{:S(2)}, u32[]{:S(2)}) collective-permute-start(f32[6,18,1]{2,1,0:T(8,128)S(1)} %get-tuple-element.25), channel_id=1, source_target_pairs={{1,0},{2,1},{3,2},{4,3},{5,4},{6,5},{7,6},{8,7},{9,8},{10,9},{11,1... | collective-permute-start | bytes 1304 | tf_op jit(solution)/shard_map/ppermute | solution.py:21
  26.5 6.2 %collective-permute-start.5 = (f32[6,18,1]{2,1,0:T(8,128)S(1)}, f32[6,18,1]{2,1,0:T(8,128)S(1)}, u32[]{:S(2)}, u32[]{:S(2)}) collective-permute-start(f32[6,18,1]{2,1,0:T(8,128)S(1)} %get-tuple-element.26), channel_id=1, source_target_pairs={{0,1},{1,2},{2,3},{3,4},{4,5},{5,6},{6,7},{7,8},{8,9},{9,10},{10,1... | collective-permute-start | bytes 1304 | tf_op jit(solution)/shard_map/ppermute | solution.py:20
  34.2 27.9 %all-to-all-start = ((f32[16,4,128]{2,1,0:T(4,128)}), f32[16,4,128]{2,1,0:T(4,128)S(1)}, u32[]{:S(2)}, u32[]{:S(2)}) async-start(f32[16,4,128]{2,1,0:T(4,128)} %bitcast.34), calls=%async_computation | async-start | bytes 65536 | tf_op jit(solution)/shard_map/all_to_all | solution.py:117
  68.0 15.8 %all-to-all-start.1 = ((f32[16,4,128]{2,1,0:T(4,128)}), f32[16,4,128]{2,1,0:T(4,128)S(1)}, u32[]{:S(2)}, u32[]{:S(2)}) async-start(f32[16,4,128]{2,1,0:T(4,128)} %get-tuple-element.10), calls=%async_computation.1 | async-start | bytes 65536 | tf_op jit(solution)/shard_map/all_to_all | solution.py:120
  84.6 2.6 %collective-permute-start.7 = (f32[1,16,128]{2,1,0:T(8,128)S(1)}, f32[1,16,128]{2,1,0:T(8,128)S(1)}, u32[]{:S(2)}, u32[]{:S(2)}) collective-permute-start(f32[1,16,128]{2,1,0:T(8,128)S(1)} %get-tuple-element.37), channel_id=1, source_target_pairs={{0,128},{128,256},{256,384},{1,129},{129,257},{257,385},{2,130},{1... | collective-permute-start | bytes 24584 | tf_op jit(solution)/shard_map/ppermute | solution.py:20
  85.9 4.9 %collective-permute-start.6 = (f32[1,16,128]{2,1,0:T(8,128)S(1)}, f32[1,16,128]{2,1,0:T(8,128)S(1)}, u32[]{:S(2)}, u32[]{:S(2)}) collective-permute-start(f32[1,16,128]{2,1,0:T(8,128)S(1)} %get-tuple-element.38), channel_id=1, source_target_pairs={{128,0},{256,128},{384,256},{129,1},{257,129},{385,257},{130,2},{2... | collective-permute-start | bytes 24584 | tf_op jit(solution)/shard_map/ppermute | solution.py:21
  90.8 10.3 %collective-permute-start.9 = (f32[6,1,128]{2,1,0:T(1,128)S(1)}, f32[6,1,128]{2,1,0:T(1,128)S(1)}, u32[]{:S(2)}, u32[]{:S(2)}) collective-permute-start(f32[6,1,128]{2,1,0:T(1,128)S(1)} %get-tuple-element.33), channel_id=1, source_target_pairs={{0,16},{16,32},{32,48},{48,64},{64,80},{80,96},{96,112},{1,17},{17... | collective-permute-start | bytes 9224 | tf_op jit(solution)/shard_map/ppermute | solution.py:20
  99.2 9.1 %collective-permute-start.8 = (f32[6,1,128]{2,1,0:T(1,128)S(1)}, f32[6,1,128]{2,1,0:T(1,128)S(1)}, u32[]{:S(2)}, u32[]{:S(2)}) collective-permute-start(f32[6,1,128]{2,1,0:T(1,128)S(1)} %get-tuple-element.34), channel_id=1, source_target_pairs={{16,0},{32,16},{48,32},{64,48},{80,64},{96,80},{112,96},{17,1},{33... | collective-permute-start | bytes 9224 | tf_op jit(solution)/shard_map/ppermute | solution.py:21
  108.4 7.0 %collective-permute-start.10 = (f32[6,18,1]{2,1,0:T(8,128)S(1)}, f32[6,18,1]{2,1,0:T(8,128)S(1)}, u32[]{:S(2)}, u32[]{:S(2)}) collective-permute-start(f32[6,18,1]{2,1,0:T(8,128)S(1)} %get-tuple-element.23), channel_id=1, source_target_pairs={{1,0},{2,1},{3,2},{4,3},{5,4},{6,5},{7,6},{8,7},{9,8},{10,9},{11,1... | collective-permute-start | bytes 1304 | tf_op jit(solution)/shard_map/ppermute | solution.py:21
  111.9 6.8 %collective-permute-start.11 = (f32[6,18,1]{2,1,0:T(8,128)S(1)}, f32[6,18,1]{2,1,0:T(8,128)S(1)}, u32[]{:S(2)}, u32[]{:S(2)}) collective-permute-start(f32[6,18,1]{2,1,0:T(8,128)S(1)} %get-tuple-element.24), channel_id=1, source_target_pairs={{0,1},{1,2},{2,3},{3,4},{4,5},{5,6},{6,7},{7,8},{8,9},{9,10},{10,1... | collective-permute-start | bytes 1304 | tf_op jit(solution)/shard_map/ppermute | solution.py:20
  157.7 65.0 %all-to-all-start.4 = ((f32[16,4,41,128]{3,1,2,0:T(4,128)}), f32[16,4,41,128]{3,1,2,0:T(4,128)S(1)}, u32[]{:S(2)}, u32[]{:S(2)}) async-start(f32[16,4,41,128]{3,1,2,0:T(4,128)} %get-tuple-element.7), calls=%async_computation.4 | async-start | bytes 2686976 | tf_op jit(solution)/shard_map/all_to_all | solution.py:128
where the time goes:
time: 230 us; the launch traced here: 229 us
  waiting for transfers between devices  94 us (41%)
  starting transfers between devices  64.4 us (28%)
  blocking collectives  32.2 us (14%)
  other arithmetic  20.6 us (9%)
  local copies, waits for them, and re-layouts  14.5 us (6%)
    all_to_all x1, waiting for transfers between devices, local(): lax.all_to_all(on_loan, 'cols', split_axis=0, concat_axis=0, tiled=True)  56 us
    ppermute x6, starting transfers between devices, with_halo(): before = lax.ppermute(last, axis, up)  25.6 us
    all_to_all x1, blocking collectives, local(): lax.all_to_all(lines, 'cols', split_axis=0, concat_axis=0, tiled=True)  17.4 us
    reduce_sum x4, other arithmetic, react(): jnp.sum(select_rows(conductance, kinds) * fresh * (level - select_rows(re...  17.1 us
    all_to_all x1, starting transfers between devices, local(): lax.all_to_all(lines, 'cols', split_axis=0, concat_axis=0, tiled=True)  16.4 us
    all_to_all x1, blocking collectives, local(): lax.all_to_all(loan_current, 'cols', split_axis=0, concat_axis=0, tiled=T...  14.8 us
    ppermute x6, starting transfers between devices, with_halo(): after = lax.ppermute(leading, axis, down)  12.7 us
    ppermute x6, waiting for transfers between devices, with_halo(): after = lax.ppermute(leading, axis, down)  12.3 us
  transfers between devices with their start and end apart: 15, of which 10 were waited for; matrix products, arithmetic and copies ran while one was open for 7% of the time, Pallas kernels for 0%

commit v1 on v0

v1 whole, which is shorter than its diff:
```python
import jax
import jax.numpy as jnp
from jax import lax
from jax.experimental import pallas as pl
from jax.experimental.pallas import tpu as pltpu
from jax.sharding import PartitionSpec as P

STATES = 41
ATRIAL = 21
SCAR = 5
REGIONS = 8
HALF = 8
ROWS = 168
BLOCKS = 64

EARLY = (7, 6, 3, 2, 1, 0)
LATE = (5, 4)

VMEM = pl.BlockSpec(memory_space=pltpu.VMEM)
SMEM = pl.BlockSpec(memory_space=pltpu.SMEM)


def to_heavy(m):
    return [(HALF + i, i ^ m) for i in range(HALF)]


def to_light(m):
    return [(i ^ m, HALF + i) for i in range(HALF)]


def f32(*shape):
    return jax.ShapeDtypeStruct(shape, jnp.float32)


def partner(plan_ref, m):
    return HALF + jnp.bitwise_xor(plan_ref[80], m)


def gate(state, level, half, slope, rate, weight, rest):
    bent = (level - half) * slope
    steady = 0.5 + 0.5 * jnp.tanh(bent)
    decay = jnp.exp(rate * (1.0 + 0.5 * jnp.tanh(bent + bent)))
    fresh = steady + (state - steady) * decay
    return fresh, weight * fresh * (level - rest)


def react_home(tab_ref, in_ref, level, tags, out_ref):
    first, second = tags == 0, tags == 1
    current = jnp.zeros_like(level)
    for k in range(STATES):
        table = [[tab_ref[(t * 3 + m) * STATES + k] for m in range(3)] for t in range(5)]
        if k < SCAR:
            args = [jnp.where(first, a, jnp.where(second, b, c)) for a, b, c in table]
        elif k < ATRIAL:
            args = [jnp.where(first, a, b) for a, b, c in table]
        else:
            args = [a for a, b, c in table]
        rows = [(x * STATES + k) * 16 for x in range(4)]
        state = jnp.concatenate([in_ref[r : r + 16, :] for r in rows], axis=0)
        fresh, part = gate(state, level, *args)
        if k >= SCAR:
            live = first if k >= ATRIAL else tags != 2
            fresh = jnp.where(live, fresh, 0.0)
            part = jnp.where(live, part, 0.0)
        current = current + part
        for x in range(4):
            out_ref[rows[x] : rows[x] + 16, :] = fresh[16 * x : 16 * x + 16, :]
    return current


def react_lent(tab_ref, in_refs, levels, out_refs):
    low = lax.broadcasted_iota(jnp.int32, (8, 128), 0) < 4
    tags, currents = [], []
    for ref in in_refs:
        last = ref[ROWS - 8 : ROWS, :]
        tags.append(jnp.where(low, pltpu.roll(last, 4, 0), last))
        currents.append(jnp.zeros((8, 128), jnp.float32))
    for r in range(ROWS // 8):
        k0, k1 = 2 * r, min(2 * r + 1, STATES - 1)
        models = 3 if k0 < SCAR else 2 if k0 < ATRIAL else 1
        table = [
            [
                jnp.where(low, tab_ref[(t * 3 + m) * STATES + k0], tab_ref[(t * 3 + m) * STATES + k1])
                for m in range(models)
            ]
            for t in range(5)
        ]
        for j, ref in enumerate(in_refs):
            kind = tags[j]
            if models == 3:
                args = [jnp.where(kind == 0.0, a, jnp.where(kind == 1.0, b, c)) for a, b, c in table]
            elif models == 2:
                args = [jnp.where(kind == 0.0, a, b) for a, b in table]
            else:
                args = [a for (a,) in table]
            state = ref[8 * r : 8 * r + 8, :]
            fresh, part = gate(state, levels[j], *args)
            if k1 >= SCAR:
                top0 = 2.5 if k0 < SCAR else 1.5 if k0 < ATRIAL else 0.5
                top1 = 2.5 if k1 < SCAR else 1.5 if k1 < ATRIAL else 0.5
                if 2 * r + 1 >= STATES:
                    top1 = -1.0
                live = kind < (top0 if top0 == top1 else jnp.where(low, top0, top1))
                fresh = jnp.where(live, fresh, 0.0)
                part = jnp.where(live, part, 0.0)
            currents[j] = currents[j] + part
            if out_refs is not None:
                if 2 * r + 1 >= STATES:
                    fresh = jnp.where(low, fresh, state)
                out_refs[j][8 * r : 8 * r + 8, :] = fresh
    return [c + pltpu.roll(c, 4, 0) for c in currents]


def gather_lines(plan_ref, m, line_ref, hold_ref):
    p = partner(plan_ref, m)
    for s in range(4):
        row = line_ref[pl.ds(plan_ref[p * 4 + s], 1), :]
        hold_ref[s : s + 1, :] = row
        hold_ref[4 + s : 5 + s, :] = row
    return hold_ref[...]


def put_lines(plan_ref, m, hold_ref, value, line_ref):
    hold_ref[...] = value
    p = partner(plan_ref, m)
    for s in range(4):

        @pl.when(s < plan_ref[64 + p])
        def _():
            line_ref[pl.ds(plan_ref[p * 4 + s], 1), :] = hold_ref[s : s + 1, :]


def put_states(plan_ref, m, message_ref, out_ref):
    p = partner(plan_ref, m)
    for s in range(4):

        @pl.when(s < plan_ref[64 + p])
        def _():
            block = plan_ref[p * 4 + s]
            start = (block // 16) * (STATES * 16) + block % 16
            out_ref[pl.ds(start, STATES, stride=16), :] = message_ref[pl.ds(s, STATES, stride=4), :]


def stencil(coef_ref, planes_ref, before_ref, after_ref, fibre_ref, out_ref):
    lane = lax.broadcasted_iota(jnp.int32, (18, 128), 1)
    planes, slopes, sums = [], [], []
    for x in range(6):
        plane = planes_ref[x]
        lower = jnp.where(lane == 0, before_ref[x], pltpu.roll(plane, 1, 1))
        upper = jnp.where(lane == 127, after_ref[x], pltpu.roll(plane, 127, 1))
        planes.append(plane)
        slopes.append(upper - lower)
        sums.append(upper + lower)
    for x in range(1, 5):
        fibre = fibre_ref[x - 1]

        def coef(row):
            value = jnp.full((16, 128), coef_ref[row * REGIONS])
            for r in range(1, REGIONS):
                value = jnp.where(fibre == r, coef_ref[row * REGIONS + r], value)
            return value

        here, left, right = planes[x], planes[x - 1], planes[x + 1]
        centre = here[1:17]
        twice = 2.0 * centre
        total = coef(0) * (right[1:17] + left[1:17] - twice)
        total = total + coef(1) * (here[2:18] + here[0:16] - twice)
        total = total + coef(2) * (sums[x][1:17] - twice)
        total = total + 0.5 * coef(3) * (right[2:18] - right[0:16] - left[2:18] + left[0:16])
        total = total + 0.5 * coef(4) * (slopes[x + 1][1:17] - slopes[x - 1][1:17])
        total = total + 0.5 * coef(5) * (slopes[x][2:18] - slopes[x][0:16])
        out_ref[16 * (x - 1) : 16 * x, :] = centre + total


def diffuse_kernel(plan_ref, coef_ref, planes_ref, before_ref, after_ref, fibre_ref, out_ref, *line_refs):
    stencil(coef_ref, planes_ref, before_ref, after_ref, fibre_ref, out_ref)
    for m, ref in zip(LATE, line_refs):
        p = partner(plan_ref, m)
        for s in range(4):
            ref[s : s + 1, :] = out_ref[pl.ds(plan_ref[p * 4 + s], 1), :]


def home_kernel(tab_ref, states_ref, level_ref, tags_ref, out_ref, current_ref):
    current_ref[...] = react_home(tab_ref, states_ref, level_ref[...], tags_ref[...], out_ref)


def lender_kernel(tab_ref, *refs):
    n = len(LATE)
    messages, lines, outs, hold_ref = refs[:n], refs[n : 2 * n], refs[2 * n : 3 * n], refs[3 * n]
    levels = []
    for ref in lines:
        hold_ref[0:4, :] = ref[...]
        hold_ref[4:8, :] = ref[...]
        levels.append(hold_ref[...])
    for ref, current in zip(outs, react_lent(tab_ref, messages, levels, None)):
        ref[...] = current[0:4, :]


def first_kernel(plan_ref, tab_ref, level_ref, current_ref, *refs):
    n, l = len(EARLY), len(LATE)
    messages, lent = refs[:n], refs[n : n + l]
    out_ref, fresh = refs[n + l], refs[n + l + 1 : 2 * n + l + 1]
    hold_ref, sum_ref = refs[2 * n + l + 1 :]
    sum_ref[...] = current_ref[...]
    levels = [gather_lines(plan_ref, m, level_ref, hold_ref) for m in EARLY]
    currents = react_lent(tab_ref, messages, levels, fresh)
    for m, value in zip(EARLY, currents):
        put_lines(plan_ref, m, hold_ref, value, sum_ref)
    for m, ref in zip(LATE, lent):
        hold_ref[0:4, :] = ref[...]
        put_lines(plan_ref, m, hold_ref, hold_ref[...], sum_ref)
    out_ref[...] = level_ref[...] - 0.25 * sum_ref[...]


def second_kernel(plan_ref, tab_ref, coef_ref, planes_ref, before_ref, after_ref, fibre_ref, states_ref, tags_ref, *refs):
    n = len(EARLY)
    messages = refs[:n]
    level_ref, volt_ref, out_ref = refs[n : n + 3]
    hold_ref, sum_ref = refs[n + 3 : n + 5]
    fresh = refs[n + 5 :]
    stencil(coef_ref, planes_ref, before_ref, after_ref, fibre_ref, level_ref)
    sum_ref[...] = react_home(tab_ref, states_ref, level_ref[...], tags_ref[...], out_ref)
    levels = [gather_lines(plan_ref, m, level_ref, hold_ref) for m in EARLY]
    currents = react_lent(tab_ref, messages, levels, fresh)
    for m, value, ref in zip(EARLY, currents, fresh):
        put_lines(plan_ref, m, hold_ref, value, sum_ref)
        put_states(plan_ref, m, ref, out_ref)
    volt_ref[...] = level_ref[...] - 0.25 * sum_ref[...]


def last_kernel(plan_ref, tab_ref, first_ref, second_ref, volt_in, states_in, *refs):
    l = len(LATE)
    messages, (volt_ref, out_ref, hold_ref), fresh = refs[:l], refs[l : l + 3], refs[l + 3 :]
    volt_ref[...] = volt_in[...]
    out_ref[...] = states_in[...]
    levels = [gather_lines(plan_ref, m, first_ref, hold_ref) for m in LATE]
    react_lent(tab_ref, messages, levels, fresh)
    levels = [gather_lines(plan_ref, m, second_ref, hold_ref) for m in LATE]
    currents = react_lent(tab_ref, fresh, levels, fresh)
    for m, level, value, ref in zip(LATE, levels, currents, fresh):
        put_lines(plan_ref, m, hold_ref, level - 0.25 * value, volt_ref)
        put_states(plan_ref, m, ref, out_ref)


def call(body, outs, ins, scratch=(), flops=0, **kwargs):
    size = sum(4 * v.size for v in ins) + sum(4 * v.size for v in outs)
    return pl.pallas_call(
        body,
        out_shape=tuple(outs),
        in_specs=[SMEM if v.ndim == 1 else VMEM for v in ins],
        out_specs=tuple(VMEM for _ in outs),
        scratch_shapes=[pltpu.VMEM(s, jnp.float32) for s in scratch],
        compiler_params=pltpu.CompilerParams(vmem_limit_bytes=32 * 1024 * 1024),
        cost_estimate=pl.CostEstimate(flops=flops, bytes_accessed=size, transcendentals=0),
        **kwargs,
    )(*ins)


def shift(value, axis):
    peers = lax.axis_size(axis)
    return (
        lax.ppermute(value[0], axis, [(i, i + 1) for i in range(peers - 1)]),
        lax.ppermute(value[1], axis, [(i + 1, i) for i in range(peers - 1)]),
    )


def halo(field):
    before, after = shift((field[-1:], field[:1]), "depth")
    field = jnp.concatenate([before, field, after], axis=0)
    before, after = shift((field[:, -1:], field[:, :1]), "rows")
    field = jnp.concatenate([before, field, after], axis=1)
    before, after = shift((field[:, :, 127], field[:, :, 0]), "cols")
    return field, before[..., None], after[..., None]


def tied(value, *others):
    return lax.optimization_barrier((value, *others))[0]


def local(
    voltage,
    states,
    cell_tags,
    fibre_ids,
    loan_states,
    loan_tags,
    lend_block,
    lend_count,
    diffuse_main,
    diffuse_cross,
    gate_half,
    gate_slope,
    gate_rate,
    conductance,
    reversal,
):
    line = (BLOCKS, 128)
    own = lax.axis_index("cols") % HALF
    plan = jnp.concatenate([lend_block.reshape(-1), lend_count.reshape(-1), own[None].astype(jnp.int32)])
    table = jnp.concatenate(
        [t.reshape(-1) for t in (gate_half, 0.5 / gate_slope, -gate_rate, conductance, reversal)]
    )
    coef = jnp.concatenate([diffuse_main.reshape(-1), diffuse_cross.reshape(-1)])
    home = states.transpose(0, 2, 1, 3).reshape(4 * STATES * 16, 128)
    tags = cell_tags.reshape(line)

    held = loan_states[0].transpose(0, 2, 1, 3)
    held_tags = loan_tags[0].astype(jnp.float32)
    message = {}
    for m in EARLY + LATE:
        source = jnp.bitwise_xor(own, m)
        body = lax.dynamic_index_in_dim(held, source, 0, keepdims=False).reshape(STATES * 4, 128)
        kinds = lax.dynamic_index_in_dim(held_tags, source, 0, keepdims=False)
        message[m] = jnp.concatenate([body, kinds], axis=0)

    got = {}
    for m in EARLY[:3]:
        got[m] = lax.ppermute(message[m], "cols", to_heavy(m))
    diffused, *lines = call(
        diffuse_kernel,
        [f32(*line)] + [f32(4, 128) for _ in LATE],
        [plan, coef, *halo(voltage), fibre_ids],
    )
    lines = [lax.ppermute(v, "cols", to_light(m)) for m, v in zip(LATE, lines)]
    for m in EARLY[3:]:
        got[m] = lax.ppermute(tied(message[m], diffused), "cols", to_heavy(m))
    first, current = call(home_kernel, [f32(*home.shape), f32(*line)], [table, home, diffused, tags])
    back = call(
        lender_kernel,
        [f32(4, 128) for _ in LATE],
        [table, *(message[m] for m in LATE), *lines],
        scratch=[(8, 128)],
    )
    back = [lax.ppermute(v, "cols", to_heavy(m)) for m, v in zip(LATE, back)]
    for m in LATE:
        got[m] = lax.ppermute(tied(message[m], got[EARLY[3]], *back), "cols", to_heavy(m))
    volt, *fresh = call(
        first_kernel,
        [f32(*line)] + [f32(ROWS, 128) for _ in EARLY],
        [plan, table, diffused, current, *(got[m] for m in EARLY), *back],
        scratch=[(8, 128), line],
    )
    again, volt, out = call(
        second_kernel,
        [f32(*line), f32(*line), f32(*home.shape)],
        [plan, table, coef, *halo(volt.reshape(4, 16, 128)), fibre_ids, first, tags, *fresh],
        scratch=[(8, 128), line] + [(ROWS, 128) for _ in EARLY],
    )
    volt, out = call(
        last_kernel,
        [f32(*line), f32(*home.shape)],
        [plan, table, diffused, again, volt, out, *(got[m] for m in LATE)],
        scratch=[(8, 128)] + [(ROWS, 128) for _ in LATE],
    )
    return volt.reshape(4, 16, 128), out.reshape(4, STATES, 16, 128).transpose(0, 2, 1, 3)


def solution(mesh):
    brick = P("depth", "rows", "cols")
    every = ("depth", "rows", "cols")
    in_specs = (
        brick,
        P("depth", "rows", None, "cols"),
        brick,
        brick,
        P(every, None, None, None, None),
        P(every, None, None, None),
        P(every, None, None),
        P(every, None),
    ) + (P(),) * 7
    out_specs = (brick, P("depth", "rows", None, "cols"))
    return jax.shard_map(local, mesh=mesh, in_specs=in_specs, out_specs=out_specs, check_vma=False)
```

time: 230 us -> 130 us (0.57)
  the two profiles are of different devices: /device:TPU:38 before, /device:TPU:113 now
where the time goes in v1:
time: 130 us; the launch traced here: 129 us
  starting transfers between devices  72.4 us (56%)
  waiting for transfers between devices  40.1 us (31%)
  Pallas kernels  9.93 us (8%)
  local copies, waits for them, and re-layouts  4 us (3%)
  other arithmetic  1.67 us (1%)
  between operations  1.3 us (1%)
    ppermute x6, starting transfers between devices, shift(): lax.ppermute(value[1], axis, [(i + 1, i) for i in range(peers - 1)])  26.6 us
    ppermute x3, waiting for transfers between devices, local(): got[m] = lax.ppermute(tied(message[m], diffused), 'cols', to_heavy(m))  22.2 us
    ppermute x6, starting transfers between devices, shift(): lax.ppermute(value[0], axis, [(i, i + 1) for i in range(peers - 1)])  18.5 us
    ppermute x2, starting transfers between devices, local(): lines = [lax.ppermute(v, 'cols', to_light(m)) for m, v in zip(LATE, lines)]  14.5 us
    pallas_call x6, Pallas kernels, call(): pl.pallas_call(body, out_shape=tuple(outs), in_specs=[SMEM if v.ndim == 1...  9.93 us
    ppermute x2, waiting for transfers between devices, local(): lax.ppermute(tied(message[m], got[EARLY[3]], *back), 'cols', to_heavy(m))  6.66 us
    ppermute x2, waiting for transfers between devices, local(): back = [lax.ppermute(v, 'cols', to_heavy(m)) for m, v in zip(LATE, back)]  6.52 us
    ppermute x6, waiting for transfers between devices, shift(): lax.ppermute(value[1], axis, [(i + 1, i) for i in range(peers - 1)])  3.97 us
  transfers between devices with their start and end apart: 24, of which 9 were waited for; matrix products, arithmetic and copies ran while one was open for 4% of the time, Pallas kernels for 5%

profile of v1, /device:TPU:113, one launch (start us, length us, event | category | flops | bytes accessed | tf_op | source)
XLA Modules:
  0.0 129.4 jit_solution(12388810705583061934)
XLA Ops:
  0.6 0.7 fusion.9
  1.4 2.6 %collective-permute-start.1 = (f32[1,16,128]{2,1,0:T(8,128)S(1)}, f32[1,16,128]{2,1,0:T(8,128)S(1)}, u32[]{:S(2)}, u32[]{:S(2)}) collective-permute-start(f32[1,16,128]{2,1,0:T(8,128)S(1)} %get-tuple-element.76), channel_id=1, source_target_pairs={{128,0},{256,128},{384,256},{129,1},{257,129},{385,257},{130,2},{2... | collective-permute-start | bytes 24584 | tf_op jit(solution)/shard_map/ppermute | solution.py:263
  3.9 3.0 %collective-permute-start = (f32[1,16,128]{2,1,0:T(8,128)S(1)}, f32[1,16,128]{2,1,0:T(8,128)S(1)}, u32[]{:S(2)}, u32[]{:S(2)}) collective-permute-start(f32[1,16,128]{2,1,0:T(8,128)S(1)} %get-tuple-element.77), channel_id=1, source_target_pairs={{0,128},{128,256},{256,384},{1,129},{129,257},{257,385},{2,130},{1... | collective-permute-start | bytes 24584 | tf_op jit(solution)/shard_map/ppermute | solution.py:262
  7.0 0.8 convert_element_type.4
  7.8 0.0 copy-start.5
  7.8 0.0 copy-start.4
  7.8 1.2 dynamic-slice_bitcast_fusion
  9.0 0.0 copy-start.12
  9.1 1.3 collective-permute-start.6
  10.5 1.3 collective-permute-start.7
  11.9 1.3 collective-permute-start.8
  13.3 0.7 pad_maximum_fusion.3
  14.0 0.1 reshape.128
  14.0 0.1 reshape.129
  14.2 3.1 %collective-permute-start.2 = (f32[6,1,128]{2,1,0:T(1,128)S(1)}, f32[6,1,128]{2,1,0:T(1,128)S(1)}, u32[]{:S(2)}, u32[]{:S(2)}) collective-permute-start(f32[6,1,128]{2,1,0:T(1,128)S(1)} %get-tuple-element.64), channel_id=1, source_target_pairs={{0,16},{16,32},{32,48},{48,64},{64,80},{80,96},{96,112},{1,17},{17... | collective-permute-start | bytes 9224 | tf_op jit(solution)/shard_map/ppermute | solution.py:262
  17.3 5.8 %collective-permute-start.3 = (f32[6,1,128]{2,1,0:T(1,128)S(1)}, f32[6,1,128]{2,1,0:T(1,128)S(1)}, u32[]{:S(2)}, u32[]{:S(2)}) collective-permute-start(f32[6,1,128]{2,1,0:T(1,128)S(1)} %get-tuple-element.65), channel_id=1, source_target_pairs={{16,0},{32,16},{48,32},{64,48},{80,64},{96,80},{112,96},{17,1},{33... | collective-permute-start | bytes 9224 | tf_op jit(solution)/shard_map/ppermute | solution.py:263
  23.1 0.1 pad_maximum_fusion.13.coef_ref
  23.2 0.1 copy.22
  23.3 0.1 reshape.121
  23.4 0.5 collective-permute-done.3
  23.8 0.2 slice_reduce_fusion.2
  24.0 1.9 %collective-permute-start.5 = (f32[6,18]{1,0:T(8,128)S(1)}, f32[6,18]{1,0:T(8,128)S(1)}, u32[]{:S(2)}, u32[]{:S(2)}) collective-permute-start(f32[6,18]{1,0:T(8,128)S(1)} %get-tuple-element.52), channel_id=1, source_target_pairs={{1,0},{2,1},{3,2},{4,3},{5,4},{6,5},{7,6},{8,7},{9,8},{10,9},{11,1... | collective-permute-start | bytes 1304 | tf_op jit(solution)/shard_map/ppermute | solution.py:263
  25.9 4.8 %collective-permute-start.4 = (f32[6,18]{1,0:T(8,128)S(1)}, f32[6,18]{1,0:T(8,128)S(1)}, u32[]{:S(2)}, u32[]{:S(2)}) collective-permute-start(f32[6,18]{1,0:T(8,128)S(1)} %get-tuple-element.53), channel_id=1, source_target_pairs={{0,1},{1,2},{2,3},{3,4},{4,5},{5,6},{6,7},{7,8},{8,9},{9,10},{10,1... | collective-permute-start | bytes 1304 | tf_op jit(solution)/shard_map/ppermute | solution.py:262
  30.7 0.1 pad_add_fusion.plan_ref
  30.9 0.6 collective-permute-done.4
  31.4 0.1 copy.23.before_ref
  31.6 0.1 copy.24.after_ref
  31.7 0.7 shard_map.158
  32.4 13.2 %collective-permute-start.12 = (f32[4,128]{1,0:T(4,128)S(1)}, f32[4,128]{1,0:T(4,128)S(1)}, u32[]{:S(2)}, u32[]{:S(2)}) collective-permute-start(f32[4,128]{1,0:T(4,128)S(1)} %get-tuple-element.31), channel_id=1, source_target_pairs={{5,8},{4,9},{7,10},{6,11},{1,12},{0,13},{3,14},{2,15},{21,24},{20,... | collective-permute-start | bytes 6152 | tf_op jit(solution)/shard_map/ppermute | solution.py:324
  45.6 1.3 collective-permute-start.13
  47.0 0.1 reshape.123
  47.0 0.1 reshape.126
  47.1 0.1 reshape.127
  47.2 0.1 reshape.124
  47.3 0.1 reshape.125
  47.4 0.1 concatenate.46.tab_ref
  47.5 0.1 collective-permute-done.13.refs_3_
  47.6 0.8 shard_map.160
  48.4 1.3 collective-permute-start.14
  49.7 1.3 collective-permute-start.15
  51.0 6.5 %collective-permute-done.14.refs_6_ = f32[4,128]{1,0:T(4,128)S(1)} collective-permute-done((f32[4,128]{1,0:T(4,128)S(1)}, f32[4,128]{1,0:T(4,128)S(1)}, u32[]{:S(2)}, u32[]{:S(2)}) %collective-permute-start.14) | collective-permute-done | bytes 2080 | tf_op jit(solution)/shard_map/ppermute | solution.py:334
  57.6 1.3 collective-permute-start.10
  58.9 1.3 collective-permute-start.9
  60.2 1.3 collective-permute-start.11
  61.5 1.7 %shard_map.159 = (f32[2624,128]{1,0:T(8,128)S(1)}, f32[64,128]{1,0:T(8,128)S(1)}) custom-call(f32[615]{0:T(1024)S(1)} %concatenate.46.tab_ref, f32[2624,128]{1,0:T(8,128)S(1)} %bitcast.67, f32[64,128]{1,0:T(8,128)S(1)} %get-tuple-element.26.level_ref.first_ref, s32[64,128]{1,0:T(8,128)S(1)} %bitcast.70), custom_call_target="tpu_custom_call" | custom-call | bytes 2787740 | tf_op jit(solution)/shard_map/pallas_call | solution.py:247
  63.2 20.5 %collective-permute-done.10.refs_4_ = f32[168,128]{1,0:T(8,128)S(1)} collective-permute-done((f32[168,128]{1,0:T(8,128)}, f32[168,128]{1,0:T(8,128)S(1)}, u32[]{:S(2)}, u32[]{:S(2)}) %collective-permute-start.10) | collective-permute-done | bytes 86048 | tf_op jit(solution)/shard_map/ppermute | solution.py:326
  83.7 1.7 %collective-permute-done.9.refs_3_ = f32[168,128]{1,0:T(8,128)S(1)} collective-permute-done((f32[168,128]{1,0:T(8,128)S(1)}, f32[168,128]{1,0:T(8,128)S(1)}, u32[]{:S(2)}, u32[]{:S(2)}) %collective-permute-start.9) | collective-permute-done | bytes 86048 | tf_op jit(solution)/shard_map/ppermute | solution.py:326
  85.4 1.4 %shard_map.161 = (f32[64,128]{1,0:T(8,128)S(1)}, f32[168,128]{1,0:T(8,128)S(1)}, f32[168,128]{1,0:T(8,128)S(1)}, f32[168,128]{1,0:T(8,128)S(1)}, f32[168,128]{1,...) custom-call(s32[81]{0:T(128)S(1)} %pad_add_fusion.plan_ref, f32[615]{0:T(1024)S(1)} %concatenate.46.tab_ref, ...), custom_call_target="tpu_custom_call" | custom-call | bytes 1137376 | tf_op jit(solution)/shard_map/pallas_call | solution.py:247
  86.9 1.9 %collective-permute-start.16 = (f32[1,16,128]{2,1,0:T(8,128)S(1)}, f32[1,16,128]{2,1,0:T(8,128)S(1)}, u32[]{:S(2)}, u32[]{:S(2)}) collective-permute-start(f32[1,16,128]{2,1,0:T(8,128)S(1)} %get-tuple-element.66), channel_id=1, source_target_pairs={{0,128},{128,256},{256,384},{1,129},{129,257},{257,385},{2,130},{1... | collective-permute-start | bytes 24584 | tf_op jit(solution)/shard_map/ppermute | solution.py:262
  88.8 2.4 %collective-permute-start.17 = (f32[1,16,128]{2,1,0:T(8,128)S(1)}, f32[1,16,128]{2,1,0:T(8,128)S(1)}, u32[]{:S(2)}, u32[]{:S(2)}) collective-permute-start(f32[1,16,128]{2,1,0:T(8,128)S(1)} %get-tuple-element.67), channel_id=1, source_target_pairs={{128,0},{256,128},{384,256},{129,1},{257,129},{385,257},{130,2},{2... | collective-permute-start | bytes 24584 | tf_op jit(solution)/shard_map/ppermute | solution.py:263
  91.2 2.5 %collective-permute-done.17 = f32[1,16,128]{2,1,0:T(8,128)S(1)} collective-permute-done((f32[1,16,128]{2,1,0:T(8,128)S(1)}, f32[1,16,128]{2,1,0:T(8,128)S(1)}, u32[]{:S(2)}, u32[]{:S(2)}) %collective-permute-start.17) | collective-permute-done | bytes 8224 | tf_op jit(solution)/shard_map/ppermute | solution.py:263
  93.8 2.1 %collective-permute-start.18 = (f32[6,1,128]{2,1,0:T(1,128)S(1)}, f32[6,1,128]{2,1,0:T(1,128)S(1)}, u32[]{:S(2)}, u32[]{:S(2)}) collective-permute-start(f32[6,1,128]{2,1,0:T(1,128)S(1)} %get-tuple-element.62), channel_id=1, source_target_pairs={{0,16},{16,32},{32,48},{48,64},{64,80},{80,96},{96,112},{1,17},{17... | collective-permute-start | bytes 9224 | tf_op jit(solution)/shard_map/ppermute | solution.py:262
  95.8 6.9 %collective-permute-start.19 = (f32[6,1,128]{2,1,0:T(1,128)S(1)}, f32[6,1,128]{2,1,0:T(1,128)S(1)}, u32[]{:S(2)}, u32[]{:S(2)}) collective-permute-start(f32[6,1,128]{2,1,0:T(1,128)S(1)} %get-tuple-element.63), channel_id=1, source_target_pairs={{16,0},{32,16},{48,32},{64,48},{80,64},{96,80},{112,96},{17,1},{33... | collective-permute-start | bytes 9224 | tf_op jit(solution)/shard_map/ppermute | solution.py:263
  102.7 1.3 collective-permute-start.22
  104.0 1.3 collective-permute-start.23
  105.4 0.2 slice_reduce_fusion
  105.6 3.6 %collective-permute-start.20 = (f32[6,18]{1,0:T(8,128)S(1)}, f32[6,18]{1,0:T(8,128)S(1)}, u32[]{:S(2)}, u32[]{:S(2)}) collective-permute-start(f32[6,18]{1,0:T(8,128)S(1)} %get-tuple-element.51), channel_id=1, source_target_pairs={{0,1},{1,2},{2,3},{3,4},{4,5},{5,6},{6,7},{7,8},{8,9},{9,10},{10,1... | collective-permute-start | bytes 1304 | tf_op jit(solution)/shard_map/ppermute | solution.py:262
  109.2 7.0 %collective-permute-start.21 = (f32[6,18]{1,0:T(8,128)S(1)}, f32[6,18]{1,0:T(8,128)S(1)}, u32[]{:S(2)}, u32[]{:S(2)}) collective-permute-start(f32[6,18]{1,0:T(8,128)S(1)} %get-tuple-element.50), channel_id=1, source_target_pairs={{1,0},{2,1},{3,2},{4,3},{5,4},{6,5},{7,6},{8,7},{9,8},{10,9},{11,1... | collective-permute-start | bytes 1304 | tf_op jit(solution)/shard_map/ppermute | solution.py:263
  116.2 0.1 copy.25.before_ref
  116.4 1.0 collective-permute-done.21
  117.3 0.1 copy.26.after_ref
  117.4 3.1 %shard_map.162 = (f32[64,128]{1,0:T(8,128)S(1)}, f32[64,128]{1,0:T(8,128)S(1)}, f32[2624,128]{1,0:T(8,128)S(1)}) custom-call(s32[81]{0:T(128)S(1)} %pad_add_fusion.plan_ref, f32[615]{0:T(1024)S(1)} %concatenate.46.tab_ref, f32[48]{0:T(128)S(1)} %pad_maximum_fusion.13.coef_ref, f32[6,18,128]{2,1,0:T(8,128)S(1)} %pad_maximum_fusion.9.planes_ref, ...), custom_call_target="tpu_custom_call" | custom-call | bytes 3393280 | tf_op jit(solution)/shard_map/pallas_call | solution.py:247
  120.5 6.7 %collective-permute-done.23.refs_1_ = f32[168,128]{1,0:T(8,128)S(1)} collective-permute-done((f32[168,128]{1,0:T(8,128)S(1)}, f32[168,128]{1,0:T(8,128)S(1)}, u32[]{:S(2)}, u32[]{:S(2)}) %collective-permute-start.23) | collective-permute-done | bytes 86048 | tf_op jit(solution)/shard_map/ppermute | solution.py:336
  127.2 2.2 %shard_map.163 = (f32[64,128]{1,0:T(8,128)}, f32[2624,128]{1,0:T(8,128)}) custom-call(s32[81]{0:T(128)S(1)} %pad_add_fusion.plan_ref, f32[615]{0:T(1024)S(1)} %concatenate.46.tab_ref, f32[64,128]{1,0:T(8,128)S(1)} %get-tuple-element.26.level_ref.first_ref, f32[64,128]{1,0:T(8,128)S(1)} %get-tuple-element.43.second_ref, ...), custom_call_target="tpu_custom_call" | custom-call | bytes 2992864 | tf_op jit(solution)/shard_map/pallas_call | solution.py:247
  (62 shorter events, 0.5 us)
Async XLA Ops:
  0.6 12.6 %copy-start.10 = (f32[3,41]{1,0:T(4,128)S(1)}, f32[3,41]{1,0:T(4,128)}, u32[]{:S(2)}) copy-start(f32[3,41]{1,0:T(4,128)} %param.26) | copy-start | bytes 1480
  1.4 12.8 %collective-permute-start.1 = (f32[1,16,128]{2,1,0:T(8,128)S(1)}, f32[1,16,128]{2,1,0:T(8,128)S(1)}, u32[]{:S(2)}, u32[]{:S(2)}) collective-permute-start(f32[1,16,128]{2,1,0:T(8,128)S(1)} %get-tuple-element.76), channel_id=1, source_target_pairs={{128,0},{256,128},{384,256},{129,1},{257,129},{385,257},{130,2},{2... | collective-permute-start | bytes 24584 | tf_op jit(solution)/shard_map/ppermute | solution.py:263
  3.9 10.2 %collective-permute-start = (f32[1,16,128]{2,1,0:T(8,128)S(1)}, f32[1,16,128]{2,1,0:T(8,128)S(1)}, u32[]{:S(2)}, u32[]{:S(2)}) collective-permute-start(f32[1,16,128]{2,1,0:T(8,128)S(1)} %get-tuple-element.77), channel_id=1, source_target_pairs={{0,128},{128,256},{256,384},{1,129},{129,257},{257,385},{2,130},{1... | collective-permute-start | bytes 24584 | tf_op jit(solution)/shard_map/ppermute | solution.py:262
  7.8 6.2 %copy-start.5 = (f32[3,8]{1,0:T(4,128)S(1)}, f32[3,8]{1,0:T(4,128)}, u32[]{:S(2)}) copy-start(f32[3,8]{1,0:T(4,128)} %param.23) | copy-start | bytes 292
  7.8 6.3 %copy-start.6 = (f32[3,8]{1,0:T(4,128)S(1)}, f32[3,8]{1,0:T(4,128)}, u32[]{:S(2)}) copy-start(f32[3,8]{1,0:T(4,128)} %param.24) | copy-start | bytes 292
  7.8 6.4 %copy-start.3 = (f32[4,16,128]{2,1,0:T(8,128)S(1)}, f32[4,16,128]{2,1,0:T(8,128)}, u32[]{:S(2)}) copy-start(f32[4,16,128]{2,1,0:T(8,128)} %param.15) | copy-start | bytes 98308
  7.8 15.4 %copy-start.4 = (s32[1,16,4]{1,2,0:T(4,128)S(1)}, s32[1,16,4]{1,2,0:T(4,128)}, u32[]{:S(2)}) copy-start(s32[1,16,4]{1,2,0:T(4,128)} %param.21) | copy-start | bytes 772
  9.0 21.7 %copy-start.12 = (s32[1,16]{1,0:T(1,128)S(1)}, s32[1,16]{1,0:T(1,128)}, u32[]{:S(2)}) copy-start(s32[1,16]{1,0:T(1,128)} %param.22) | copy-start | bytes 196
  9.1 22.7 %copy-start.2 = (s32[4,16,128]{2,1,0:T(8,128)S(1)}, s32[4,16,128]{2,1,0:T(8,128)}, u32[]{:S(2)}) copy-start(s32[4,16,128]{2,1,0:T(8,128)} %fibre_ref.3) | copy-start | bytes 98308
  9.1 51.0 %collective-permute-start.6 = (f32[168,128]{1,0:T(8,128)S(1)}, f32[168,128]{1,0:T(8,128)S(1)}, u32[]{:S(2)}, u32[]{:S(2)}) collective-permute-start(f32[168,128]{1,0:T(8,128)S(1)} %pad_maximum_fusion), channel_id=1, source_target_pairs={{8,7},{9,6},{10,5},{11,4},{12,3},{13,2},{14,1},{15,0},{24,23},{25,... | collective-permute-start | bytes 258056 | tf_op jit(solution)/shard_map/ppermute | solution.py:318
  10.5 36.5 %copy-start.7 = (f32[3,41]{1,0:T(4,128)S(1)}, f32[3,41]{1,0:T(4,128)}, u32[]{:S(2)}) copy-start(f32[3,41]{1,0:T(4,128)} %param.25) | copy-start | bytes 1480
  10.5 36.6 %copy-start.8 = (f32[3,41]{1,0:T(4,128)S(1)}, f32[3,41]{1,0:T(4,128)}, u32[]{:S(2)}) copy-start(f32[3,41]{1,0:T(4,128)} %param.28) | copy-start | bytes 1480
  10.5 36.6 %copy-start.9 = (f32[3,41]{1,0:T(4,128)S(1)}, f32[3,41]{1,0:T(4,128)}, u32[]{:S(2)}) copy-start(f32[3,41]{1,0:T(4,128)} %param.29) | copy-start | bytes 1480
  10.5 36.8 %copy-start.11 = (f32[3,41]{1,0:T(4,128)S(1)}, f32[3,41]{1,0:T(4,128)}, u32[]{:S(2)}) copy-start(f32[3,41]{1,0:T(4,128)} %param.27) | copy-start | bytes 1480
  10.5 52.7 %collective-permute-start.7 = (f32[168,128]{1,0:T(8,128)S(1)}, f32[168,128]{1,0:T(8,128)S(1)}, u32[]{:S(2)}, u32[]{:S(2)}) collective-permute-start(f32[168,128]{1,0:T(8,128)S(1)} %pad_maximum_fusion.1), channel_id=1, source_target_pairs={{8,6},{9,7},{10,4},{11,5},{12,2},{13,3},{14,0},{15,1},{24,22},{25,... | collective-permute-start | bytes 258056 | tf_op jit(solution)/shard_map/ppermute | solution.py:318
  11.9 51.3 %collective-permute-start.8 = (f32[168,128]{1,0:T(8,128)S(1)}, f32[168,128]{1,0:T(8,128)S(1)}, u32[]{:S(2)}, u32[]{:S(2)}) collective-permute-start(f32[168,128]{1,0:T(8,128)S(1)} %pad_maximum_fusion.2), channel_id=1, source_target_pairs={{8,3},{9,2},{10,1},{11,0},{12,7},{13,6},{14,5},{15,4},{24,19},{25,... | collective-permute-start | bytes 258056 | tf_op jit(solution)/shard_map/ppermute | solution.py:318
  13.2 48.2 %copy-start = (f32[4,16,41,128]{3,1,2,0:T(8,128)S(1)}, f32[4,16,41,128]{3,1,2,0:T(8,128)}, u32[]{:S(2)}) copy-start(f32[4,16,41,128]{3,1,2,0:T(8,128)} %param.16) | copy-start | bytes 4030468
  13.3 48.2 %copy-start.1 = (s32[4,16,128]{2,1,0:T(8,128)S(1)}, s32[4,16,128]{2,1,0:T(8,128)}, u32[]{:S(2)}) copy-start(s32[4,16,128]{2,1,0:T(8,128)} %param.17) | copy-start | bytes 98308
  14.2 9.2 %collective-permute-start.2 = (f32[6,1,128]{2,1,0:T(1,128)S(1)}, f32[6,1,128]{2,1,0:T(1,128)S(1)}, u32[]{:S(2)}, u32[]{:S(2)}) collective-permute-start(f32[6,1,128]{2,1,0:T(1,128)S(1)} %get-tuple-element.64), channel_id=1, source_target_pairs={{0,16},{16,32},{32,48},{48,64},{64,80},{80,96},{96,112},{1,17},{17... | collective-permute-start | bytes 9224 | tf_op jit(solution)/shard_map/ppermute | solution.py:262
  17.3 6.5 %collective-permute-start.3 = (f32[6,1,128]{2,1,0:T(1,128)S(1)}, f32[6,1,128]{2,1,0:T(1,128)S(1)}, u32[]{:S(2)}, u32[]{:S(2)}) collective-permute-start(f32[6,1,128]{2,1,0:T(1,128)S(1)} %get-tuple-element.65), channel_id=1, source_target_pairs={{16,0},{32,16},{48,32},{64,48},{80,64},{96,80},{112,96},{17,1},{33... | collective-permute-start | bytes 9224 | tf_op jit(solution)/shard_map/ppermute | solution.py:263
  24.0 7.6 %collective-permute-start.5 = (f32[6,18]{1,0:T(8,128)S(1)}, f32[6,18]{1,0:T(8,128)S(1)}, u32[]{:S(2)}, u32[]{:S(2)}) collective-permute-start(f32[6,18]{1,0:T(8,128)S(1)} %get-tuple-element.52), channel_id=1, source_target_pairs={{1,0},{2,1},{3,2},{4,3},{5,4},{6,5},{7,6},{8,7},{9,8},{10,9},{11,1... | collective-permute-start | bytes 1304 | tf_op jit(solution)/shard_map/ppermute | solution.py:263
  25.9 5.5 %collective-permute-start.4 = (f32[6,18]{1,0:T(8,128)S(1)}, f32[6,18]{1,0:T(8,128)S(1)}, u32[]{:S(2)}, u32[]{:S(2)}) collective-permute-start(f32[6,18]{1,0:T(8,128)S(1)} %get-tuple-element.53), channel_id=1, source_target_pairs={{0,1},{1,2},{2,3},{3,4},{4,5},{5,6},{6,7},{7,8},{8,9},{9,10},{10,1... | collective-permute-start | bytes 1304 | tf_op jit(solution)/shard_map/ppermute | solution.py:262
  32.4 15.1 %collective-permute-start.12 = (f32[4,128]{1,0:T(4,128)S(1)}, f32[4,128]{1,0:T(4,128)S(1)}, u32[]{:S(2)}, u32[]{:S(2)}) collective-permute-start(f32[4,128]{1,0:T(4,128)S(1)} %get-tuple-element.31), channel_id=1, source_target_pairs={{5,8},{4,9},{7,10},{6,11},{1,12},{0,13},{3,14},{2,15},{21,24},{20,... | collective-permute-start | bytes 6152 | tf_op jit(solution)/shard_map/ppermute | solution.py:324
  45.6 2.0 %collective-permute-start.13 = (f32[4,128]{1,0:T(4,128)S(1)}, f32[4,128]{1,0:T(4,128)S(1)}, u32[]{:S(2)}, u32[]{:S(2)}) collective-permute-start(f32[4,128]{1,0:T(4,128)S(1)} %get-tuple-element.32), channel_id=1, source_target_pairs={{4,8},{5,9},{6,10},{7,11},{0,12},{1,13},{2,14},{3,15},{20,24},{21,... | collective-permute-start | bytes 6152 | tf_op jit(solution)/shard_map/ppermute | solution.py:324
  48.4 9.1 %collective-permute-start.14 = (f32[4,128]{1,0:T(4,128)S(1)}, f32[4,128]{1,0:T(4,128)S(1)}, u32[]{:S(2)}, u32[]{:S(2)}) collective-permute-start(f32[4,128]{1,0:T(4,128)S(1)} %get-tuple-element.33), channel_id=1, source_target_pairs={{8,5},{9,4},{10,7},{11,6},{12,1},{13,0},{14,3},{15,2},{24,21},{25,... | collective-permute-start | bytes 6152 | tf_op jit(solution)/shard_map/ppermute | solution.py:334
  49.7 9.1 %collective-permute-start.15 = (f32[4,128]{1,0:T(4,128)S(1)}, f32[4,128]{1,0:T(4,128)S(1)}, u32[]{:S(2)}, u32[]{:S(2)}) collective-permute-start(f32[4,128]{1,0:T(4,128)S(1)} %get-tuple-element.34), channel_id=1, source_target_pairs={{8,4},{9,5},{10,6},{11,7},{12,0},{13,1},{14,2},{15,3},{24,20},{25,... | collective-permute-start | bytes 6152 | tf_op jit(solution)/shard_map/ppermute | solution.py:334
  57.6 26.1 %collective-permute-start.10 = (f32[168,128]{1,0:T(8,128)}, f32[168,128]{1,0:T(8,128)S(1)}, u32[]{:S(2)}, u32[]{:S(2)}) collective-permute-start(f32[168,128]{1,0:T(8,128)} %get-tuple-element.29), channel_id=1, source_target_pairs={{8,1},{9,0},{10,3},{11,2},{12,5},{13,4},{14,7},{15,6},{24,17},{25,... | collective-permute-start | bytes 258056 | tf_op jit(solution)/shard_map/ppermute | solution.py:326
  58.9 26.6 %collective-permute-start.9 = (f32[168,128]{1,0:T(8,128)S(1)}, f32[168,128]{1,0:T(8,128)S(1)}, u32[]{:S(2)}, u32[]{:S(2)}) collective-permute-start(f32[168,128]{1,0:T(8,128)S(1)} %get-tuple-element.28), channel_id=1, source_target_pairs={{8,2},{9,3},{10,0},{11,1},{12,6},{13,7},{14,4},{15,5},{24,18},{25,... | collective-permute-start | bytes 258056 | tf_op jit(solution)/shard_map/ppermute | solution.py:326
  60.2 25.3 %collective-permute-start.11 = (f32[168,128]{1,0:T(8,128)S(1)}, f32[168,128]{1,0:T(8,128)S(1)}, u32[]{:S(2)}, u32[]{:S(2)}) collective-permute-start(f32[168,128]{1,0:T(8,128)S(1)} %pad_maximum_fusion.5), channel_id=1, source_target_pairs={{8,0},{9,1},{10,2},{11,3},{12,4},{13,5},{14,6},{15,7},{24,16},{25,... | collective-permute-start | bytes 258056 | tf_op jit(solution)/shard_map/ppermute | solution.py:326
  86.9 4.3 %collective-permute-start.16 = (f32[1,16,128]{2,1,0:T(8,128)S(1)}, f32[1,16,128]{2,1,0:T(8,128)S(1)}, u32[]{:S(2)}, u32[]{:S(2)}) collective-permute-start(f32[1,16,128]{2,1,0:T(8,128)S(1)} %get-tuple-element.66), channel_id=1, source_target_pairs={{0,128},{128,256},{256,384},{1,129},{129,257},{257,385},{2,130},{1... | collective-permute-start | bytes 24584 | tf_op jit(solution)/shard_map/ppermute | solution.py:262
  88.8 5.0 %collective-permute-start.17 = (f32[1,16,128]{2,1,0:T(8,128)S(1)}, f32[1,16,128]{2,1,0:T(8,128)S(1)}, u32[]{:S(2)}, u32[]{:S(2)}) collective-permute-start(f32[1,16,128]{2,1,0:T(8,128)S(1)} %get-tuple-element.67), channel_id=1, source_target_pairs={{128,0},{256,128},{384,256},{129,1},{257,129},{385,257},{130,2},{2... | collective-permute-start | bytes 24584 | tf_op jit(solution)/shard_map/ppermute | solution.py:263
  93.8 11.6 %collective-permute-start.18 = (f32[6,1,128]{2,1,0:T(1,128)S(1)}, f32[6,1,128]{2,1,0:T(1,128)S(1)}, u32[]{:S(2)}, u32[]{:S(2)}) collective-permute-start(f32[6,1,128]{2,1,0:T(1,128)S(1)} %get-tuple-element.62), channel_id=1, source_target_pairs={{0,16},{16,32},{32,48},{48,64},{64,80},{80,96},{96,112},{1,17},{17... | collective-permute-start | bytes 9224 | tf_op jit(solution)/shard_map/ppermute | solution.py:262
  95.8 9.5 %collective-permute-start.19 = (f32[6,1,128]{2,1,0:T(1,128)S(1)}, f32[6,1,128]{2,1,0:T(1,128)S(1)}, u32[]{:S(2)}, u32[]{:S(2)}) collective-permute-start(f32[6,1,128]{2,1,0:T(1,128)S(1)} %get-tuple-element.63), channel_id=1, source_target_pairs={{16,0},{32,16},{48,32},{64,48},{80,64},{96,80},{112,96},{17,1},{33... | collective-permute-start | bytes 9224 | tf_op jit(solution)/shard_map/ppermute | solution.py:263
  102.7 17.8 %collective-permute-start.22 = (f32[168,128]{1,0:T(8,128)S(1)}, f32[168,128]{1,0:T(8,128)S(1)}, u32[]{:S(2)}, u32[]{:S(2)}) collective-permute-start(f32[168,128]{1,0:T(8,128)S(1)} %get-tuple-element.46.refs_0_), channel_id=1, source_target_pairs={{8,5},{9,4},{10,7},{11,6},{12,1},{13,0},{14,3},{15,2},{24,21},{25,... | collective-permute-start | bytes 258056 | tf_op jit(solution)/shard_map/ppermute | solution.py:336
  104.0 23.1 %collective-permute-start.23 = (f32[168,128]{1,0:T(8,128)S(1)}, f32[168,128]{1,0:T(8,128)S(1)}, u32[]{:S(2)}, u32[]{:S(2)}) collective-permute-start(f32[168,128]{1,0:T(8,128)S(1)} %get-tuple-element.47.refs_1_), channel_id=1, source_target_pairs={{8,4},{9,5},{10,6},{11,7},{12,0},{13,1},{14,2},{15,3},{24,20},{25,... | collective-permute-start | bytes 258056 | tf_op jit(solution)/shard_map/ppermute | solution.py:336
  105.6 10.7 %collective-permute-start.20 = (f32[6,18]{1,0:T(8,128)S(1)}, f32[6,18]{1,0:T(8,128)S(1)}, u32[]{:S(2)}, u32[]{:S(2)}) collective-permute-start(f32[6,18]{1,0:T(8,128)S(1)} %get-tuple-element.51), channel_id=1, source_target_pairs={{0,1},{1,2},{2,3},{3,4},{4,5},{5,6},{6,7},{7,8},{8,9},{9,10},{10,1... | collective-permute-start | bytes 1304 | tf_op jit(solution)/shard_map/ppermute | solution.py:262
  109.2 8.1 %collective-permute-start.21 = (f32[6,18]{1,0:T(8,128)S(1)}, f32[6,18]{1,0:T(8,128)S(1)}, u32[]{:S(2)}, u32[]{:S(2)}) collective-permute-start(f32[6,18]{1,0:T(8,128)S(1)} %get-tuple-element.50), channel_id=1, source_target_pairs={{1,0},{2,1},{3,2},{4,3},{5,4},{6,5},{7,6},{8,7},{9,8},{10,9},{11,1... | collective-permute-start | bytes 1304 | tf_op jit(solution)/shard_map/ppermute | solution.py:263

commit v2 on v1

--- a/solution.py
+++ b/solution.py
@@ -13,7 +13,7 @@
 ROWS = 168
 BLOCKS = 64
 
-EARLY = (7, 6, 3, 2, 1, 0)
+EARLY = (7, 3, 2, 1, 0, 6)
 LATE = (5, 4)
 
 VMEM = pl.BlockSpec(memory_space=pltpu.VMEM)
@@ -264,16 +264,29 @@
     )
 
 
-def halo(field):
-    before, after = shift((field[-1:], field[:1]), "depth")
+def beside_depth(field):
+    place, peers = lax.axis_index("depth"), lax.axis_size("depth")
+    layers = lax.all_gather(jnp.concatenate([field[:1], field[-1:]], axis=0), "depth")
+    lower = lax.dynamic_index_in_dim(layers, jnp.maximum(place - 1, 0), 0, keepdims=False)
+    upper = lax.dynamic_index_in_dim(layers, jnp.minimum(place + 1, peers - 1), 0, keepdims=False)
+    return jnp.where(place > 0, lower[1:], 0.0), jnp.where(place < peers - 1, upper[:1], 0.0)
+
+
+def halo(field, send=lambda phase, *after: ()):
+    field = tied(field, *send("depth", field))
+    before, after = beside_depth(field)
     field = jnp.concatenate([before, field, after], axis=0)
+    field = tied(field, *send("rows", field))
     before, after = shift((field[:, -1:], field[:, :1]), "rows")
     field = jnp.concatenate([before, field, after], axis=1)
+    field = tied(field, *send("cols", field))
     before, after = shift((field[:, :, 127], field[:, :, 0]), "cols")
     return field, before[..., None], after[..., None]
 
 
 def tied(value, *others):
+    if not others:
+        return value
     return lax.optimization_barrier((value, *others))[0]
 
 
@@ -305,45 +318,65 @@
     tags = cell_tags.reshape(line)
 
     held = loan_states[0].transpose(0, 2, 1, 3)
-    held_tags = loan_tags[0].astype(jnp.float32)
     message = {}
     for m in EARLY + LATE:
         source = jnp.bitwise_xor(own, m)
         body = lax.dynamic_index_in_dim(held, source, 0, keepdims=False).reshape(STATES * 4, 128)
-        kinds = lax.dynamic_index_in_dim(held_tags, source, 0, keepdims=False)
-        message[m] = jnp.concatenate([body, kinds], axis=0)
+        kinds = lax.dynamic_index_in_dim(loan_tags[0], source, 0, keepdims=False)
+        message[m] = jnp.concatenate([body, kinds.astype(jnp.float32)], axis=0)
 
     got = {}
-    for m in EARLY[:3]:
-        got[m] = lax.ppermute(message[m], "cols", to_heavy(m))
+
+    def send(m, *after):
+        got[m] = lax.ppermute(tied(message[m], *after), "cols", to_heavy(m))
+
+    e0, e1, e2, e3, e4, e5 = EARLY
+    send(e0)
+    send(e1)
+    send(e2)
+
+    def beside(phase, field):
+        if phase == "depth":
+            return message[e0], message[e1], message[e2]
+        if phase == "cols":
+            send(e3, field, got[e0])
+            return (got[e0],)
+        return ()
+
     diffused, *lines = call(
         diffuse_kernel,
         [f32(*line)] + [f32(4, 128) for _ in LATE],
-        [plan, coef, *halo(voltage), fibre_ids],
-    )
-    lines = [lax.ppermute(v, "cols", to_light(m)) for m, v in zip(LATE, lines)]
-    for m in EARLY[3:]:
-        got[m] = lax.ppermute(tied(message[m], diffused), "cols", to_heavy(m))
+        [plan, coef, *halo(voltage, beside), fibre_ids],
+    )
+    send(e4, diffused, got[e1])
+    send(e5, diffused, got[e2])
+    lines = [lax.ppermute(tied(v, got[e1], got[e2]), "cols", to_light(m)) for m, v in zip(LATE, lines)]
     first, current = call(home_kernel, [f32(*home.shape), f32(*line)], [table, home, diffused, tags])
     back = call(
         lender_kernel,
         [f32(4, 128) for _ in LATE],
-        [table, *(message[m] for m in LATE), *lines],
+        [table, *(message[m] for m in LATE), *(tied(v, current, got[e3]) for v in lines)],
         scratch=[(8, 128)],
     )
     back = [lax.ppermute(v, "cols", to_heavy(m)) for m, v in zip(LATE, back)]
-    for m in LATE:
-        got[m] = lax.ppermute(tied(message[m], got[EARLY[3]], *back), "cols", to_heavy(m))
     volt, *fresh = call(
         first_kernel,
         [f32(*line)] + [f32(ROWS, 128) for _ in EARLY],
         [plan, table, diffused, current, *(got[m] for m in EARLY), *back],
         scratch=[(8, 128), line],
     )
+
+    def beside_second(phase, field):
+        if phase == "depth":
+            send(LATE[0], field)
+        elif phase == "rows":
+            send(LATE[1], field)
+        return ()
+
     again, volt, out = call(
         second_kernel,
         [f32(*line), f32(*line), f32(*home.shape)],
-        [plan, table, coef, *halo(volt.reshape(4, 16, 128)), fibre_ids, first, tags, *fresh],
+        [plan, table, coef, *halo(volt.reshape(4, 16, 128), beside_second), fibre_ids, first, tags, *fresh],
         scratch=[(8, 128), line] + [(ROWS, 128) for _ in EARLY],
     )
     volt, out = call(

time: 130 us -> 113 us (0.87)
  the two profiles are of different devices: /device:TPU:113 before, /device:TPU:88 now
where the time goes in v2:
time: 113 us; the launch traced here: 112 us
  starting transfers between devices  62.9 us (56%)
  waiting for transfers between devices  21.9 us (19%)
  blocking collectives  10.6 us (9%)
  Pallas kernels  10.1 us (9%)
  local copies, waits for them, and re-layouts  3.27 us (3%)
  other arithmetic  2.41 us (2%)
  between operations  1.28 us (1%)
    ppermute x4, starting transfers between devices, shift(): lax.ppermute(value[1], axis, [(i + 1, i) for i in range(peers - 1)])  19.7 us
    ppermute x2, starting transfers between devices, local(): lax.ppermute(tied(v, got[e1], got[e2]), 'cols', to_light(m))  17.4 us
    ppermute x8, waiting for transfers between devices, send(): got[m] = lax.ppermute(tied(message[m], *after), 'cols', to_heavy(m))  15.3 us
    ppermute x4, starting transfers between devices, shift(): lax.ppermute(value[0], axis, [(i, i + 1) for i in range(peers - 1)])  12.9 us
    all_gather x2, blocking collectives, beside_depth(): lax.all_gather(jnp.concatenate([field[:1], field[-1:]], axis=0), 'depth')  10.6 us
    ppermute x8, starting transfers between devices, send(): got[m] = lax.ppermute(tied(message[m], *after), 'cols', to_heavy(m))  10.3 us
    pallas_call x6, Pallas kernels, call(): pl.pallas_call(body, out_shape=tuple(outs), in_specs=[SMEM if v.ndim == 1...  10.1 us
    ppermute x2, waiting for transfers between devices, local(): back = [lax.ppermute(v, 'cols', to_heavy(m)) for m, v in zip(LATE, back)]  3.54 us
  transfers between devices with their start and end apart: 20, of which 8 were waited for; matrix products, arithmetic and copies ran while one was open for 3% of the time, Pallas kernels for 6%

profile of v2, /device:TPU:88, one launch (start us, length us, event | category | flops | bytes accessed | tf_op | source)
XLA Modules:
  0.0 112.5 jit_solution(3281959961389967706)
XLA Ops:
  0.7 0.8 fusion.19
  1.5 0.0 copy-start.4
  1.5 1.2 %dynamic-slice_bitcast_fusion = (f32[1,41,4,128]{3,2,1,0:T(4,128)S(1)}, f32[1,41,4,128]{3,2,1,0:T(4,128)S(1)}, f32[1,41,4,128]{3,2,1,0:T(4,128)S(1)}, f32[1,41,4...) fusion(f32[1,16,4,41,128]{4,2,3,1,0:T(4,128)} %param.19, ...), kind=kLoop, calls=%fused_computation.8 | loop fusion | bytes 1343520 | tf_op jit(solution)/shard_map/jit(dynamic_index_in_dim)/dynamic_slice | solution.py:324
  2.8 0.0 copy-start.12
  2.9 1.3 %collective-permute-start.2 = (f32[168,128]{1,0:T(8,128)S(1)}, f32[168,128]{1,0:T(8,128)S(1)}, u32[]{:S(2)}, u32[]{:S(2)}) collective-permute-start(f32[168,128]{1,0:T(8,128)S(1)} %pad_maximum_fusion), channel_id=1, source_target_pairs={{8,7},{9,6},{10,5},{11,4},{12,3},{13,2},{14,1},{15,0},{24,23},{25,... | collective-permute-start | bytes 258056 | tf_op jit(solution)/shard_map/ppermute | solution.py:331
  4.2 0.0 copy-start.2
  4.2 1.3 %collective-permute-start.5 = (f32[168,128]{1,0:T(8,128)S(1)}, f32[168,128]{1,0:T(8,128)S(1)}, u32[]{:S(2)}, u32[]{:S(2)}) collective-permute-start(f32[168,128]{1,0:T(8,128)S(1)} %pad_maximum_fusion.1), channel_id=1, source_target_pairs={{8,3},{9,2},{10,1},{11,0},{12,7},{13,6},{14,5},{15,4},{24,19},{25,... | collective-permute-start | bytes 258056 | tf_op jit(solution)/shard_map/ppermute | solution.py:331
  5.6 1.3 %collective-permute-start.6 = (f32[168,128]{1,0:T(8,128)S(1)}, f32[168,128]{1,0:T(8,128)S(1)}, u32[]{:S(2)}, u32[]{:S(2)}) collective-permute-start(f32[168,128]{1,0:T(8,128)S(1)} %pad_maximum_fusion.2), channel_id=1, source_target_pairs={{8,2},{9,3},{10,0},{11,1},{12,6},{13,7},{14,4},{15,5},{24,18},{25,... | collective-permute-start | bytes 258056 | tf_op jit(solution)/shard_map/ppermute | solution.py:331
  6.9 0.0 copy-start.7
  7.0 0.0 copy-start.11
  7.0 5.4 %all-gather = f32[8,16,128]{2,1,0:T(8,128)S(1)} all-gather(f32[2,16,128]{2,1,0:T(8,128)S(1)} %pad_maximum_fusion.11), channel_id=2, replica_groups=mesh['depth'=4,'rows'=8,'cols'=16] {'depth'}, dimensions={0}, use_global_device_ids=true | all-gather | bytes 81920 | tf_op jit(solution)/shard_map/all_gather | solution.py:269
  12.4 3.4 %collective-permute-start = (f32[6,1,128]{2,1,0:T(1,128)S(1)}, f32[6,1,128]{2,1,0:T(1,128)S(1)}, u32[]{:S(2)}, u32[]{:S(2)}) collective-permute-start(f32[6,1,128]{2,1,0:T(1,128)S(1)} %get-tuple-element.80), channel_id=1, source_target_pairs={{0,16},{16,32},{32,48},{48,64},{64,80},{80,96},{96,112},{1,17},{17... | collective-permute-start | bytes 9224 | tf_op jit(solution)/shard_map/ppermute | solution.py:262
  15.8 6.1 %collective-permute-start.1 = (f32[6,1,128]{2,1,0:T(1,128)S(1)}, f32[6,1,128]{2,1,0:T(1,128)S(1)}, u32[]{:S(2)}, u32[]{:S(2)}) collective-permute-start(f32[6,1,128]{2,1,0:T(1,128)S(1)} %get-tuple-element.81), channel_id=1, source_target_pairs={{16,0},{32,16},{48,32},{64,48},{80,64},{96,80},{112,96},{17,1},{33... | collective-permute-start | bytes 9224 | tf_op jit(solution)/shard_map/ppermute | solution.py:263
  21.9 0.1 reshape.199
  22.0 0.1 reshape.200
  22.1 0.1 copy.27
  22.1 0.1 reshape.192
  22.4 0.1 pad_maximum_fusion.16.coef_ref
  22.4 0.6 pad_maximum_fusion.3
  23.1 0.7 pad_maximum_fusion.4
  23.8 0.1 pad_add_fusion.plan_ref
  23.9 0.2 slice_reduce_fusion.2
  24.1 3.8 %collective-permute-start.3 = (f32[6,18]{1,0:T(8,128)S(1)}, f32[6,18]{1,0:T(8,128)S(1)}, u32[]{:S(2)}, u32[]{:S(2)}) collective-permute-start(f32[6,18]{1,0:T(8,128)S(1)} %get-tuple-element.65), channel_id=1, source_target_pairs={{0,1},{1,2},{2,3},{3,4},{4,5},{5,6},{6,7},{7,8},{8,9},{9,10},{10,1... | collective-permute-start | bytes 1304 | tf_op jit(solution)/shard_map/ppermute | solution.py:262
  27.9 4.0 %collective-permute-start.4 = (f32[6,18]{1,0:T(8,128)S(1)}, f32[6,18]{1,0:T(8,128)S(1)}, u32[]{:S(2)}, u32[]{:S(2)}) collective-permute-start(f32[6,18]{1,0:T(8,128)S(1)} %get-tuple-element.64), channel_id=1, source_target_pairs={{1,0},{2,1},{3,2},{4,3},{5,4},{6,5},{7,6},{8,7},{9,8},{10,9},{11,1... | collective-permute-start | bytes 1304 | tf_op jit(solution)/shard_map/ppermute | solution.py:263
  32.0 1.3 %collective-permute-start.7 = (f32[168,128]{1,0:T(8,128)}, f32[168,128]{1,0:T(8,128)S(1)}, u32[]{:S(2)}, u32[]{:S(2)}) collective-permute-start(f32[168,128]{1,0:T(8,128)} %pad_maximum_fusion.3), channel_id=1, source_target_pairs={{8,1},{9,0},{10,3},{11,2},{12,5},{13,4},{14,7},{15,6},{24,17},{25,... | collective-permute-start | bytes 258056 | tf_op jit(solution)/shard_map/ppermute | solution.py:331
  33.3 0.1 copy.28.before_ref
  33.4 1.1 collective-permute-done.4
  34.5 0.1 copy.29.after_ref
  34.7 0.7 shard_map.158
  35.4 1.3 %collective-permute-start.8 = (f32[168,128]{1,0:T(8,128)}, f32[168,128]{1,0:T(8,128)S(1)}, u32[]{:S(2)}, u32[]{:S(2)}) collective-permute-start(f32[168,128]{1,0:T(8,128)} %get-tuple-element.37), channel_id=1, source_target_pairs={{8,0},{9,1},{10,2},{11,3},{12,4},{13,5},{14,6},{15,7},{24,16},{25,... | collective-permute-start | bytes 258056 | tf_op jit(solution)/shard_map/ppermute | solution.py:331
  36.7 1.9 %collective-permute-done.6.refs_2_ = f32[168,128]{1,0:T(8,128)S(1)} collective-permute-done((f32[168,128]{1,0:T(8,128)S(1)}, f32[168,128]{1,0:T(8,128)S(1)}, u32[]{:S(2)}, u32[]{:S(2)}) %collective-permute-start.6) | collective-permute-done | bytes 86048 | tf_op jit(solution)/shard_map/ppermute | solution.py:331
  38.6 16.1 %collective-permute-start.10 = (f32[4,128]{1,0:T(4,128)S(1)}, f32[4,128]{1,0:T(4,128)S(1)}, u32[]{:S(2)}, u32[]{:S(2)}) collective-permute-start(f32[4,128]{1,0:T(4,128)S(1)} %get-tuple-element.40), channel_id=1, source_target_pairs={{5,8},{4,9},{7,10},{6,11},{1,12},{0,13},{3,14},{2,15},{21,24},{20,... | collective-permute-start | bytes 6152 | tf_op jit(solution)/shard_map/ppermute | solution.py:353
  54.7 1.3 %collective-permute-start.11 = (f32[4,128]{1,0:T(4,128)S(1)}, f32[4,128]{1,0:T(4,128)S(1)}, u32[]{:S(2)}, u32[]{:S(2)}) collective-permute-start(f32[4,128]{1,0:T(4,128)S(1)} %get-tuple-element.43), channel_id=1, source_target_pairs={{4,8},{5,9},{6,10},{7,11},{0,12},{1,13},{2,14},{3,15},{20,24},{21,... | collective-permute-start | bytes 6152 | tf_op jit(solution)/shard_map/ppermute | solution.py:353
  56.0 1.3 %collective-permute-start.9 = (f32[168,128]{1,0:T(8,128)}, f32[168,128]{1,0:T(8,128)S(1)}, u32[]{:S(2)}, u32[]{:S(2)}) collective-permute-start(f32[168,128]{1,0:T(8,128)} %get-tuple-element.38), channel_id=1, source_target_pairs={{8,6},{9,7},{10,4},{11,5},{12,2},{13,3},{14,0},{15,1},{24,22},{25,... | collective-permute-start | bytes 258056 | tf_op jit(solution)/shard_map/ppermute | solution.py:331
  57.3 0.1 reshape.194
  57.4 0.1 reshape.197
  57.5 0.1 reshape.198
  57.6 0.1 reshape.195
  57.7 0.1 reshape.196
  57.8 0.1 concatenate.52.tab_ref
  57.8 1.7 %shard_map.159 = (f32[2624,128]{1,0:T(8,128)S(1)}, f32[64,128]{1,0:T(8,128)S(1)}) custom-call(f32[615]{0:T(1024)S(1)} %concatenate.52.tab_ref, f32[2624,128]{1,0:T(8,128)S(1)} %bitcast.77, f32[64,128]{1,0:T(8,128)S(1)} %get-tuple-element.34.level_ref.first_ref, s32[64,128]{1,0:T(8,128)S(1)} %bitcast.80), custom_call_target="tpu_custom_call" | custom-call | bytes 2787740 | tf_op jit(solution)/shard_map/pallas_call | solution.py:247
  59.6 0.8 shard_map.160
  60.4 1.3 %collective-permute-start.12 = (f32[4,128]{1,0:T(4,128)S(1)}, f32[4,128]{1,0:T(4,128)S(1)}, u32[]{:S(2)}, u32[]{:S(2)}) collective-permute-start(f32[4,128]{1,0:T(4,128)S(1)} %get-tuple-element.45), channel_id=1, source_target_pairs={{8,5},{9,4},{10,7},{11,6},{12,1},{13,0},{14,3},{15,2},{24,21},{25,... | collective-permute-start | bytes 6152 | tf_op jit(solution)/shard_map/ppermute | solution.py:361
  61.7 1.3 %collective-permute-start.13 = (f32[4,128]{1,0:T(4,128)S(1)}, f32[4,128]{1,0:T(4,128)S(1)}, u32[]{:S(2)}, u32[]{:S(2)}) collective-permute-start(f32[4,128]{1,0:T(4,128)S(1)} %get-tuple-element.46), channel_id=1, source_target_pairs={{8,4},{9,5},{10,6},{11,7},{12,0},{13,1},{14,2},{15,3},{24,20},{25,... | collective-permute-start | bytes 6152 | tf_op jit(solution)/shard_map/ppermute | solution.py:361
  63.0 5.4 %collective-permute-done.9.refs_5_ = f32[168,128]{1,0:T(8,128)S(1)} collective-permute-done((f32[168,128]{1,0:T(8,128)}, f32[168,128]{1,0:T(8,128)S(1)}, u32[]{:S(2)}, u32[]{:S(2)}) %collective-permute-start.9) | collective-permute-done | bytes 86048 | tf_op jit(solution)/shard_map/ppermute | solution.py:331
  68.4 0.6 collective-permute-done.12.refs_6_
  69.0 3.0 %collective-permute-done.13.refs_7_ = f32[4,128]{1,0:T(4,128)S(1)} collective-permute-done((f32[4,128]{1,0:T(4,128)S(1)}, f32[4,128]{1,0:T(4,128)S(1)}, u32[]{:S(2)}, u32[]{:S(2)}) %collective-permute-start.13) | collective-permute-done | bytes 2080 | tf_op jit(solution)/shard_map/ppermute | solution.py:361
  72.0 1.4 %shard_map.161 = (f32[64,128]{1,0:T(8,128)S(1)}, f32[168,128]{1,0:T(8,128)S(1)}, f32[168,128]{1,0:T(8,128)S(1)}, f32[168,128]{1,0:T(8,128)S(1)}, f32[168,128]{1,...) custom-call(s32[81]{0:T(128)S(1)} %pad_add_fusion.plan_ref, f32[615]{0:T(1024)S(1)} %concatenate.52.tab_ref, ...), custom_call_target="tpu_custom_call" | custom-call | bytes 1137376 | tf_op jit(solution)/shard_map/pallas_call | solution.py:247
  73.4 5.2 %all-gather.1 = f32[8,16,128]{2,1,0:T(8,128)S(1)} all-gather(f32[2,16,128]{2,1,0:T(8,128)S(1)} %pad_maximum_fusion.12), channel_id=3, replica_groups=mesh['depth'=4,'rows'=8,'cols'=16] {'depth'}, dimensions={0}, use_global_device_ids=true | all-gather | bytes 81920 | tf_op jit(solution)/shard_map/all_gather | solution.py:269
  78.7 3.2 %collective-permute-start.14 = (f32[6,1,128]{2,1,0:T(1,128)S(1)}, f32[6,1,128]{2,1,0:T(1,128)S(1)}, u32[]{:S(2)}, u32[]{:S(2)}) collective-permute-start(f32[6,1,128]{2,1,0:T(1,128)S(1)} %get-tuple-element.78), channel_id=1, source_target_pairs={{0,16},{16,32},{32,48},{48,64},{64,80},{80,96},{96,112},{1,17},{17... | collective-permute-start | bytes 9224 | tf_op jit(solution)/shard_map/ppermute | solution.py:262
  81.9 6.2 %collective-permute-start.15 = (f32[6,1,128]{2,1,0:T(1,128)S(1)}, f32[6,1,128]{2,1,0:T(1,128)S(1)}, u32[]{:S(2)}, u32[]{:S(2)}) collective-permute-start(f32[6,1,128]{2,1,0:T(1,128)S(1)} %get-tuple-element.79), channel_id=1, source_target_pairs={{16,0},{32,16},{48,32},{64,48},{80,64},{96,80},{112,96},{17,1},{33... | collective-permute-start | bytes 9224 | tf_op jit(solution)/shard_map/ppermute | solution.py:263
  88.2 1.3 %collective-permute-start.19 = (f32[168,128]{1,0:T(8,128)S(1)}, f32[168,128]{1,0:T(8,128)S(1)}, u32[]{:S(2)}, u32[]{:S(2)}) collective-permute-start(f32[168,128]{1,0:T(8,128)S(1)} %get-tuple-element.59.refs_1_), channel_id=1, source_target_pairs={{8,4},{9,5},{10,6},{11,7},{12,0},{13,1},{14,2},{15,3},{24,20},{25,... | collective-permute-start | bytes 258056 | tf_op jit(solution)/shard_map/ppermute | solution.py:331
  89.5 1.3 %collective-permute-start.18 = (f32[168,128]{1,0:T(8,128)S(1)}, f32[168,128]{1,0:T(8,128)S(1)}, u32[]{:S(2)}, u32[]{:S(2)}) collective-permute-start(f32[168,128]{1,0:T(8,128)S(1)} %get-tuple-element.58.refs_0_), channel_id=1, source_target_pairs={{8,5},{9,4},{10,7},{11,6},{12,1},{13,0},{14,3},{15,2},{24,21},{25,... | collective-permute-start | bytes 258056 | tf_op jit(solution)/shard_map/ppermute | solution.py:331
  90.8 0.2 slice_reduce_fusion
  91.0 2.5 %collective-permute-start.16 = (f32[6,18]{1,0:T(8,128)S(1)}, f32[6,18]{1,0:T(8,128)S(1)}, u32[]{:S(2)}, u32[]{:S(2)}) collective-permute-start(f32[6,18]{1,0:T(8,128)S(1)} %get-tuple-element.63), channel_id=1, source_target_pairs={{0,1},{1,2},{2,3},{3,4},{4,5},{5,6},{6,7},{7,8},{8,9},{9,10},{10,1... | collective-permute-start | bytes 1304 | tf_op jit(solution)/shard_map/ppermute | solution.py:262
  93.5 3.4 %collective-permute-start.17 = (f32[6,18]{1,0:T(8,128)S(1)}, f32[6,18]{1,0:T(8,128)S(1)}, u32[]{:S(2)}, u32[]{:S(2)}) collective-permute-start(f32[6,18]{1,0:T(8,128)S(1)} %get-tuple-element.62), channel_id=1, source_target_pairs={{1,0},{2,1},{3,2},{4,3},{5,4},{6,5},{7,6},{8,7},{9,8},{10,9},{11,1... | collective-permute-start | bytes 1304 | tf_op jit(solution)/shard_map/ppermute | solution.py:263
  96.9 0.0 collective-permute-done.16
  96.9 0.1 copy.30.before_ref
  97.0 2.0 %collective-permute-done.17 = f32[6,18]{1,0:T(8,128)S(1)} collective-permute-done((f32[6,18]{1,0:T(8,128)S(1)}, f32[6,18]{1,0:T(8,128)S(1)}, u32[]{:S(2)}, u32[]{:S(2)}) %collective-permute-start.17) | collective-permute-done | bytes 464 | tf_op jit(solution)/shard_map/ppermute | solution.py:263
  99.0 0.1 copy.31.after_ref
  99.1 3.1 %shard_map.162 = (f32[64,128]{1,0:T(8,128)S(1)}, f32[64,128]{1,0:T(8,128)S(1)}, f32[2624,128]{1,0:T(8,128)S(1)}) custom-call(s32[81]{0:T(128)S(1)} %pad_add_fusion.plan_ref, f32[615]{0:T(1024)S(1)} %concatenate.52.tab_ref, f32[48]{0:T(128)S(1)} %pad_maximum_fusion.16.coef_ref, f32[6,18,128]{2,1,0:T(8,128)S(1)} %pad_maximum_fusion.9.planes_ref, ...), custom_call_target="tpu_custom_call" | custom-call | bytes 3393280 | tf_op jit(solution)/shard_map/pallas_call | solution.py:247
  102.2 4.4 %collective-permute-done.19.refs_1_ = f32[168,128]{1,0:T(8,128)S(1)} collective-permute-done((f32[168,128]{1,0:T(8,128)S(1)}, f32[168,128]{1,0:T(8,128)S(1)}, u32[]{:S(2)}, u32[]{:S(2)}) %collective-permute-start.19) | collective-permute-done | bytes 86048 | tf_op jit(solution)/shard_map/ppermute | solution.py:331
  106.6 3.6 %collective-permute-done.18.refs_0_ = f32[168,128]{1,0:T(8,128)S(1)} collective-permute-done((f32[168,128]{1,0:T(8,128)S(1)}, f32[168,128]{1,0:T(8,128)S(1)}, u32[]{:S(2)}, u32[]{:S(2)}) %collective-permute-start.18) | collective-permute-done | bytes 86048 | tf_op jit(solution)/shard_map/ppermute | solution.py:331
  110.2 2.3 %shard_map.163 = (f32[64,128]{1,0:T(8,128)}, f32[2624,128]{1,0:T(8,128)}) custom-call(s32[81]{0:T(128)S(1)} %pad_add_fusion.plan_ref, f32[615]{0:T(1024)S(1)} %concatenate.52.tab_ref, f32[64,128]{1,0:T(8,128)S(1)} %get-tuple-element.34.level_ref.first_ref, f32[64,128]{1,0:T(8,128)S(1)} %get-tuple-element.55.second_ref, ...), custom_call_target="tpu_custom_call" | custom-call | bytes 2992864 | tf_op jit(solution)/shard_map/pallas_call | solution.py:247
  (57 shorter events, 0.5 us)
Async XLA Ops:
  0.6 6.3 %copy-start.3 = (f32[4,16,128]{2,1,0:T(8,128)S(1)}, f32[4,16,128]{2,1,0:T(8,128)}, u32[]{:S(2)}) copy-start(f32[4,16,128]{2,1,0:T(8,128)} %param.15) | copy-start | bytes 98308
  1.5 20.4 %copy-start.5 = (f32[3,8]{1,0:T(4,128)S(1)}, f32[3,8]{1,0:T(4,128)}, u32[]{:S(2)}) copy-start(f32[3,8]{1,0:T(4,128)} %param.23) | copy-start | bytes 292
  1.5 20.5 %copy-start.6 = (f32[3,8]{1,0:T(4,128)S(1)}, f32[3,8]{1,0:T(4,128)}, u32[]{:S(2)}) copy-start(f32[3,8]{1,0:T(4,128)} %param.24) | copy-start | bytes 292
  1.5 20.5 %copy-start.10 = (f32[3,41]{1,0:T(4,128)S(1)}, f32[3,41]{1,0:T(4,128)}, u32[]{:S(2)}) copy-start(f32[3,41]{1,0:T(4,128)} %param.26) | copy-start | bytes 1480
  1.5 20.5 %copy-start.4 = (s32[1,16,4]{1,2,0:T(4,128)S(1)}, s32[1,16,4]{1,2,0:T(4,128)}, u32[]{:S(2)}) copy-start(s32[1,16,4]{1,2,0:T(4,128)} %param.21) | copy-start | bytes 772
  2.8 21.0 %copy-start.12 = (s32[1,16]{1,0:T(1,128)S(1)}, s32[1,16]{1,0:T(1,128)}, u32[]{:S(2)}) copy-start(s32[1,16]{1,0:T(1,128)} %param.22) | copy-start | bytes 196
  2.9 21.0 %collective-permute-start.2 = (f32[168,128]{1,0:T(8,128)S(1)}, f32[168,128]{1,0:T(8,128)S(1)}, u32[]{:S(2)}, u32[]{:S(2)}) collective-permute-start(f32[168,128]{1,0:T(8,128)S(1)} %pad_maximum_fusion), channel_id=1, source_target_pairs={{8,7},{9,6},{10,5},{11,4},{12,3},{13,2},{14,1},{15,0},{24,23},{25,... | collective-permute-start | bytes 258056 | tf_op jit(solution)/shard_map/ppermute | solution.py:331
  4.2 30.5 %copy-start.2 = (s32[4,16,128]{2,1,0:T(8,128)S(1)}, s32[4,16,128]{2,1,0:T(8,128)}, u32[]{:S(2)}) copy-start(s32[4,16,128]{2,1,0:T(8,128)} %fibre_ref.3) | copy-start | bytes 98308
  4.2 31.2 %collective-permute-start.5 = (f32[168,128]{1,0:T(8,128)S(1)}, f32[168,128]{1,0:T(8,128)S(1)}, u32[]{:S(2)}, u32[]{:S(2)}) collective-permute-start(f32[168,128]{1,0:T(8,128)S(1)} %pad_maximum_fusion.1), channel_id=1, source_target_pairs={{8,3},{9,2},{10,1},{11,0},{12,7},{13,6},{14,5},{15,4},{24,19},{25,... | collective-permute-start | bytes 258056 | tf_op jit(solution)/shard_map/ppermute | solution.py:331
  5.6 33.0 %collective-permute-start.6 = (f32[168,128]{1,0:T(8,128)S(1)}, f32[168,128]{1,0:T(8,128)S(1)}, u32[]{:S(2)}, u32[]{:S(2)}) collective-permute-start(f32[168,128]{1,0:T(8,128)S(1)} %pad_maximum_fusion.2), channel_id=1, source_target_pairs={{8,2},{9,3},{10,0},{11,1},{12,6},{13,7},{14,4},{15,5},{24,18},{25,... | collective-permute-start | bytes 258056 | tf_op jit(solution)/shard_map/ppermute | solution.py:331
  6.9 50.4 %copy-start.7 = (f32[3,41]{1,0:T(4,128)S(1)}, f32[3,41]{1,0:T(4,128)}, u32[]{:S(2)}) copy-start(f32[3,41]{1,0:T(4,128)} %param.25) | copy-start | bytes 1480
  6.9 50.5 %copy-start.8 = (f32[3,41]{1,0:T(4,128)S(1)}, f32[3,41]{1,0:T(4,128)}, u32[]{:S(2)}) copy-start(f32[3,41]{1,0:T(4,128)} %param.28) | copy-start | bytes 1480
  7.0 50.5 %copy-start.9 = (f32[3,41]{1,0:T(4,128)S(1)}, f32[3,41]{1,0:T(4,128)}, u32[]{:S(2)}) copy-start(f32[3,41]{1,0:T(4,128)} %param.29) | copy-start | bytes 1480
  7.0 50.7 %copy-start.11 = (f32[3,41]{1,0:T(4,128)S(1)}, f32[3,41]{1,0:T(4,128)}, u32[]{:S(2)}) copy-start(f32[3,41]{1,0:T(4,128)} %param.27) | copy-start | bytes 1480
  7.0 50.9 %copy-start = (f32[4,16,41,128]{3,1,2,0:T(8,128)S(1)}, f32[4,16,41,128]{3,1,2,0:T(8,128)}, u32[]{:S(2)}) copy-start(f32[4,16,41,128]{3,1,2,0:T(8,128)} %param.16) | copy-start | bytes 4030468
  7.0 50.8 %copy-start.1 = (s32[4,16,128]{2,1,0:T(8,128)S(1)}, s32[4,16,128]{2,1,0:T(8,128)}, u32[]{:S(2)}) copy-start(s32[4,16,128]{2,1,0:T(8,128)} %param.17) | copy-start | bytes 98308
  12.4 11.5 %collective-permute-start = (f32[6,1,128]{2,1,0:T(1,128)S(1)}, f32[6,1,128]{2,1,0:T(1,128)S(1)}, u32[]{:S(2)}, u32[]{:S(2)}) collective-permute-start(f32[6,1,128]{2,1,0:T(1,128)S(1)} %get-tuple-element.80), channel_id=1, source_target_pairs={{0,16},{16,32},{32,48},{48,64},{64,80},{80,96},{96,112},{1,17},{17... | collective-permute-start | bytes 9224 | tf_op jit(solution)/shard_map/ppermute | solution.py:262
  15.8 8.1 %collective-permute-start.1 = (f32[6,1,128]{2,1,0:T(1,128)S(1)}, f32[6,1,128]{2,1,0:T(1,128)S(1)}, u32[]{:S(2)}, u32[]{:S(2)}) collective-permute-start(f32[6,1,128]{2,1,0:T(1,128)S(1)} %get-tuple-element.81), channel_id=1, source_target_pairs={{16,0},{32,16},{48,32},{64,48},{80,64},{96,80},{112,96},{17,1},{33... | collective-permute-start | bytes 9224 | tf_op jit(solution)/shard_map/ppermute | solution.py:263
  24.1 9.2 %collective-permute-start.3 = (f32[6,18]{1,0:T(8,128)S(1)}, f32[6,18]{1,0:T(8,128)S(1)}, u32[]{:S(2)}, u32[]{:S(2)}) collective-permute-start(f32[6,18]{1,0:T(8,128)S(1)} %get-tuple-element.65), channel_id=1, source_target_pairs={{0,1},{1,2},{2,3},{3,4},{4,5},{5,6},{6,7},{7,8},{8,9},{9,10},{10,1... | collective-permute-start | bytes 1304 | tf_op jit(solution)/shard_map/ppermute | solution.py:262
  27.9 6.6 %collective-permute-start.4 = (f32[6,18]{1,0:T(8,128)S(1)}, f32[6,18]{1,0:T(8,128)S(1)}, u32[]{:S(2)}, u32[]{:S(2)}) collective-permute-start(f32[6,18]{1,0:T(8,128)S(1)} %get-tuple-element.64), channel_id=1, source_target_pairs={{1,0},{2,1},{3,2},{4,3},{5,4},{6,5},{7,6},{8,7},{9,8},{10,9},{11,1... | collective-permute-start | bytes 1304 | tf_op jit(solution)/shard_map/ppermute | solution.py:263
  32.0 27.6 %collective-permute-start.7 = (f32[168,128]{1,0:T(8,128)}, f32[168,128]{1,0:T(8,128)S(1)}, u32[]{:S(2)}, u32[]{:S(2)}) collective-permute-start(f32[168,128]{1,0:T(8,128)} %pad_maximum_fusion.3), channel_id=1, source_target_pairs={{8,1},{9,0},{10,3},{11,2},{12,5},{13,4},{14,7},{15,6},{24,17},{25,... | collective-permute-start | bytes 258056 | tf_op jit(solution)/shard_map/ppermute | solution.py:331
  35.4 27.6 %collective-permute-start.8 = (f32[168,128]{1,0:T(8,128)}, f32[168,128]{1,0:T(8,128)S(1)}, u32[]{:S(2)}, u32[]{:S(2)}) collective-permute-start(f32[168,128]{1,0:T(8,128)} %get-tuple-element.37), channel_id=1, source_target_pairs={{8,0},{9,1},{10,2},{11,3},{12,4},{13,5},{14,6},{15,7},{24,16},{25,... | collective-permute-start | bytes 258056 | tf_op jit(solution)/shard_map/ppermute | solution.py:331
  38.6 21.0 %collective-permute-start.10 = (f32[4,128]{1,0:T(4,128)S(1)}, f32[4,128]{1,0:T(4,128)S(1)}, u32[]{:S(2)}, u32[]{:S(2)}) collective-permute-start(f32[4,128]{1,0:T(4,128)S(1)} %get-tuple-element.40), channel_id=1, source_target_pairs={{5,8},{4,9},{7,10},{6,11},{1,12},{0,13},{3,14},{2,15},{21,24},{20,... | collective-permute-start | bytes 6152 | tf_op jit(solution)/shard_map/ppermute | solution.py:353
  54.7 4.9 %collective-permute-start.11 = (f32[4,128]{1,0:T(4,128)S(1)}, f32[4,128]{1,0:T(4,128)S(1)}, u32[]{:S(2)}, u32[]{:S(2)}) collective-permute-start(f32[4,128]{1,0:T(4,128)S(1)} %get-tuple-element.43), channel_id=1, source_target_pairs={{4,8},{5,9},{6,10},{7,11},{0,12},{1,13},{2,14},{3,15},{20,24},{21,... | collective-permute-start | bytes 6152 | tf_op jit(solution)/shard_map/ppermute | solution.py:353
  56.0 12.4 %collective-permute-start.9 = (f32[168,128]{1,0:T(8,128)}, f32[168,128]{1,0:T(8,128)S(1)}, u32[]{:S(2)}, u32[]{:S(2)}) collective-permute-start(f32[168,128]{1,0:T(8,128)} %get-tuple-element.38), channel_id=1, source_target_pairs={{8,6},{9,7},{10,4},{11,5},{12,2},{13,3},{14,0},{15,1},{24,22},{25,... | collective-permute-start | bytes 258056 | tf_op jit(solution)/shard_map/ppermute | solution.py:331
  60.4 8.6 %collective-permute-start.12 = (f32[4,128]{1,0:T(4,128)S(1)}, f32[4,128]{1,0:T(4,128)S(1)}, u32[]{:S(2)}, u32[]{:S(2)}) collective-permute-start(f32[4,128]{1,0:T(4,128)S(1)} %get-tuple-element.45), channel_id=1, source_target_pairs={{8,5},{9,4},{10,7},{11,6},{12,1},{13,0},{14,3},{15,2},{24,21},{25,... | collective-permute-start | bytes 6152 | tf_op jit(solution)/shard_map/ppermute | solution.py:361
  61.7 10.3 %collective-permute-start.13 = (f32[4,128]{1,0:T(4,128)S(1)}, f32[4,128]{1,0:T(4,128)S(1)}, u32[]{:S(2)}, u32[]{:S(2)}) collective-permute-start(f32[4,128]{1,0:T(4,128)S(1)} %get-tuple-element.46), channel_id=1, source_target_pairs={{8,4},{9,5},{10,6},{11,7},{12,0},{13,1},{14,2},{15,3},{24,20},{25,... | collective-permute-start | bytes 6152 | tf_op jit(solution)/shard_map/ppermute | solution.py:361
  78.7 12.1 %collective-permute-start.14 = (f32[6,1,128]{2,1,0:T(1,128)S(1)}, f32[6,1,128]{2,1,0:T(1,128)S(1)}, u32[]{:S(2)}, u32[]{:S(2)}) collective-permute-start(f32[6,1,128]{2,1,0:T(1,128)S(1)} %get-tuple-element.78), channel_id=1, source_target_pairs={{0,16},{16,32},{32,48},{48,64},{64,80},{80,96},{96,112},{1,17},{17... | collective-permute-start | bytes 9224 | tf_op jit(solution)/shard_map/ppermute | solution.py:262
  81.9 8.8 %collective-permute-start.15 = (f32[6,1,128]{2,1,0:T(1,128)S(1)}, f32[6,1,128]{2,1,0:T(1,128)S(1)}, u32[]{:S(2)}, u32[]{:S(2)}) collective-permute-start(f32[6,1,128]{2,1,0:T(1,128)S(1)} %get-tuple-element.79), channel_id=1, source_target_pairs={{16,0},{32,16},{48,32},{64,48},{80,64},{96,80},{112,96},{17,1},{33... | collective-permute-start | bytes 9224 | tf_op jit(solution)/shard_map/ppermute | solution.py:263
  88.2 18.4 %collective-permute-start.19 = (f32[168,128]{1,0:T(8,128)S(1)}, f32[168,128]{1,0:T(8,128)S(1)}, u32[]{:S(2)}, u32[]{:S(2)}) collective-permute-start(f32[168,128]{1,0:T(8,128)S(1)} %get-tuple-element.59.refs_1_), channel_id=1, source_target_pairs={{8,4},{9,5},{10,6},{11,7},{12,0},{13,1},{14,2},{15,3},{24,20},{25,... | collective-permute-start | bytes 258056 | tf_op jit(solution)/shard_map/ppermute | solution.py:331
  89.5 20.7 %collective-permute-start.18 = (f32[168,128]{1,0:T(8,128)S(1)}, f32[168,128]{1,0:T(8,128)S(1)}, u32[]{:S(2)}, u32[]{:S(2)}) collective-permute-start(f32[168,128]{1,0:T(8,128)S(1)} %get-tuple-element.58.refs_0_), channel_id=1, source_target_pairs={{8,5},{9,4},{10,7},{11,6},{12,1},{13,0},{14,3},{15,2},{24,21},{25,... | collective-permute-start | bytes 258056 | tf_op jit(solution)/shard_map/ppermute | solution.py:331
  91.0 5.9 %collective-permute-start.16 = (f32[6,18]{1,0:T(8,128)S(1)}, f32[6,18]{1,0:T(8,128)S(1)}, u32[]{:S(2)}, u32[]{:S(2)}) collective-permute-start(f32[6,18]{1,0:T(8,128)S(1)} %get-tuple-element.63), channel_id=1, source_target_pairs={{0,1},{1,2},{2,3},{3,4},{4,5},{5,6},{6,7},{7,8},{8,9},{9,10},{10,1... | collective-permute-start | bytes 1304 | tf_op jit(solution)/shard_map/ppermute | solution.py:262
  93.5 5.5 %collective-permute-start.17 = (f32[6,18]{1,0:T(8,128)S(1)}, f32[6,18]{1,0:T(8,128)S(1)}, u32[]{:S(2)}, u32[]{:S(2)}) collective-permute-start(f32[6,18]{1,0:T(8,128)S(1)} %get-tuple-element.62), channel_id=1, source_target_pairs={{1,0},{2,1},{3,2},{4,3},{5,4},{6,5},{7,6},{8,7},{9,8},{10,9},{11,1... | collective-permute-start | bytes 1304 | tf_op jit(solution)/shard_map/ppermute | solution.py:263

commit v3 on v2

--- a/solution.py
+++ b/solution.py
@@ -14,6 +14,7 @@
 BLOCKS = 64
 
 EARLY = (7, 3, 2, 1, 0, 6)
+SOON = 4
 LATE = (5, 4)
 
 VMEM = pl.BlockSpec(memory_space=pltpu.VMEM)
@@ -196,15 +197,25 @@
         ref[...] = current[0:4, :]
 
 
+def early_kernel(plan_ref, tab_ref, level_ref, current_ref, *refs):
+    messages, out_ref, fresh, hold_ref = refs[:SOON], refs[SOON], refs[SOON + 1 : 2 * SOON + 1], refs[-1]
+    out_ref[...] = current_ref[...]
+    levels = [gather_lines(plan_ref, m, level_ref, hold_ref) for m in EARLY[:SOON]]
+    currents = react_lent(tab_ref, messages, levels, fresh)
+    for m, value in zip(EARLY[:SOON], currents):
+        put_lines(plan_ref, m, hold_ref, value, out_ref)
+
+
 def first_kernel(plan_ref, tab_ref, level_ref, current_ref, *refs):
-    n, l = len(EARLY), len(LATE)
+    rest = EARLY[SOON:]
+    n, l = len(rest), len(LATE)
     messages, lent = refs[:n], refs[n : n + l]
     out_ref, fresh = refs[n + l], refs[n + l + 1 : 2 * n + l + 1]
     hold_ref, sum_ref = refs[2 * n + l + 1 :]
     sum_ref[...] = current_ref[...]
-    levels = [gather_lines(plan_ref, m, level_ref, hold_ref) for m in EARLY]
+    levels = [gather_lines(plan_ref, m, level_ref, hold_ref) for m in rest]
     currents = react_lent(tab_ref, messages, levels, fresh)
-    for m, value in zip(EARLY, currents):
+    for m, value in zip(rest, currents):
         put_lines(plan_ref, m, hold_ref, value, sum_ref)
     for m, ref in zip(LATE, lent):
         hold_ref[0:4, :] = ref[...]
@@ -212,34 +223,21 @@
     out_ref[...] = level_ref[...] - 0.25 * sum_ref[...]
 
 
-def second_kernel(plan_ref, tab_ref, coef_ref, planes_ref, before_ref, after_ref, fibre_ref, states_ref, tags_ref, *refs):
-    n = len(EARLY)
-    messages = refs[:n]
-    level_ref, volt_ref, out_ref = refs[n : n + 3]
-    hold_ref, sum_ref = refs[n + 3 : n + 5]
-    fresh = refs[n + 5 :]
+def second_kernel(plan_ref, tab_ref, coef_ref, planes_ref, before_ref, after_ref, fibre_ref, first_ref, states_ref, tags_ref, *refs):
+    n, l = len(EARLY), len(LATE)
+    early, late = refs[:n], refs[n : n + l]
+    volt_ref, out_ref, hold_ref, level_ref, sum_ref = refs[n + l : n + l + 5]
+    fresh = refs[n + l + 5 :]
+    levels = [gather_lines(plan_ref, m, first_ref, hold_ref) for m in LATE]
+    react_lent(tab_ref, late, levels, fresh[n:])
     stencil(coef_ref, planes_ref, before_ref, after_ref, fibre_ref, level_ref)
     sum_ref[...] = react_home(tab_ref, states_ref, level_ref[...], tags_ref[...], out_ref)
-    levels = [gather_lines(plan_ref, m, level_ref, hold_ref) for m in EARLY]
-    currents = react_lent(tab_ref, messages, levels, fresh)
-    for m, value, ref in zip(EARLY, currents, fresh):
+    levels = [gather_lines(plan_ref, m, level_ref, hold_ref) for m in EARLY + LATE]
+    currents = react_lent(tab_ref, (*early, *fresh[n:]), levels, fresh)
+    for m, value, ref in zip(EARLY + LATE, currents, fresh):
         put_lines(plan_ref, m, hold_ref, value, sum_ref)
         put_states(plan_ref, m, ref, out_ref)
     volt_ref[...] = level_ref[...] - 0.25 * sum_ref[...]
-
-
-def last_kernel(plan_ref, tab_ref, first_ref, second_ref, volt_in, states_in, *refs):
-    l = len(LATE)
-    messages, (volt_ref, out_ref, hold_ref), fresh = refs[:l], refs[l : l + 3], refs[l + 3 :]
-    volt_ref[...] = volt_in[...]
-    out_ref[...] = states_in[...]
-    levels = [gather_lines(plan_ref, m, first_ref, hold_ref) for m in LATE]
-    react_lent(tab_ref, messages, levels, fresh)
-    levels = [gather_lines(plan_ref, m, second_ref, hold_ref) for m in LATE]
-    currents = react_lent(tab_ref, fresh, levels, fresh)
-    for m, level, value, ref in zip(LATE, levels, currents, fresh):
-        put_lines(plan_ref, m, hold_ref, level - 0.25 * value, volt_ref)
-        put_states(plan_ref, m, ref, out_ref)
 
 
 def call(body, outs, ins, scratch=(), flops=0, **kwargs):
@@ -270,6 +268,28 @@
     lower = lax.dynamic_index_in_dim(layers, jnp.maximum(place - 1, 0), 0, keepdims=False)
     upper = lax.dynamic_index_in_dim(layers, jnp.minimum(place + 1, peers - 1), 0, keepdims=False)
     return jnp.where(place > 0, lower[1:], 0.0), jnp.where(place < peers - 1, upper[:1], 0.0)
+
+
+def halo_depth_last(field, send):
+    send("rows", field)
+    before, after = shift((field[:, -1:], field[:, :1]), "rows")
+    field = jnp.concatenate([before, field, after], axis=1)
+    before, after = shift((field[:, :, 127], field[:, :, 0]), "cols")
+    count = field.shape[1]
+
+    def face(x):
+        columns = jnp.pad(jnp.stack([before[x], after[x]]), ((0, 4), (0, 128 - count)))
+        return jnp.concatenate([field[x], columns], axis=0)
+
+    place, peers = lax.axis_index("depth"), lax.axis_size("depth")
+    layers = lax.all_gather(jnp.stack([face(0), face(-1)]), "depth")
+    lower = lax.dynamic_index_in_dim(layers, jnp.maximum(place - 1, 0), 0, keepdims=False)[1:]
+    upper = lax.dynamic_index_in_dim(layers, jnp.minimum(place + 1, peers - 1), 0, keepdims=False)[:1]
+    lower, upper = jnp.where(place > 0, lower, 0.0), jnp.where(place < peers - 1, upper, 0.0)
+    field = jnp.concatenate([lower[:, :count], field, upper[:, :count]], axis=0)
+    before = jnp.concatenate([lower[:, count, :count], before, upper[:, count, :count]], axis=0)
+    after = jnp.concatenate([lower[:, count + 1, :count], after, upper[:, count + 1, :count]], axis=0)
+    return field, before[..., None], after[..., None]
 
 
 def halo(field, send=lambda phase, *after: ()):
@@ -351,39 +371,41 @@
     send(e4, diffused, got[e1])
     send(e5, diffused, got[e2])
     lines = [lax.ppermute(tied(v, got[e1], got[e2]), "cols", to_light(m)) for m, v in zip(LATE, lines)]
-    first, current = call(home_kernel, [f32(*home.shape), f32(*line)], [table, home, diffused, tags])
     back = call(
         lender_kernel,
         [f32(4, 128) for _ in LATE],
-        [table, *(message[m] for m in LATE), *(tied(v, current, got[e3]) for v in lines)],
+        [table, *(message[m] for m in LATE), *lines],
         scratch=[(8, 128)],
     )
+    first, current = call(
+        home_kernel, [f32(*home.shape), f32(*line)], [table, home, tied(diffused, *back), tags]
+    )
     back = [lax.ppermute(v, "cols", to_heavy(m)) for m, v in zip(LATE, back)]
-    volt, *fresh = call(
+    current, *fresh = call(
+        early_kernel,
+        [f32(*line)] + [f32(ROWS, 128) for _ in EARLY[:SOON]],
+        [plan, table, diffused, current, *(got[m] for m in EARLY[:SOON])],
+        scratch=[(8, 128)],
+    )
+    volt, *others = call(
         first_kernel,
-        [f32(*line)] + [f32(ROWS, 128) for _ in EARLY],
-        [plan, table, diffused, current, *(got[m] for m in EARLY), *back],
+        [f32(*line)] + [f32(ROWS, 128) for _ in EARLY[SOON:]],
+        [plan, table, diffused, current, *(got[m] for m in EARLY[SOON:]), *back],
         scratch=[(8, 128), line],
     )
+    fresh += others
 
     def beside_second(phase, field):
-        if phase == "depth":
-            send(LATE[0], field)
-        elif phase == "rows":
-            send(LATE[1], field)
-        return ()
-
-    again, volt, out = call(
+        for m in LATE:
+            send(m, field)
+
+    planes = halo_depth_last(volt.reshape(4, 16, 128), beside_second)
+    late = [got[m] for m in LATE]
+    volt, out = call(
         second_kernel,
-        [f32(*line), f32(*line), f32(*home.shape)],
-        [plan, table, coef, *halo(volt.reshape(4, 16, 128), beside_second), fibre_ids, first, tags, *fresh],
-        scratch=[(8, 128), line] + [(ROWS, 128) for _ in EARLY],
-    )
-    volt, out = call(
-        last_kernel,
         [f32(*line), f32(*home.shape)],
-        [plan, table, diffused, again, volt, out, *(got[m] for m in LATE)],
-        scratch=[(8, 128)] + [(ROWS, 128) for _ in LATE],
+        [plan, table, coef, *planes, fibre_ids, diffused, first, tags, *fresh, *late],
+        scratch=[(8, 128), line, line] + [(ROWS, 128) for _ in EARLY + LATE],
     )
     return volt.reshape(4, 16, 128), out.reshape(4, STATES, 16, 128).transpose(0, 2, 1, 3)
 

time: 113 us -> 108 us (0.956)
  the two profiles are of different devices: /device:TPU:88 before, /device:TPU:7 now
where the time goes in v3:
time: 108 us; the launch traced here: 107 us
  starting transfers between devices  45 us (42%)
  waiting for transfers between devices  27.6 us (26%)
  blocking collectives  17.6 us (16%)
  Pallas kernels  10 us (9%)
  local copies, waits for them, and re-layouts  3.27 us (3%)
  other arithmetic  2.48 us (2%)
  between operations  1.31 us (1%)
    ppermute x2, starting transfers between devices, local(): lax.ppermute(tied(v, got[e1], got[e2]), 'cols', to_light(m))  12.9 us
    ppermute x4, starting transfers between devices, shift(): lax.ppermute(value[0], axis, [(i, i + 1) for i in range(peers - 1)])  12.4 us
    ppermute x4, waiting for transfers between devices, shift(): lax.ppermute(value[1], axis, [(i + 1, i) for i in range(peers - 1)])  11.9 us
    all_gather x1, blocking collectives, halo_depth_last(): layers = lax.all_gather(jnp.stack([face(0), face(-1)]), 'depth')  11.7 us
    ppermute x8, starting transfers between devices, send(): got[m] = lax.ppermute(tied(message[m], *after), 'cols', to_heavy(m))  10.3 us
    pallas_call x6, Pallas kernels, call(): pl.pallas_call(body, out_shape=tuple(outs), in_specs=[SMEM if v.ndim == 1...  10 us
    ppermute x2, waiting for transfers between devices, local(): back = [lax.ppermute(v, 'cols', to_heavy(m)) for m, v in zip(LATE, back)]  8.67 us
    ppermute x8, waiting for transfers between devices, send(): got[m] = lax.ppermute(tied(message[m], *after), 'cols', to_heavy(m))  6.93 us
  transfers between devices with their start and end apart: 20, of which 7 were waited for; matrix products, arithmetic and copies ran while one was open for 3% of the time, Pallas kernels for 4%

profile of v3, /device:TPU:7, one launch (start us, length us, event | category | flops | bytes accessed | tf_op | source)
XLA Modules:
  0.0 107.2 jit_solution(10390845950453830931)
XLA Ops:
  0.7 0.8 fusion.19
  1.5 0.0 copy-start.10
  1.5 0.0 copy-start.4
  1.5 1.2 %dynamic-slice_bitcast_fusion = (f32[1,41,4,128]{3,2,1,0:T(4,128)S(1)}, f32[1,41,4,128]{3,2,1,0:T(4,128)S(1)}, f32[1,41,4,128]{3,2,1,0:T(4,128)S(1)}, f32[1,41,4...) fusion(f32[1,16,4,41,128]{4,2,3,1,0:T(4,128)} %param.19, ...), kind=kLoop, calls=%fused_computation.8 | loop fusion | bytes 1343520 | tf_op jit(solution)/shard_map/jit(dynamic_index_in_dim)/dynamic_slice | solution.py:344
  2.8 0.0 copy-start.12
  2.9 1.3 %collective-permute-start.2 = (f32[168,128]{1,0:T(8,128)S(1)}, f32[168,128]{1,0:T(8,128)S(1)}, u32[]{:S(2)}, u32[]{:S(2)}) collective-permute-start(f32[168,128]{1,0:T(8,128)S(1)} %pad_maximum_fusion), channel_id=1, source_target_pairs={{8,7},{9,6},{10,5},{11,4},{12,3},{13,2},{14,1},{15,0},{24,23},{25,... | collective-permute-start | bytes 258056 | tf_op jit(solution)/shard_map/ppermute | solution.py:351
  4.2 0.0 copy-start.2
  4.2 1.3 %collective-permute-start.5 = (f32[168,128]{1,0:T(8,128)S(1)}, f32[168,128]{1,0:T(8,128)S(1)}, u32[]{:S(2)}, u32[]{:S(2)}) collective-permute-start(f32[168,128]{1,0:T(8,128)S(1)} %pad_maximum_fusion.1), channel_id=1, source_target_pairs={{8,3},{9,2},{10,1},{11,0},{12,7},{13,6},{14,5},{15,4},{24,19},{25,... | collective-permute-start | bytes 258056 | tf_op jit(solution)/shard_map/ppermute | solution.py:351
  5.6 1.3 %collective-permute-start.6 = (f32[168,128]{1,0:T(8,128)S(1)}, f32[168,128]{1,0:T(8,128)S(1)}, u32[]{:S(2)}, u32[]{:S(2)}) collective-permute-start(f32[168,128]{1,0:T(8,128)S(1)} %pad_maximum_fusion.2), channel_id=1, source_target_pairs={{8,2},{9,3},{10,0},{11,1},{12,6},{13,7},{14,4},{15,5},{24,18},{25,... | collective-permute-start | bytes 258056 | tf_op jit(solution)/shard_map/ppermute | solution.py:351
  6.9 0.0 copy-start.7
  6.9 0.0 copy-start.8
  7.0 0.0 copy-start.9
  7.0 5.9 %all-gather = f32[8,16,128]{2,1,0:T(8,128)S(1)} all-gather(f32[2,16,128]{2,1,0:T(8,128)S(1)} %pad_maximum_fusion.12), channel_id=2, replica_groups=mesh['depth'=4,'rows'=8,'cols'=16] {'depth'}, dimensions={0}, use_global_device_ids=true | all-gather | bytes 81920 | tf_op jit(solution)/shard_map/all_gather | solution.py:267
  12.9 4.7 %collective-permute-start = (f32[6,1,128]{2,1,0:T(1,128)S(1)}, f32[6,1,128]{2,1,0:T(1,128)S(1)}, u32[]{:S(2)}, u32[]{:S(2)}) collective-permute-start(f32[6,1,128]{2,1,0:T(1,128)S(1)} %get-tuple-element.74), channel_id=1, source_target_pairs={{0,16},{16,32},{32,48},{48,64},{64,80},{80,96},{96,112},{1,17},{17... | collective-permute-start | bytes 9224 | tf_op jit(solution)/shard_map/ppermute | solution.py:260
  17.6 1.9 %collective-permute-start.1 = (f32[6,1,128]{2,1,0:T(1,128)S(1)}, f32[6,1,128]{2,1,0:T(1,128)S(1)}, u32[]{:S(2)}, u32[]{:S(2)}) collective-permute-start(f32[6,1,128]{2,1,0:T(1,128)S(1)} %get-tuple-element.75), channel_id=1, source_target_pairs={{16,0},{32,16},{48,32},{64,48},{80,64},{96,80},{112,96},{17,1},{33... | collective-permute-start | bytes 9224 | tf_op jit(solution)/shard_map/ppermute | solution.py:261
  19.6 0.1 reshape.197
  19.6 0.1 reshape.198
  19.7 0.1 copy.27
  19.8 0.1 reshape.190
  20.0 0.1 pad_maximum_fusion.16.coef_ref
  20.1 0.6 pad_maximum_fusion.5
  20.8 0.7 pad_maximum_fusion.6
  21.4 0.1 pad_add_fusion.plan_ref
  21.6 4.0 %collective-permute-done.1 = f32[6,1,128]{2,1,0:T(1,128)S(1)} collective-permute-done((f32[6,1,128]{2,1,0:T(1,128)S(1)}, f32[6,1,128]{2,1,0:T(1,128)S(1)}, u32[]{:S(2)}, u32[]{:S(2)}) %collective-permute-start.1) | collective-permute-done | bytes 3104 | tf_op jit(solution)/shard_map/ppermute | solution.py:261
  25.6 6.9 %collective-permute-done.2.refs_0_ = f32[168,128]{1,0:T(8,128)S(1)} collective-permute-done((f32[168,128]{1,0:T(8,128)S(1)}, f32[168,128]{1,0:T(8,128)S(1)}, u32[]{:S(2)}, u32[]{:S(2)}) %collective-permute-start.2) | collective-permute-done | bytes 86048 | tf_op jit(solution)/shard_map/ppermute | solution.py:351
  32.5 0.2 slice_reduce_fusion
  32.7 1.3 %collective-permute-start.3 = (f32[6,18]{1,0:T(8,128)S(1)}, f32[6,18]{1,0:T(8,128)S(1)}, u32[]{:S(2)}, u32[]{:S(2)}) collective-permute-start(f32[6,18]{1,0:T(8,128)S(1)} %get-tuple-element.57), channel_id=1, source_target_pairs={{0,1},{1,2},{2,3},{3,4},{4,5},{5,6},{6,7},{7,8},{8,9},{9,10},{10,1... | collective-permute-start | bytes 1304 | tf_op jit(solution)/shard_map/ppermute | solution.py:260
  34.0 1.3 %collective-permute-start.4 = (f32[6,18]{1,0:T(8,128)S(1)}, f32[6,18]{1,0:T(8,128)S(1)}, u32[]{:S(2)}, u32[]{:S(2)}) collective-permute-start(f32[6,18]{1,0:T(8,128)S(1)} %get-tuple-element.56), channel_id=1, source_target_pairs={{1,0},{2,1},{3,2},{4,3},{5,4},{6,5},{7,6},{8,7},{9,8},{10,9},{11,1... | collective-permute-start | bytes 1304 | tf_op jit(solution)/shard_map/ppermute | solution.py:261
  35.3 1.3 %collective-permute-start.9 = (f32[168,128]{1,0:T(8,128)}, f32[168,128]{1,0:T(8,128)S(1)}, u32[]{:S(2)}, u32[]{:S(2)}) collective-permute-start(f32[168,128]{1,0:T(8,128)} %pad_maximum_fusion.5), channel_id=1, source_target_pairs={{8,1},{9,0},{10,3},{11,2},{12,5},{13,4},{14,7},{15,6},{24,17},{25,... | collective-permute-start | bytes 258056 | tf_op jit(solution)/shard_map/ppermute | solution.py:351
  36.6 0.1 copy.28.before_ref
  36.8 1.6 %collective-permute-done.4 = f32[6,18]{1,0:T(8,128)S(1)} collective-permute-done((f32[6,18]{1,0:T(8,128)S(1)}, f32[6,18]{1,0:T(8,128)S(1)}, u32[]{:S(2)}, u32[]{:S(2)}) %collective-permute-start.4) | collective-permute-done | bytes 464 | tf_op jit(solution)/shard_map/ppermute | solution.py:261
  38.3 0.1 copy.29.after_ref
  38.5 0.7 shard_map.158
  39.2 1.3 %collective-permute-start.10 = (f32[168,128]{1,0:T(8,128)}, f32[168,128]{1,0:T(8,128)S(1)}, u32[]{:S(2)}, u32[]{:S(2)}) collective-permute-start(f32[168,128]{1,0:T(8,128)} %get-tuple-element.42), channel_id=1, source_target_pairs={{8,0},{9,1},{10,2},{11,3},{12,4},{13,5},{14,6},{15,7},{24,16},{25,... | collective-permute-start | bytes 258056 | tf_op jit(solution)/shard_map/ppermute | solution.py:351
  40.5 11.5 %collective-permute-start.7 = (f32[4,128]{1,0:T(4,128)S(1)}, f32[4,128]{1,0:T(4,128)S(1)}, u32[]{:S(2)}, u32[]{:S(2)}) collective-permute-start(f32[4,128]{1,0:T(4,128)S(1)} %get-tuple-element.33), channel_id=1, source_target_pairs={{5,8},{4,9},{7,10},{6,11},{1,12},{0,13},{3,14},{2,15},{21,24},{20,... | collective-permute-start | bytes 6152 | tf_op jit(solution)/shard_map/ppermute | solution.py:373
  52.0 1.5 %collective-permute-start.8 = (f32[4,128]{1,0:T(4,128)S(1)}, f32[4,128]{1,0:T(4,128)S(1)}, u32[]{:S(2)}, u32[]{:S(2)}) collective-permute-start(f32[4,128]{1,0:T(4,128)S(1)} %get-tuple-element.35), channel_id=1, source_target_pairs={{4,8},{5,9},{6,10},{7,11},{0,12},{1,13},{2,14},{3,15},{20,24},{21,... | collective-permute-start | bytes 6152 | tf_op jit(solution)/shard_map/ppermute | solution.py:373
  53.4 1.3 %collective-permute-start.11 = (f32[168,128]{1,0:T(8,128)}, f32[168,128]{1,0:T(8,128)S(1)}, u32[]{:S(2)}, u32[]{:S(2)}) collective-permute-start(f32[168,128]{1,0:T(8,128)} %get-tuple-element.43), channel_id=1, source_target_pairs={{8,6},{9,7},{10,4},{11,5},{12,2},{13,3},{14,0},{15,1},{24,22},{25,... | collective-permute-start | bytes 258056 | tf_op jit(solution)/shard_map/ppermute | solution.py:351
  54.8 0.1 reshape.192
  54.8 0.1 reshape.195
  54.9 0.1 reshape.196
  55.0 0.1 reshape.193
  55.1 0.1 reshape.194
  55.2 0.1 concatenate.61.tab_ref
  55.3 0.8 shard_map.159
  56.1 1.3 %collective-permute-start.12 = (f32[4,128]{1,0:T(4,128)S(1)}, f32[4,128]{1,0:T(4,128)S(1)}, u32[]{:S(2)}, u32[]{:S(2)}) collective-permute-start(f32[4,128]{1,0:T(4,128)S(1)} %get-tuple-element.36), channel_id=1, source_target_pairs={{8,5},{9,4},{10,7},{11,6},{12,1},{13,0},{14,3},{15,2},{24,21},{25,... | collective-permute-start | bytes 6152 | tf_op jit(solution)/shard_map/ppermute | solution.py:383
  57.4 1.3 %collective-permute-start.13 = (f32[4,128]{1,0:T(4,128)S(1)}, f32[4,128]{1,0:T(4,128)S(1)}, u32[]{:S(2)}, u32[]{:S(2)}) collective-permute-start(f32[4,128]{1,0:T(4,128)S(1)} %get-tuple-element.37), channel_id=1, source_target_pairs={{8,4},{9,5},{10,6},{11,7},{12,0},{13,1},{14,2},{15,3},{24,20},{25,... | collective-permute-start | bytes 6152 | tf_op jit(solution)/shard_map/ppermute | solution.py:383
  58.7 1.7 %shard_map.160 = (f32[2624,128]{1,0:T(8,128)S(1)}, f32[64,128]{1,0:T(8,128)S(1)}) custom-call(f32[615]{0:T(1024)S(1)} %concatenate.61.tab_ref, f32[2624,128]{1,0:T(8,128)S(1)} %bitcast.93, f32[64,128]{1,0:T(8,128)S(1)} %get-tuple-element.38.level_ref.first_ref, s32[64,128]{1,0:T(8,128)S(1)} %bitcast.97), custom_call_target="tpu_custom_call" | custom-call | bytes 2787740 | tf_op jit(solution)/shard_map/pallas_call | solution.py:245
  60.4 1.1 %shard_map.161 = (f32[64,128]{1,0:T(8,128)S(1)}, f32[168,128]{1,0:T(8,128)S(1)}, f32[168,128]{1,0:T(8,128)S(1)}, f32[168,128]{1,0:T(8,128)S(1)}, f32[168,128]{1,0:T(8,128)S(1)}) custom-call(s32[81]{0:T(128)S(1)} %pad_add_fusion.plan_ref, f32[615]{0:T(1024)S(1)} %concatenate.61.tab_ref, f32[64,128]{1,0:T(8,128)S(1)} %get-tuple-element.38.level_ref.first_ref, ...), custom_call_target="tpu_custom_call" | custom-call | bytes 789216 | tf_op jit(solution)/shard_map/pallas_call | solution.py:245
  61.5 7.4 %collective-permute-done.12.refs_2_ = f32[4,128]{1,0:T(4,128)S(1)} collective-permute-done((f32[4,128]{1,0:T(4,128)S(1)}, f32[4,128]{1,0:T(4,128)S(1)}, u32[]{:S(2)}, u32[]{:S(2)}) %collective-permute-start.12) | collective-permute-done | bytes 2080 | tf_op jit(solution)/shard_map/ppermute | solution.py:383
  68.9 1.3 %collective-permute-done.13.refs_3_ = f32[4,128]{1,0:T(4,128)S(1)} collective-permute-done((f32[4,128]{1,0:T(4,128)S(1)}, f32[4,128]{1,0:T(4,128)S(1)}, u32[]{:S(2)}, u32[]{:S(2)}) %collective-permute-start.13) | collective-permute-done | bytes 2080 | tf_op jit(solution)/shard_map/ppermute | solution.py:383
  70.2 1.0 shard_map.162
  71.2 3.0 %collective-permute-start.14 = (f32[4,1,128]{2,1,0:T(1,128)S(1)}, f32[4,1,128]{2,1,0:T(1,128)S(1)}, u32[]{:S(2)}, u32[]{:S(2)}) collective-permute-start(f32[4,1,128]{2,1,0:T(1,128)S(1)} %get-tuple-element.76), channel_id=1, source_target_pairs={{0,16},{16,32},{32,48},{48,64},{64,80},{80,96},{96,112},{1,17},{17... | collective-permute-start | bytes 6152 | tf_op jit(solution)/shard_map/ppermute | solution.py:260
  74.2 2.3 %collective-permute-start.15 = (f32[4,1,128]{2,1,0:T(1,128)S(1)}, f32[4,1,128]{2,1,0:T(1,128)S(1)}, u32[]{:S(2)}, u32[]{:S(2)}) collective-permute-start(f32[4,1,128]{2,1,0:T(1,128)S(1)} %get-tuple-element.77), channel_id=1, source_target_pairs={{16,0},{32,16},{48,32},{64,48},{80,64},{96,80},{112,96},{17,1},{33... | collective-permute-start | bytes 6152 | tf_op jit(solution)/shard_map/ppermute | solution.py:261
  76.5 1.3 %collective-permute-start.18 = (f32[168,128]{1,0:T(8,128)S(1)}, f32[168,128]{1,0:T(8,128)S(1)}, u32[]{:S(2)}, u32[]{:S(2)}) collective-permute-start(f32[168,128]{1,0:T(8,128)S(1)} %get-tuple-element.52.refs_0_), channel_id=1, source_target_pairs={{8,5},{9,4},{10,7},{11,6},{12,1},{13,0},{14,3},{15,2},{24,21},{25,... | collective-permute-start | bytes 258056 | tf_op jit(solution)/shard_map/ppermute | solution.py:351
  77.8 1.3 %collective-permute-start.19 = (f32[168,128]{1,0:T(8,128)S(1)}, f32[168,128]{1,0:T(8,128)S(1)}, u32[]{:S(2)}, u32[]{:S(2)}) collective-permute-start(f32[168,128]{1,0:T(8,128)S(1)} %get-tuple-element.53.refs_1_), channel_id=1, source_target_pairs={{8,4},{9,5},{10,6},{11,7},{12,0},{13,1},{14,2},{15,3},{24,20},{25,... | collective-permute-start | bytes 258056 | tf_op jit(solution)/shard_map/ppermute | solution.py:351
  79.1 3.1 %collective-permute-done.15 = f32[4,1,128]{2,1,0:T(1,128)S(1)} collective-permute-done((f32[4,1,128]{2,1,0:T(1,128)S(1)}, f32[4,1,128]{2,1,0:T(1,128)S(1)}, u32[]{:S(2)}, u32[]{:S(2)}) %collective-permute-start.15) | collective-permute-done | bytes 2080 | tf_op jit(solution)/shard_map/ppermute | solution.py:261
  82.2 0.2 slice_reduce_fusion.3
  82.3 3.4 %collective-permute-start.16 = (f32[4,18]{1,0:T(4,128)S(1)}, f32[4,18]{1,0:T(4,128)S(1)}, u32[]{:S(2)}, u32[]{:S(2)}) collective-permute-start(f32[4,18]{1,0:T(4,128)S(1)} %get-tuple-element.58), channel_id=1, source_target_pairs={{0,1},{1,2},{2,3},{3,4},{4,5},{5,6},{6,7},{7,8},{8,9},{9,10},{10,1... | collective-permute-start | bytes 872 | tf_op jit(solution)/shard_map/ppermute | solution.py:260
  85.7 1.3 %collective-permute-start.17 = (f32[4,18]{1,0:T(4,128)S(1)}, f32[4,18]{1,0:T(4,128)S(1)}, u32[]{:S(2)}, u32[]{:S(2)}) collective-permute-start(f32[4,18]{1,0:T(4,128)S(1)} %get-tuple-element.59), channel_id=1, source_target_pairs={{1,0},{2,1},{3,2},{4,3},{5,4},{6,5},{7,6},{8,7},{9,8},{10,9},{11,1... | collective-permute-start | bytes 872 | tf_op jit(solution)/shard_map/ppermute | solution.py:261
  87.0 3.3 %collective-permute-done.17 = f32[4,18]{1,0:T(4,128)S(1)} collective-permute-done((f32[4,18]{1,0:T(4,128)S(1)}, f32[4,18]{1,0:T(4,128)S(1)}, u32[]{:S(2)}, u32[]{:S(2)}) %collective-permute-start.17) | collective-permute-done | bytes 320 | tf_op jit(solution)/shard_map/ppermute | solution.py:261
  90.4 11.7 %all-gather.1 = f32[8,24,128]{2,1,0:T(8,128)S(1)} all-gather(f32[2,24,128]{2,1,0:T(8,128)S(1)} %pad_maximum_fusion.11), channel_id=3, replica_groups=mesh['depth'=4,'rows'=8,'cols'=16] {'depth'}, dimensions={0}, use_global_device_ids=true | all-gather | bytes 122880 | tf_op jit(solution)/shard_map/all_gather | solution.py:285
  102.2 0.1 copy.30.before_ref
  102.3 0.1 copy.31.after_ref
  102.5 4.8 %shard_map.163 = (f32[64,128]{1,0:T(8,128)}, f32[2624,128]{1,0:T(8,128)}) custom-call(s32[81]{0:T(128)S(1)} %pad_add_fusion.plan_ref, f32[615]{0:T(1024)S(1)} %concatenate.61.tab_ref, f32[48]{0:T(128)S(1)} %pad_maximum_fusion.16.coef_ref, f32[6,18,128]{2,1,0:T(8,128)S(1)} %pad_maximum_fusion.9.planes_ref, f32[6,18,1]{2,1,0:T(8,128)S(1)} %copy.30.before_ref, ...), custom_call_target="tpu_custom_call" | custom-call | bytes 3565312 | tf_op jit(solution)/shard_map/pallas_call | solution.py:245
  (67 shorter events, 0.5 us)
Async XLA Ops:
  0.6 6.3 %copy-start.3 = (f32[4,16,128]{2,1,0:T(8,128)S(1)}, f32[4,16,128]{2,1,0:T(8,128)}, u32[]{:S(2)}) copy-start(f32[4,16,128]{2,1,0:T(8,128)} %param.15) | copy-start | bytes 98308
  1.5 18.0 %copy-start.5 = (f32[3,8]{1,0:T(4,128)S(1)}, f32[3,8]{1,0:T(4,128)}, u32[]{:S(2)}) copy-start(f32[3,8]{1,0:T(4,128)} %param.23) | copy-start | bytes 292
  1.5 18.1 %copy-start.6 = (f32[3,8]{1,0:T(4,128)S(1)}, f32[3,8]{1,0:T(4,128)}, u32[]{:S(2)}) copy-start(f32[3,8]{1,0:T(4,128)} %param.24) | copy-start | bytes 292
  1.5 18.2 %copy-start.10 = (f32[3,41]{1,0:T(4,128)S(1)}, f32[3,41]{1,0:T(4,128)}, u32[]{:S(2)}) copy-start(f32[3,41]{1,0:T(4,128)} %param.26) | copy-start | bytes 1480
  1.5 18.2 %copy-start.4 = (s32[1,16,4]{1,2,0:T(4,128)S(1)}, s32[1,16,4]{1,2,0:T(4,128)}, u32[]{:S(2)}) copy-start(s32[1,16,4]{1,2,0:T(4,128)} %param.21) | copy-start | bytes 772
  2.8 18.6 %copy-start.12 = (s32[1,16]{1,0:T(1,128)S(1)}, s32[1,16]{1,0:T(1,128)}, u32[]{:S(2)}) copy-start(s32[1,16]{1,0:T(1,128)} %param.22) | copy-start | bytes 196
  2.9 29.6 %collective-permute-start.2 = (f32[168,128]{1,0:T(8,128)S(1)}, f32[168,128]{1,0:T(8,128)S(1)}, u32[]{:S(2)}, u32[]{:S(2)}) collective-permute-start(f32[168,128]{1,0:T(8,128)S(1)} %pad_maximum_fusion), channel_id=1, source_target_pairs={{8,7},{9,6},{10,5},{11,4},{12,3},{13,2},{14,1},{15,0},{24,23},{25,... | collective-permute-start | bytes 258056 | tf_op jit(solution)/shard_map/ppermute | solution.py:351
  4.2 34.3 %copy-start.2 = (s32[4,16,128]{2,1,0:T(8,128)S(1)}, s32[4,16,128]{2,1,0:T(8,128)}, u32[]{:S(2)}) copy-start(s32[4,16,128]{2,1,0:T(8,128)} %fibre_ref.3) | copy-start | bytes 98308
  4.2 35.0 %collective-permute-start.5 = (f32[168,128]{1,0:T(8,128)S(1)}, f32[168,128]{1,0:T(8,128)S(1)}, u32[]{:S(2)}, u32[]{:S(2)}) collective-permute-start(f32[168,128]{1,0:T(8,128)S(1)} %pad_maximum_fusion.1), channel_id=1, source_target_pairs={{8,3},{9,2},{10,1},{11,0},{12,7},{13,6},{14,5},{15,4},{24,19},{25,... | collective-permute-start | bytes 258056 | tf_op jit(solution)/shard_map/ppermute | solution.py:351
  5.6 34.9 %collective-permute-start.6 = (f32[168,128]{1,0:T(8,128)S(1)}, f32[168,128]{1,0:T(8,128)S(1)}, u32[]{:S(2)}, u32[]{:S(2)}) collective-permute-start(f32[168,128]{1,0:T(8,128)S(1)} %pad_maximum_fusion.2), channel_id=1, source_target_pairs={{8,2},{9,3},{10,0},{11,1},{12,6},{13,7},{14,4},{15,5},{24,18},{25,... | collective-permute-start | bytes 258056 | tf_op jit(solution)/shard_map/ppermute | solution.py:351
  6.9 47.8 %copy-start.7 = (f32[3,41]{1,0:T(4,128)S(1)}, f32[3,41]{1,0:T(4,128)}, u32[]{:S(2)}) copy-start(f32[3,41]{1,0:T(4,128)} %param.25) | copy-start | bytes 1480
  6.9 47.9 %copy-start.8 = (f32[3,41]{1,0:T(4,128)S(1)}, f32[3,41]{1,0:T(4,128)}, u32[]{:S(2)}) copy-start(f32[3,41]{1,0:T(4,128)} %param.28) | copy-start | bytes 1480
  7.0 48.0 %copy-start.9 = (f32[3,41]{1,0:T(4,128)S(1)}, f32[3,41]{1,0:T(4,128)}, u32[]{:S(2)}) copy-start(f32[3,41]{1,0:T(4,128)} %param.29) | copy-start | bytes 1480
  7.0 48.1 %copy-start.11 = (f32[3,41]{1,0:T(4,128)S(1)}, f32[3,41]{1,0:T(4,128)}, u32[]{:S(2)}) copy-start(f32[3,41]{1,0:T(4,128)} %param.27) | copy-start | bytes 1480
  12.9 8.7 %collective-permute-start = (f32[6,1,128]{2,1,0:T(1,128)S(1)}, f32[6,1,128]{2,1,0:T(1,128)S(1)}, u32[]{:S(2)}, u32[]{:S(2)}) collective-permute-start(f32[6,1,128]{2,1,0:T(1,128)S(1)} %get-tuple-element.74), channel_id=1, source_target_pairs={{0,16},{16,32},{32,48},{48,64},{64,80},{80,96},{96,112},{1,17},{17... | collective-permute-start | bytes 9224 | tf_op jit(solution)/shard_map/ppermute | solution.py:260
  17.6 8.0 %collective-permute-start.1 = (f32[6,1,128]{2,1,0:T(1,128)S(1)}, f32[6,1,128]{2,1,0:T(1,128)S(1)}, u32[]{:S(2)}, u32[]{:S(2)}) collective-permute-start(f32[6,1,128]{2,1,0:T(1,128)S(1)} %get-tuple-element.75), channel_id=1, source_target_pairs={{16,0},{32,16},{48,32},{64,48},{80,64},{96,80},{112,96},{17,1},{33... | collective-permute-start | bytes 9224 | tf_op jit(solution)/shard_map/ppermute | solution.py:261
  19.8 38.9 %copy-start = (f32[4,16,41,128]{3,1,2,0:T(8,128)S(1)}, f32[4,16,41,128]{3,1,2,0:T(8,128)}, u32[]{:S(2)}) copy-start(f32[4,16,41,128]{3,1,2,0:T(8,128)} %param.16) | copy-start | bytes 4030468
  19.8 38.9 %copy-start.1 = (s32[4,16,128]{2,1,0:T(8,128)S(1)}, s32[4,16,128]{2,1,0:T(8,128)}, u32[]{:S(2)}) copy-start(s32[4,16,128]{2,1,0:T(8,128)} %param.17) | copy-start | bytes 98308
  32.7 3.9 %collective-permute-start.3 = (f32[6,18]{1,0:T(8,128)S(1)}, f32[6,18]{1,0:T(8,128)S(1)}, u32[]{:S(2)}, u32[]{:S(2)}) collective-permute-start(f32[6,18]{1,0:T(8,128)S(1)} %get-tuple-element.57), channel_id=1, source_target_pairs={{0,1},{1,2},{2,3},{3,4},{4,5},{5,6},{6,7},{7,8},{8,9},{9,10},{10,1... | collective-permute-start | bytes 1304 | tf_op jit(solution)/shard_map/ppermute | solution.py:260
  34.0 4.4 %collective-permute-start.4 = (f32[6,18]{1,0:T(8,128)S(1)}, f32[6,18]{1,0:T(8,128)S(1)}, u32[]{:S(2)}, u32[]{:S(2)}) collective-permute-start(f32[6,18]{1,0:T(8,128)S(1)} %get-tuple-element.56), channel_id=1, source_target_pairs={{1,0},{2,1},{3,2},{4,3},{5,4},{6,5},{7,6},{8,7},{9,8},{10,9},{11,1... | collective-permute-start | bytes 1304 | tf_op jit(solution)/shard_map/ppermute | solution.py:261
  35.3 25.1 %collective-permute-start.9 = (f32[168,128]{1,0:T(8,128)}, f32[168,128]{1,0:T(8,128)S(1)}, u32[]{:S(2)}, u32[]{:S(2)}) collective-permute-start(f32[168,128]{1,0:T(8,128)} %pad_maximum_fusion.5), channel_id=1, source_target_pairs={{8,1},{9,0},{10,3},{11,2},{12,5},{13,4},{14,7},{15,6},{24,17},{25,... | collective-permute-start | bytes 258056 | tf_op jit(solution)/shard_map/ppermute | solution.py:351
  39.2 31.0 %collective-permute-start.10 = (f32[168,128]{1,0:T(8,128)}, f32[168,128]{1,0:T(8,128)S(1)}, u32[]{:S(2)}, u32[]{:S(2)}) collective-permute-start(f32[168,128]{1,0:T(8,128)} %get-tuple-element.42), channel_id=1, source_target_pairs={{8,0},{9,1},{10,2},{11,3},{12,4},{13,5},{14,6},{15,7},{24,16},{25,... | collective-permute-start | bytes 258056 | tf_op jit(solution)/shard_map/ppermute | solution.py:351
  40.5 14.8 %collective-permute-start.7 = (f32[4,128]{1,0:T(4,128)S(1)}, f32[4,128]{1,0:T(4,128)S(1)}, u32[]{:S(2)}, u32[]{:S(2)}) collective-permute-start(f32[4,128]{1,0:T(4,128)S(1)} %get-tuple-element.33), channel_id=1, source_target_pairs={{5,8},{4,9},{7,10},{6,11},{1,12},{0,13},{3,14},{2,15},{21,24},{20,... | collective-permute-start | bytes 6152 | tf_op jit(solution)/shard_map/ppermute | solution.py:373
  52.0 3.3 %collective-permute-start.8 = (f32[4,128]{1,0:T(4,128)S(1)}, f32[4,128]{1,0:T(4,128)S(1)}, u32[]{:S(2)}, u32[]{:S(2)}) collective-permute-start(f32[4,128]{1,0:T(4,128)S(1)} %get-tuple-element.35), channel_id=1, source_target_pairs={{4,8},{5,9},{6,10},{7,11},{0,12},{1,13},{2,14},{3,15},{20,24},{21,... | collective-permute-start | bytes 6152 | tf_op jit(solution)/shard_map/ppermute | solution.py:373
  53.4 16.8 %collective-permute-start.11 = (f32[168,128]{1,0:T(8,128)}, f32[168,128]{1,0:T(8,128)S(1)}, u32[]{:S(2)}, u32[]{:S(2)}) collective-permute-start(f32[168,128]{1,0:T(8,128)} %get-tuple-element.43), channel_id=1, source_target_pairs={{8,6},{9,7},{10,4},{11,5},{12,2},{13,3},{14,0},{15,1},{24,22},{25,... | collective-permute-start | bytes 258056 | tf_op jit(solution)/shard_map/ppermute | solution.py:351
  56.1 12.8 %collective-permute-start.12 = (f32[4,128]{1,0:T(4,128)S(1)}, f32[4,128]{1,0:T(4,128)S(1)}, u32[]{:S(2)}, u32[]{:S(2)}) collective-permute-start(f32[4,128]{1,0:T(4,128)S(1)} %get-tuple-element.36), channel_id=1, source_target_pairs={{8,5},{9,4},{10,7},{11,6},{12,1},{13,0},{14,3},{15,2},{24,21},{25,... | collective-permute-start | bytes 6152 | tf_op jit(solution)/shard_map/ppermute | solution.py:383
  57.4 12.8 %collective-permute-start.13 = (f32[4,128]{1,0:T(4,128)S(1)}, f32[4,128]{1,0:T(4,128)S(1)}, u32[]{:S(2)}, u32[]{:S(2)}) collective-permute-start(f32[4,128]{1,0:T(4,128)S(1)} %get-tuple-element.37), channel_id=1, source_target_pairs={{8,4},{9,5},{10,6},{11,7},{12,0},{13,1},{14,2},{15,3},{24,20},{25,... | collective-permute-start | bytes 6152 | tf_op jit(solution)/shard_map/ppermute | solution.py:383
  71.2 7.9 %collective-permute-start.14 = (f32[4,1,128]{2,1,0:T(1,128)S(1)}, f32[4,1,128]{2,1,0:T(1,128)S(1)}, u32[]{:S(2)}, u32[]{:S(2)}) collective-permute-start(f32[4,1,128]{2,1,0:T(1,128)S(1)} %get-tuple-element.76), channel_id=1, source_target_pairs={{0,16},{16,32},{32,48},{48,64},{64,80},{80,96},{96,112},{1,17},{17... | collective-permute-start | bytes 6152 | tf_op jit(solution)/shard_map/ppermute | solution.py:260
  74.2 7.9 %collective-permute-start.15 = (f32[4,1,128]{2,1,0:T(1,128)S(1)}, f32[4,1,128]{2,1,0:T(1,128)S(1)}, u32[]{:S(2)}, u32[]{:S(2)}) collective-permute-start(f32[4,1,128]{2,1,0:T(1,128)S(1)} %get-tuple-element.77), channel_id=1, source_target_pairs={{16,0},{32,16},{48,32},{64,48},{80,64},{96,80},{112,96},{17,1},{33... | collective-permute-start | bytes 6152 | tf_op jit(solution)/shard_map/ppermute | solution.py:261
  76.5 26.0 %collective-permute-start.18 = (f32[168,128]{1,0:T(8,128)S(1)}, f32[168,128]{1,0:T(8,128)S(1)}, u32[]{:S(2)}, u32[]{:S(2)}) collective-permute-start(f32[168,128]{1,0:T(8,128)S(1)} %get-tuple-element.52.refs_0_), channel_id=1, source_target_pairs={{8,5},{9,4},{10,7},{11,6},{12,1},{13,0},{14,3},{15,2},{24,21},{25,... | collective-permute-start | bytes 258056 | tf_op jit(solution)/shard_map/ppermute | solution.py:351
  77.8 24.7 %collective-permute-start.19 = (f32[168,128]{1,0:T(8,128)S(1)}, f32[168,128]{1,0:T(8,128)S(1)}, u32[]{:S(2)}, u32[]{:S(2)}) collective-permute-start(f32[168,128]{1,0:T(8,128)S(1)} %get-tuple-element.53.refs_1_), channel_id=1, source_target_pairs={{8,4},{9,5},{10,6},{11,7},{12,0},{13,1},{14,2},{15,3},{24,20},{25,... | collective-permute-start | bytes 258056 | tf_op jit(solution)/shard_map/ppermute | solution.py:351
  82.3 4.7 %collective-permute-start.16 = (f32[4,18]{1,0:T(4,128)S(1)}, f32[4,18]{1,0:T(4,128)S(1)}, u32[]{:S(2)}, u32[]{:S(2)}) collective-permute-start(f32[4,18]{1,0:T(4,128)S(1)} %get-tuple-element.58), channel_id=1, source_target_pairs={{0,1},{1,2},{2,3},{3,4},{4,5},{5,6},{6,7},{7,8},{8,9},{9,10},{10,1... | collective-permute-start | bytes 872 | tf_op jit(solution)/shard_map/ppermute | solution.py:260
  85.7 4.6 %collective-permute-start.17 = (f32[4,18]{1,0:T(4,128)S(1)}, f32[4,18]{1,0:T(4,128)S(1)}, u32[]{:S(2)}, u32[]{:S(2)}) collective-permute-start(f32[4,18]{1,0:T(4,128)S(1)} %get-tuple-element.59), channel_id=1, source_target_pairs={{1,0},{2,1},{3,2},{4,3},{5,4},{6,5},{7,6},{8,7},{9,8},{10,9},{11,1... | collective-permute-start | bytes 872 | tf_op jit(solution)/shard_map/ppermute | solution.py:261

commit v4 on v3

--- a/solution.py
+++ b/solution.py
@@ -139,7 +139,8 @@
         def _():
             block = plan_ref[p * 4 + s]
             start = (block // 16) * (STATES * 16) + block % 16
-            out_ref[pl.ds(start, STATES, stride=16), :] = message_ref[pl.ds(s, STATES, stride=4), :]
+            out_ref[pl.ds(start, 40, stride=16), :] = message_ref[pl.ds(s, 40, stride=4), :]
+            out_ref[pl.ds(start + 640, 1), :] = message_ref[160 + s : 161 + s, :]
 
 
 def stencil(coef_ref, planes_ref, before_ref, after_ref, fibre_ref, out_ref):

time: 108 us -> 108 us (level)
  no operation moved by 1% of the time
where the time goes in v4:
time: 108 us; the launch traced here: 107 us
  starting transfers between devices  45 us (42%)
  waiting for transfers between devices  27.6 us (26%)
  blocking collectives  17.6 us (16%)
  Pallas kernels  9.93 us (9%)
  local copies, waits for them, and re-layouts  3.27 us (3%)
  other arithmetic  2.48 us (2%)
  between operations  1.31 us (1%)
    ppermute x2, starting transfers between devices, local(): lax.ppermute(tied(v, got[e1], got[e2]), 'cols', to_light(m))  12.9 us
    ppermute x4, starting transfers between devices, shift(): lax.ppermute(value[0], axis, [(i, i + 1) for i in range(peers - 1)])  12.4 us
    ppermute x4, waiting for transfers between devices, shift(): lax.ppermute(value[1], axis, [(i + 1, i) for i in range(peers - 1)])  11.9 us
    all_gather x1, blocking collectives, halo_depth_last(): layers = lax.all_gather(jnp.stack([face(0), face(-1)]), 'depth')  11.7 us
    ppermute x8, starting transfers between devices, send(): got[m] = lax.ppermute(tied(message[m], *after), 'cols', to_heavy(m))  10.3 us
    pallas_call x6, Pallas kernels, call(): pl.pallas_call(body, out_shape=tuple(outs), in_specs=[SMEM if v.ndim == 1...  9.93 us
    ppermute x2, waiting for transfers between devices, local(): back = [lax.ppermute(v, 'cols', to_heavy(m)) for m, v in zip(LATE, back)]  8.67 us
    ppermute x8, waiting for transfers between devices, send(): got[m] = lax.ppermute(tied(message[m], *after), 'cols', to_heavy(m))  6.93 us
  transfers between devices with their start and end apart: 20, of which 7 were waited for; matrix products, arithmetic and copies ran while one was open for 3% of the time, Pallas kernels for 4%

profile of v4, /device:TPU:7, one launch (start us, length us, event | category | flops | bytes accessed | tf_op | source)
XLA Modules:
  0.0 107.1 jit_solution(11962035150376074750)
XLA Ops:
  0.7 0.8 fusion.19
  1.5 0.0 copy-start.10
  1.5 0.0 copy-start.4
  1.5 1.2 %dynamic-slice_bitcast_fusion = (f32[1,41,4,128]{3,2,1,0:T(4,128)S(1)}, f32[1,41,4,128]{3,2,1,0:T(4,128)S(1)}, f32[1,41,4,128]{3,2,1,0:T(4,128)S(1)}, f32[1,41,4...) fusion(f32[1,16,4,41,128]{4,2,3,1,0:T(4,128)} %param.19, ...), kind=kLoop, calls=%fused_computation.8 | loop fusion | bytes 1343520 | tf_op jit(solution)/shard_map/jit(dynamic_index_in_dim)/dynamic_slice | solution.py:345
  2.8 0.0 copy-start.12
  2.9 1.3 %collective-permute-start.2 = (f32[168,128]{1,0:T(8,128)S(1)}, f32[168,128]{1,0:T(8,128)S(1)}, u32[]{:S(2)}, u32[]{:S(2)}) collective-permute-start(f32[168,128]{1,0:T(8,128)S(1)} %pad_maximum_fusion), channel_id=1, source_target_pairs={{8,7},{9,6},{10,5},{11,4},{12,3},{13,2},{14,1},{15,0},{24,23},{25,... | collective-permute-start | bytes 258056 | tf_op jit(solution)/shard_map/ppermute | solution.py:352
  4.2 0.0 copy-start.2
  4.2 1.3 %collective-permute-start.5 = (f32[168,128]{1,0:T(8,128)S(1)}, f32[168,128]{1,0:T(8,128)S(1)}, u32[]{:S(2)}, u32[]{:S(2)}) collective-permute-start(f32[168,128]{1,0:T(8,128)S(1)} %pad_maximum_fusion.1), channel_id=1, source_target_pairs={{8,3},{9,2},{10,1},{11,0},{12,7},{13,6},{14,5},{15,4},{24,19},{25,... | collective-permute-start | bytes 258056 | tf_op jit(solution)/shard_map/ppermute | solution.py:352
  5.6 1.3 %collective-permute-start.6 = (f32[168,128]{1,0:T(8,128)S(1)}, f32[168,128]{1,0:T(8,128)S(1)}, u32[]{:S(2)}, u32[]{:S(2)}) collective-permute-start(f32[168,128]{1,0:T(8,128)S(1)} %pad_maximum_fusion.2), channel_id=1, source_target_pairs={{8,2},{9,3},{10,0},{11,1},{12,6},{13,7},{14,4},{15,5},{24,18},{25,... | collective-permute-start | bytes 258056 | tf_op jit(solution)/shard_map/ppermute | solution.py:352
  6.9 0.0 copy-start.7
  6.9 0.0 copy-start.8
  7.0 0.0 copy-start.11
  7.0 5.9 %all-gather = f32[8,16,128]{2,1,0:T(8,128)S(1)} all-gather(f32[2,16,128]{2,1,0:T(8,128)S(1)} %pad_maximum_fusion.12), channel_id=2, replica_groups=mesh['depth'=4,'rows'=8,'cols'=16] {'depth'}, dimensions={0}, use_global_device_ids=true | all-gather | bytes 81920 | tf_op jit(solution)/shard_map/all_gather | solution.py:268
  12.9 4.7 %collective-permute-start = (f32[6,1,128]{2,1,0:T(1,128)S(1)}, f32[6,1,128]{2,1,0:T(1,128)S(1)}, u32[]{:S(2)}, u32[]{:S(2)}) collective-permute-start(f32[6,1,128]{2,1,0:T(1,128)S(1)} %get-tuple-element.74), channel_id=1, source_target_pairs={{0,16},{16,32},{32,48},{48,64},{64,80},{80,96},{96,112},{1,17},{17... | collective-permute-start | bytes 9224 | tf_op jit(solution)/shard_map/ppermute | solution.py:261
  17.6 1.9 %collective-permute-start.1 = (f32[6,1,128]{2,1,0:T(1,128)S(1)}, f32[6,1,128]{2,1,0:T(1,128)S(1)}, u32[]{:S(2)}, u32[]{:S(2)}) collective-permute-start(f32[6,1,128]{2,1,0:T(1,128)S(1)} %get-tuple-element.75), channel_id=1, source_target_pairs={{16,0},{32,16},{48,32},{64,48},{80,64},{96,80},{112,96},{17,1},{33... | collective-permute-start | bytes 9224 | tf_op jit(solution)/shard_map/ppermute | solution.py:262
  19.6 0.1 reshape.197
  19.6 0.1 reshape.198
  19.7 0.1 copy.27
  19.8 0.1 reshape.190
  20.0 0.1 pad_maximum_fusion.16.coef_ref
  20.1 0.6 pad_maximum_fusion.5
  20.8 0.7 pad_maximum_fusion.6
  21.4 0.1 pad_add_fusion.plan_ref
  21.6 4.0 %collective-permute-done.1 = f32[6,1,128]{2,1,0:T(1,128)S(1)} collective-permute-done((f32[6,1,128]{2,1,0:T(1,128)S(1)}, f32[6,1,128]{2,1,0:T(1,128)S(1)}, u32[]{:S(2)}, u32[]{:S(2)}) %collective-permute-start.1) | collective-permute-done | bytes 3104 | tf_op jit(solution)/shard_map/ppermute | solution.py:262
  25.6 6.9 %collective-permute-done.2.refs_0_ = f32[168,128]{1,0:T(8,128)S(1)} collective-permute-done((f32[168,128]{1,0:T(8,128)S(1)}, f32[168,128]{1,0:T(8,128)S(1)}, u32[]{:S(2)}, u32[]{:S(2)}) %collective-permute-start.2) | collective-permute-done | bytes 86048 | tf_op jit(solution)/shard_map/ppermute | solution.py:352
  32.5 0.2 slice_reduce_fusion
  32.7 1.3 %collective-permute-start.3 = (f32[6,18]{1,0:T(8,128)S(1)}, f32[6,18]{1,0:T(8,128)S(1)}, u32[]{:S(2)}, u32[]{:S(2)}) collective-permute-start(f32[6,18]{1,0:T(8,128)S(1)} %get-tuple-element.57), channel_id=1, source_target_pairs={{0,1},{1,2},{2,3},{3,4},{4,5},{5,6},{6,7},{7,8},{8,9},{9,10},{10,1... | collective-permute-start | bytes 1304 | tf_op jit(solution)/shard_map/ppermute | solution.py:261
  34.0 1.3 %collective-permute-start.4 = (f32[6,18]{1,0:T(8,128)S(1)}, f32[6,18]{1,0:T(8,128)S(1)}, u32[]{:S(2)}, u32[]{:S(2)}) collective-permute-start(f32[6,18]{1,0:T(8,128)S(1)} %get-tuple-element.56), channel_id=1, source_target_pairs={{1,0},{2,1},{3,2},{4,3},{5,4},{6,5},{7,6},{8,7},{9,8},{10,9},{11,1... | collective-permute-start | bytes 1304 | tf_op jit(solution)/shard_map/ppermute | solution.py:262
  35.3 1.3 %collective-permute-start.9 = (f32[168,128]{1,0:T(8,128)}, f32[168,128]{1,0:T(8,128)S(1)}, u32[]{:S(2)}, u32[]{:S(2)}) collective-permute-start(f32[168,128]{1,0:T(8,128)} %pad_maximum_fusion.5), channel_id=1, source_target_pairs={{8,1},{9,0},{10,3},{11,2},{12,5},{13,4},{14,7},{15,6},{24,17},{25,... | collective-permute-start | bytes 258056 | tf_op jit(solution)/shard_map/ppermute | solution.py:352
  36.6 0.1 copy.28.before_ref
  36.8 1.6 %collective-permute-done.4 = f32[6,18]{1,0:T(8,128)S(1)} collective-permute-done((f32[6,18]{1,0:T(8,128)S(1)}, f32[6,18]{1,0:T(8,128)S(1)}, u32[]{:S(2)}, u32[]{:S(2)}) %collective-permute-start.4) | collective-permute-done | bytes 464 | tf_op jit(solution)/shard_map/ppermute | solution.py:262
  38.3 0.1 copy.29.after_ref
  38.5 0.7 shard_map.158
  39.2 1.3 %collective-permute-start.10 = (f32[168,128]{1,0:T(8,128)}, f32[168,128]{1,0:T(8,128)S(1)}, u32[]{:S(2)}, u32[]{:S(2)}) collective-permute-start(f32[168,128]{1,0:T(8,128)} %get-tuple-element.42), channel_id=1, source_target_pairs={{8,0},{9,1},{10,2},{11,3},{12,4},{13,5},{14,6},{15,7},{24,16},{25,... | collective-permute-start | bytes 258056 | tf_op jit(solution)/shard_map/ppermute | solution.py:352
  40.5 11.5 %collective-permute-start.7 = (f32[4,128]{1,0:T(4,128)S(1)}, f32[4,128]{1,0:T(4,128)S(1)}, u32[]{:S(2)}, u32[]{:S(2)}) collective-permute-start(f32[4,128]{1,0:T(4,128)S(1)} %get-tuple-element.33), channel_id=1, source_target_pairs={{5,8},{4,9},{7,10},{6,11},{1,12},{0,13},{3,14},{2,15},{21,24},{20,... | collective-permute-start | bytes 6152 | tf_op jit(solution)/shard_map/ppermute | solution.py:374
  52.0 1.5 %collective-permute-start.8 = (f32[4,128]{1,0:T(4,128)S(1)}, f32[4,128]{1,0:T(4,128)S(1)}, u32[]{:S(2)}, u32[]{:S(2)}) collective-permute-start(f32[4,128]{1,0:T(4,128)S(1)} %get-tuple-element.35), channel_id=1, source_target_pairs={{4,8},{5,9},{6,10},{7,11},{0,12},{1,13},{2,14},{3,15},{20,24},{21,... | collective-permute-start | bytes 6152 | tf_op jit(solution)/shard_map/ppermute | solution.py:374
  53.4 1.3 %collective-permute-start.11 = (f32[168,128]{1,0:T(8,128)}, f32[168,128]{1,0:T(8,128)S(1)}, u32[]{:S(2)}, u32[]{:S(2)}) collective-permute-start(f32[168,128]{1,0:T(8,128)} %get-tuple-element.43), channel_id=1, source_target_pairs={{8,6},{9,7},{10,4},{11,5},{12,2},{13,3},{14,0},{15,1},{24,22},{25,... | collective-permute-start | bytes 258056 | tf_op jit(solution)/shard_map/ppermute | solution.py:352
  54.8 0.1 reshape.192
  54.8 0.1 reshape.195
  54.9 0.1 reshape.196
  55.0 0.1 reshape.193
  55.1 0.1 reshape.194
  55.2 0.1 concatenate.61.tab_ref
  55.3 0.8 shard_map.159
  56.1 1.3 %collective-permute-start.12 = (f32[4,128]{1,0:T(4,128)S(1)}, f32[4,128]{1,0:T(4,128)S(1)}, u32[]{:S(2)}, u32[]{:S(2)}) collective-permute-start(f32[4,128]{1,0:T(4,128)S(1)} %get-tuple-element.36), channel_id=1, source_target_pairs={{8,5},{9,4},{10,7},{11,6},{12,1},{13,0},{14,3},{15,2},{24,21},{25,... | collective-permute-start | bytes 6152 | tf_op jit(solution)/shard_map/ppermute | solution.py:384
  57.4 1.3 %collective-permute-start.13 = (f32[4,128]{1,0:T(4,128)S(1)}, f32[4,128]{1,0:T(4,128)S(1)}, u32[]{:S(2)}, u32[]{:S(2)}) collective-permute-start(f32[4,128]{1,0:T(4,128)S(1)} %get-tuple-element.37), channel_id=1, source_target_pairs={{8,4},{9,5},{10,6},{11,7},{12,0},{13,1},{14,2},{15,3},{24,20},{25,... | collective-permute-start | bytes 6152 | tf_op jit(solution)/shard_map/ppermute | solution.py:384
  58.7 1.7 %shard_map.160 = (f32[2624,128]{1,0:T(8,128)S(1)}, f32[64,128]{1,0:T(8,128)S(1)}) custom-call(f32[615]{0:T(1024)S(1)} %concatenate.61.tab_ref, f32[2624,128]{1,0:T(8,128)S(1)} %bitcast.93, f32[64,128]{1,0:T(8,128)S(1)} %get-tuple-element.38.level_ref.first_ref, s32[64,128]{1,0:T(8,128)S(1)} %bitcast.97), custom_call_target="tpu_custom_call" | custom-call | bytes 2787740 | tf_op jit(solution)/shard_map/pallas_call | solution.py:246
  60.4 1.1 %shard_map.161 = (f32[64,128]{1,0:T(8,128)S(1)}, f32[168,128]{1,0:T(8,128)S(1)}, f32[168,128]{1,0:T(8,128)S(1)}, f32[168,128]{1,0:T(8,128)S(1)}, f32[168,128]{1,0:T(8,128)S(1)}) custom-call(s32[81]{0:T(128)S(1)} %pad_add_fusion.plan_ref, f32[615]{0:T(1024)S(1)} %concatenate.61.tab_ref, f32[64,128]{1,0:T(8,128)S(1)} %get-tuple-element.38.level_ref.first_ref, ...), custom_call_target="tpu_custom_call" | custom-call | bytes 789216 | tf_op jit(solution)/shard_map/pallas_call | solution.py:246
  61.5 7.4 %collective-permute-done.12.refs_2_ = f32[4,128]{1,0:T(4,128)S(1)} collective-permute-done((f32[4,128]{1,0:T(4,128)S(1)}, f32[4,128]{1,0:T(4,128)S(1)}, u32[]{:S(2)}, u32[]{:S(2)}) %collective-permute-start.12) | collective-permute-done | bytes 2080 | tf_op jit(solution)/shard_map/ppermute | solution.py:384
  68.9 1.3 %collective-permute-done.13.refs_3_ = f32[4,128]{1,0:T(4,128)S(1)} collective-permute-done((f32[4,128]{1,0:T(4,128)S(1)}, f32[4,128]{1,0:T(4,128)S(1)}, u32[]{:S(2)}, u32[]{:S(2)}) %collective-permute-start.13) | collective-permute-done | bytes 2080 | tf_op jit(solution)/shard_map/ppermute | solution.py:384
  70.2 1.0 shard_map.162
  71.2 3.0 %collective-permute-start.14 = (f32[4,1,128]{2,1,0:T(1,128)S(1)}, f32[4,1,128]{2,1,0:T(1,128)S(1)}, u32[]{:S(2)}, u32[]{:S(2)}) collective-permute-start(f32[4,1,128]{2,1,0:T(1,128)S(1)} %get-tuple-element.76), channel_id=1, source_target_pairs={{0,16},{16,32},{32,48},{48,64},{64,80},{80,96},{96,112},{1,17},{17... | collective-permute-start | bytes 6152 | tf_op jit(solution)/shard_map/ppermute | solution.py:261
  74.2 2.3 %collective-permute-start.15 = (f32[4,1,128]{2,1,0:T(1,128)S(1)}, f32[4,1,128]{2,1,0:T(1,128)S(1)}, u32[]{:S(2)}, u32[]{:S(2)}) collective-permute-start(f32[4,1,128]{2,1,0:T(1,128)S(1)} %get-tuple-element.77), channel_id=1, source_target_pairs={{16,0},{32,16},{48,32},{64,48},{80,64},{96,80},{112,96},{17,1},{33... | collective-permute-start | bytes 6152 | tf_op jit(solution)/shard_map/ppermute | solution.py:262
  76.5 1.3 %collective-permute-start.18 = (f32[168,128]{1,0:T(8,128)S(1)}, f32[168,128]{1,0:T(8,128)S(1)}, u32[]{:S(2)}, u32[]{:S(2)}) collective-permute-start(f32[168,128]{1,0:T(8,128)S(1)} %get-tuple-element.52.refs_0_), channel_id=1, source_target_pairs={{8,5},{9,4},{10,7},{11,6},{12,1},{13,0},{14,3},{15,2},{24,21},{25,... | collective-permute-start | bytes 258056 | tf_op jit(solution)/shard_map/ppermute | solution.py:352
  77.8 1.3 %collective-permute-start.19 = (f32[168,128]{1,0:T(8,128)S(1)}, f32[168,128]{1,0:T(8,128)S(1)}, u32[]{:S(2)}, u32[]{:S(2)}) collective-permute-start(f32[168,128]{1,0:T(8,128)S(1)} %get-tuple-element.53.refs_1_), channel_id=1, source_target_pairs={{8,4},{9,5},{10,6},{11,7},{12,0},{13,1},{14,2},{15,3},{24,20},{25,... | collective-permute-start | bytes 258056 | tf_op jit(solution)/shard_map/ppermute | solution.py:352
  79.1 3.1 %collective-permute-done.15 = f32[4,1,128]{2,1,0:T(1,128)S(1)} collective-permute-done((f32[4,1,128]{2,1,0:T(1,128)S(1)}, f32[4,1,128]{2,1,0:T(1,128)S(1)}, u32[]{:S(2)}, u32[]{:S(2)}) %collective-permute-start.15) | collective-permute-done | bytes 2080 | tf_op jit(solution)/shard_map/ppermute | solution.py:262
  82.2 0.2 slice_reduce_fusion.3
  82.3 3.4 %collective-permute-start.16 = (f32[4,18]{1,0:T(4,128)S(1)}, f32[4,18]{1,0:T(4,128)S(1)}, u32[]{:S(2)}, u32[]{:S(2)}) collective-permute-start(f32[4,18]{1,0:T(4,128)S(1)} %get-tuple-element.58), channel_id=1, source_target_pairs={{0,1},{1,2},{2,3},{3,4},{4,5},{5,6},{6,7},{7,8},{8,9},{9,10},{10,1... | collective-permute-start | bytes 872 | tf_op jit(solution)/shard_map/ppermute | solution.py:261
  85.7 1.3 %collective-permute-start.17 = (f32[4,18]{1,0:T(4,128)S(1)}, f32[4,18]{1,0:T(4,128)S(1)}, u32[]{:S(2)}, u32[]{:S(2)}) collective-permute-start(f32[4,18]{1,0:T(4,128)S(1)} %get-tuple-element.59), channel_id=1, source_target_pairs={{1,0},{2,1},{3,2},{4,3},{5,4},{6,5},{7,6},{8,7},{9,8},{10,9},{11,1... | collective-permute-start | bytes 872 | tf_op jit(solution)/shard_map/ppermute | solution.py:262
  87.0 3.3 %collective-permute-done.17 = f32[4,18]{1,0:T(4,128)S(1)} collective-permute-done((f32[4,18]{1,0:T(4,128)S(1)}, f32[4,18]{1,0:T(4,128)S(1)}, u32[]{:S(2)}, u32[]{:S(2)}) %collective-permute-start.17) | collective-permute-done | bytes 320 | tf_op jit(solution)/shard_map/ppermute | solution.py:262
  90.4 11.7 %all-gather.1 = f32[8,24,128]{2,1,0:T(8,128)S(1)} all-gather(f32[2,24,128]{2,1,0:T(8,128)S(1)} %pad_maximum_fusion.11), channel_id=3, replica_groups=mesh['depth'=4,'rows'=8,'cols'=16] {'depth'}, dimensions={0}, use_global_device_ids=true | all-gather | bytes 122880 | tf_op jit(solution)/shard_map/all_gather | solution.py:286
  102.2 0.1 copy.30.before_ref
  102.3 0.1 copy.31.after_ref
  102.5 4.7 %shard_map.163 = (f32[64,128]{1,0:T(8,128)}, f32[2624,128]{1,0:T(8,128)}) custom-call(s32[81]{0:T(128)S(1)} %pad_add_fusion.plan_ref, f32[615]{0:T(1024)S(1)} %concatenate.61.tab_ref, f32[48]{0:T(128)S(1)} %pad_maximum_fusion.16.coef_ref, f32[6,18,128]{2,1,0:T(8,128)S(1)} %pad_maximum_fusion.9.planes_ref, f32[6,18,1]{2,1,0:T(8,128)S(1)} %copy.30.before_ref, ...), custom_call_target="tpu_custom_call" | custom-call | bytes 3565312 | tf_op jit(solution)/shard_map/pallas_call | solution.py:246
  (67 shorter events, 0.5 us)
Async XLA Ops:
  0.6 6.3 %copy-start.3 = (f32[4,16,128]{2,1,0:T(8,128)S(1)}, f32[4,16,128]{2,1,0:T(8,128)}, u32[]{:S(2)}) copy-start(f32[4,16,128]{2,1,0:T(8,128)} %param.15) | copy-start | bytes 98308
  1.5 18.0 %copy-start.5 = (f32[3,8]{1,0:T(4,128)S(1)}, f32[3,8]{1,0:T(4,128)}, u32[]{:S(2)}) copy-start(f32[3,8]{1,0:T(4,128)} %param.23) | copy-start | bytes 292
  1.5 18.1 %copy-start.6 = (f32[3,8]{1,0:T(4,128)S(1)}, f32[3,8]{1,0:T(4,128)}, u32[]{:S(2)}) copy-start(f32[3,8]{1,0:T(4,128)} %param.24) | copy-start | bytes 292
  1.5 18.2 %copy-start.10 = (f32[3,41]{1,0:T(4,128)S(1)}, f32[3,41]{1,0:T(4,128)}, u32[]{:S(2)}) copy-start(f32[3,41]{1,0:T(4,128)} %param.26) | copy-start | bytes 1480
  1.5 18.2 %copy-start.4 = (s32[1,16,4]{1,2,0:T(4,128)S(1)}, s32[1,16,4]{1,2,0:T(4,128)}, u32[]{:S(2)}) copy-start(s32[1,16,4]{1,2,0:T(4,128)} %param.21) | copy-start | bytes 772
  2.8 18.6 %copy-start.12 = (s32[1,16]{1,0:T(1,128)S(1)}, s32[1,16]{1,0:T(1,128)}, u32[]{:S(2)}) copy-start(s32[1,16]{1,0:T(1,128)} %param.22) | copy-start | bytes 196
  2.9 29.6 %collective-permute-start.2 = (f32[168,128]{1,0:T(8,128)S(1)}, f32[168,128]{1,0:T(8,128)S(1)}, u32[]{:S(2)}, u32[]{:S(2)}) collective-permute-start(f32[168,128]{1,0:T(8,128)S(1)} %pad_maximum_fusion), channel_id=1, source_target_pairs={{8,7},{9,6},{10,5},{11,4},{12,3},{13,2},{14,1},{15,0},{24,23},{25,... | collective-permute-start | bytes 258056 | tf_op jit(solution)/shard_map/ppermute | solution.py:352
  4.2 34.3 %copy-start.2 = (s32[4,16,128]{2,1,0:T(8,128)S(1)}, s32[4,16,128]{2,1,0:T(8,128)}, u32[]{:S(2)}) copy-start(s32[4,16,128]{2,1,0:T(8,128)} %fibre_ref.3) | copy-start | bytes 98308
  4.2 35.0 %collective-permute-start.5 = (f32[168,128]{1,0:T(8,128)S(1)}, f32[168,128]{1,0:T(8,128)S(1)}, u32[]{:S(2)}, u32[]{:S(2)}) collective-permute-start(f32[168,128]{1,0:T(8,128)S(1)} %pad_maximum_fusion.1), channel_id=1, source_target_pairs={{8,3},{9,2},{10,1},{11,0},{12,7},{13,6},{14,5},{15,4},{24,19},{25,... | collective-permute-start | bytes 258056 | tf_op jit(solution)/shard_map/ppermute | solution.py:352
  5.6 34.9 %collective-permute-start.6 = (f32[168,128]{1,0:T(8,128)S(1)}, f32[168,128]{1,0:T(8,128)S(1)}, u32[]{:S(2)}, u32[]{:S(2)}) collective-permute-start(f32[168,128]{1,0:T(8,128)S(1)} %pad_maximum_fusion.2), channel_id=1, source_target_pairs={{8,2},{9,3},{10,0},{11,1},{12,6},{13,7},{14,4},{15,5},{24,18},{25,... | collective-permute-start | bytes 258056 | tf_op jit(solution)/shard_map/ppermute | solution.py:352
  6.9 47.8 %copy-start.7 = (f32[3,41]{1,0:T(4,128)S(1)}, f32[3,41]{1,0:T(4,128)}, u32[]{:S(2)}) copy-start(f32[3,41]{1,0:T(4,128)} %param.25) | copy-start | bytes 1480
  6.9 47.9 %copy-start.8 = (f32[3,41]{1,0:T(4,128)S(1)}, f32[3,41]{1,0:T(4,128)}, u32[]{:S(2)}) copy-start(f32[3,41]{1,0:T(4,128)} %param.28) | copy-start | bytes 1480
  7.0 48.0 %copy-start.9 = (f32[3,41]{1,0:T(4,128)S(1)}, f32[3,41]{1,0:T(4,128)}, u32[]{:S(2)}) copy-start(f32[3,41]{1,0:T(4,128)} %param.29) | copy-start | bytes 1480
  7.0 48.1 %copy-start.11 = (f32[3,41]{1,0:T(4,128)S(1)}, f32[3,41]{1,0:T(4,128)}, u32[]{:S(2)}) copy-start(f32[3,41]{1,0:T(4,128)} %param.27) | copy-start | bytes 1480
  12.9 8.7 %collective-permute-start = (f32[6,1,128]{2,1,0:T(1,128)S(1)}, f32[6,1,128]{2,1,0:T(1,128)S(1)}, u32[]{:S(2)}, u32[]{:S(2)}) collective-permute-start(f32[6,1,128]{2,1,0:T(1,128)S(1)} %get-tuple-element.74), channel_id=1, source_target_pairs={{0,16},{16,32},{32,48},{48,64},{64,80},{80,96},{96,112},{1,17},{17... | collective-permute-start | bytes 9224 | tf_op jit(solution)/shard_map/ppermute | solution.py:261
  17.6 8.0 %collective-permute-start.1 = (f32[6,1,128]{2,1,0:T(1,128)S(1)}, f32[6,1,128]{2,1,0:T(1,128)S(1)}, u32[]{:S(2)}, u32[]{:S(2)}) collective-permute-start(f32[6,1,128]{2,1,0:T(1,128)S(1)} %get-tuple-element.75), channel_id=1, source_target_pairs={{16,0},{32,16},{48,32},{64,48},{80,64},{96,80},{112,96},{17,1},{33... | collective-permute-start | bytes 9224 | tf_op jit(solution)/shard_map/ppermute | solution.py:262
  19.8 38.9 %copy-start = (f32[4,16,41,128]{3,1,2,0:T(8,128)S(1)}, f32[4,16,41,128]{3,1,2,0:T(8,128)}, u32[]{:S(2)}) copy-start(f32[4,16,41,128]{3,1,2,0:T(8,128)} %param.16) | copy-start | bytes 4030468
  19.8 38.9 %copy-start.1 = (s32[4,16,128]{2,1,0:T(8,128)S(1)}, s32[4,16,128]{2,1,0:T(8,128)}, u32[]{:S(2)}) copy-start(s32[4,16,128]{2,1,0:T(8,128)} %param.17) | copy-start | bytes 98308
  32.7 3.9 %collective-permute-start.3 = (f32[6,18]{1,0:T(8,128)S(1)}, f32[6,18]{1,0:T(8,128)S(1)}, u32[]{:S(2)}, u32[]{:S(2)}) collective-permute-start(f32[6,18]{1,0:T(8,128)S(1)} %get-tuple-element.57), channel_id=1, source_target_pairs={{0,1},{1,2},{2,3},{3,4},{4,5},{5,6},{6,7},{7,8},{8,9},{9,10},{10,1... | collective-permute-start | bytes 1304 | tf_op jit(solution)/shard_map/ppermute | solution.py:261
  34.0 4.4 %collective-permute-start.4 = (f32[6,18]{1,0:T(8,128)S(1)}, f32[6,18]{1,0:T(8,128)S(1)}, u32[]{:S(2)}, u32[]{:S(2)}) collective-permute-start(f32[6,18]{1,0:T(8,128)S(1)} %get-tuple-element.56), channel_id=1, source_target_pairs={{1,0},{2,1},{3,2},{4,3},{5,4},{6,5},{7,6},{8,7},{9,8},{10,9},{11,1... | collective-permute-start | bytes 1304 | tf_op jit(solution)/shard_map/ppermute | solution.py:262
  35.3 25.1 %collective-permute-start.9 = (f32[168,128]{1,0:T(8,128)}, f32[168,128]{1,0:T(8,128)S(1)}, u32[]{:S(2)}, u32[]{:S(2)}) collective-permute-start(f32[168,128]{1,0:T(8,128)} %pad_maximum_fusion.5), channel_id=1, source_target_pairs={{8,1},{9,0},{10,3},{11,2},{12,5},{13,4},{14,7},{15,6},{24,17},{25,... | collective-permute-start | bytes 258056 | tf_op jit(solution)/shard_map/ppermute | solution.py:352
  39.2 31.0 %collective-permute-start.10 = (f32[168,128]{1,0:T(8,128)}, f32[168,128]{1,0:T(8,128)S(1)}, u32[]{:S(2)}, u32[]{:S(2)}) collective-permute-start(f32[168,128]{1,0:T(8,128)} %get-tuple-element.42), channel_id=1, source_target_pairs={{8,0},{9,1},{10,2},{11,3},{12,4},{13,5},{14,6},{15,7},{24,16},{25,... | collective-permute-start | bytes 258056 | tf_op jit(solution)/shard_map/ppermute | solution.py:352
  40.5 14.8 %collective-permute-start.7 = (f32[4,128]{1,0:T(4,128)S(1)}, f32[4,128]{1,0:T(4,128)S(1)}, u32[]{:S(2)}, u32[]{:S(2)}) collective-permute-start(f32[4,128]{1,0:T(4,128)S(1)} %get-tuple-element.33), channel_id=1, source_target_pairs={{5,8},{4,9},{7,10},{6,11},{1,12},{0,13},{3,14},{2,15},{21,24},{20,... | collective-permute-start | bytes 6152 | tf_op jit(solution)/shard_map/ppermute | solution.py:374
  52.0 3.3 %collective-permute-start.8 = (f32[4,128]{1,0:T(4,128)S(1)}, f32[4,128]{1,0:T(4,128)S(1)}, u32[]{:S(2)}, u32[]{:S(2)}) collective-permute-start(f32[4,128]{1,0:T(4,128)S(1)} %get-tuple-element.35), channel_id=1, source_target_pairs={{4,8},{5,9},{6,10},{7,11},{0,12},{1,13},{2,14},{3,15},{20,24},{21,... | collective-permute-start | bytes 6152 | tf_op jit(solution)/shard_map/ppermute | solution.py:374
  53.4 16.8 %collective-permute-start.11 = (f32[168,128]{1,0:T(8,128)}, f32[168,128]{1,0:T(8,128)S(1)}, u32[]{:S(2)}, u32[]{:S(2)}) collective-permute-start(f32[168,128]{1,0:T(8,128)} %get-tuple-element.43), channel_id=1, source_target_pairs={{8,6},{9,7},{10,4},{11,5},{12,2},{13,3},{14,0},{15,1},{24,22},{25,... | collective-permute-start | bytes 258056 | tf_op jit(solution)/shard_map/ppermute | solution.py:352
  56.1 12.8 %collective-permute-start.12 = (f32[4,128]{1,0:T(4,128)S(1)}, f32[4,128]{1,0:T(4,128)S(1)}, u32[]{:S(2)}, u32[]{:S(2)}) collective-permute-start(f32[4,128]{1,0:T(4,128)S(1)} %get-tuple-element.36), channel_id=1, source_target_pairs={{8,5},{9,4},{10,7},{11,6},{12,1},{13,0},{14,3},{15,2},{24,21},{25,... | collective-permute-start | bytes 6152 | tf_op jit(solution)/shard_map/ppermute | solution.py:384
  57.4 12.8 %collective-permute-start.13 = (f32[4,128]{1,0:T(4,128)S(1)}, f32[4,128]{1,0:T(4,128)S(1)}, u32[]{:S(2)}, u32[]{:S(2)}) collective-permute-start(f32[4,128]{1,0:T(4,128)S(1)} %get-tuple-element.37), channel_id=1, source_target_pairs={{8,4},{9,5},{10,6},{11,7},{12,0},{13,1},{14,2},{15,3},{24,20},{25,... | collective-permute-start | bytes 6152 | tf_op jit(solution)/shard_map/ppermute | solution.py:384
  71.2 7.9 %collective-permute-start.14 = (f32[4,1,128]{2,1,0:T(1,128)S(1)}, f32[4,1,128]{2,1,0:T(1,128)S(1)}, u32[]{:S(2)}, u32[]{:S(2)}) collective-permute-start(f32[4,1,128]{2,1,0:T(1,128)S(1)} %get-tuple-element.76), channel_id=1, source_target_pairs={{0,16},{16,32},{32,48},{48,64},{64,80},{80,96},{96,112},{1,17},{17... | collective-permute-start | bytes 6152 | tf_op jit(solution)/shard_map/ppermute | solution.py:261
  74.2 7.9 %collective-permute-start.15 = (f32[4,1,128]{2,1,0:T(1,128)S(1)}, f32[4,1,128]{2,1,0:T(1,128)S(1)}, u32[]{:S(2)}, u32[]{:S(2)}) collective-permute-start(f32[4,1,128]{2,1,0:T(1,128)S(1)} %get-tuple-element.77), channel_id=1, source_target_pairs={{16,0},{32,16},{48,32},{64,48},{80,64},{96,80},{112,96},{17,1},{33... | collective-permute-start | bytes 6152 | tf_op jit(solution)/shard_map/ppermute | solution.py:262
  76.5 26.0 %collective-permute-start.18 = (f32[168,128]{1,0:T(8,128)S(1)}, f32[168,128]{1,0:T(8,128)S(1)}, u32[]{:S(2)}, u32[]{:S(2)}) collective-permute-start(f32[168,128]{1,0:T(8,128)S(1)} %get-tuple-element.52.refs_0_), channel_id=1, source_target_pairs={{8,5},{9,4},{10,7},{11,6},{12,1},{13,0},{14,3},{15,2},{24,21},{25,... | collective-permute-start | bytes 258056 | tf_op jit(solution)/shard_map/ppermute | solution.py:352
  77.8 24.7 %collective-permute-start.19 = (f32[168,128]{1,0:T(8,128)S(1)}, f32[168,128]{1,0:T(8,128)S(1)}, u32[]{:S(2)}, u32[]{:S(2)}) collective-permute-start(f32[168,128]{1,0:T(8,128)S(1)} %get-tuple-element.53.refs_1_), channel_id=1, source_target_pairs={{8,4},{9,5},{10,6},{11,7},{12,0},{13,1},{14,2},{15,3},{24,20},{25,... | collective-permute-start | bytes 258056 | tf_op jit(solution)/shard_map/ppermute | solution.py:352
  82.3 4.7 %collective-permute-start.16 = (f32[4,18]{1,0:T(4,128)S(1)}, f32[4,18]{1,0:T(4,128)S(1)}, u32[]{:S(2)}, u32[]{:S(2)}) collective-permute-start(f32[4,18]{1,0:T(4,128)S(1)} %get-tuple-element.58), channel_id=1, source_target_pairs={{0,1},{1,2},{2,3},{3,4},{4,5},{5,6},{6,7},{7,8},{8,9},{9,10},{10,1... | collective-permute-start | bytes 872 | tf_op jit(solution)/shard_map/ppermute | solution.py:261
  85.7 4.6 %collective-permute-start.17 = (f32[4,18]{1,0:T(4,128)S(1)}, f32[4,18]{1,0:T(4,128)S(1)}, u32[]{:S(2)}, u32[]{:S(2)}) collective-permute-start(f32[4,18]{1,0:T(4,128)S(1)} %get-tuple-element.59), channel_id=1, source_target_pairs={{1,0},{2,1},{3,2},{4,3},{5,4},{6,5},{7,6},{8,7},{9,8},{10,9},{11,1... | collective-permute-start | bytes 872 | tf_op jit(solution)/shard_map/ppermute | solution.py:262
